TPU v7x, 512 devices: a whole 4x8x8 slice. The times are simulated.
512 devices in a mesh: ctx: 32 (over z, y_hi), dp: 16 (over x, y_lo, core).
Axes of the slice: x: 4, y: 8 (y_hi: 4, y_lo: 2; y = y_hi * 2 + y_lo), z: 8, core: 2. Of those that a mesh axis runs over, the one named last changes fastest.
Arguments:
- queries: bfloat16 [65536, 3584], P(('ctx', 'dp')), may hold values from -17 to 17
- keys: bfloat16 [65536, 512], P(('ctx', 'dp')), may hold values from -17 to 17
- values: bfloat16 [65536, 512], P(('ctx', 'dp')), may hold values from -6 to 6
- d_out: bfloat16 [65536, 3584], P(('ctx', 'dp')), may hold values from -6 to 6
- lengths: int32 [512], replicated, may hold values from 1 to 256, 65536 in all
Outputs:
- attended: bfloat16 [65536, 3584], P(('ctx', 'dp'))
- d_queries: bfloat16 [65536, 3584], P(('ctx', 'dp'))
- d_keys: bfloat16 [65536, 512], P(('ctx', 'dp'))
- d_values: bfloat16 [65536, 512], P(('ctx', 'dp'))
Inputs may be any that keep to these rules, and one draw needn't show every extreme that they name: The lengths sum to 65536; the longest is exactly 256.
All inputs are finite; a program needn't handle non-finite values.
Results may differ from a plain program's by a relative error of at most 0.022.
Values may be sent and summed in bfloat16 or wider, within the bound.
No kernel may reach another device: no remote copies, remote signals or barrier semaphores. Data moves between devices by JAX's collectives and lax.ppermute only.
A program may use at most 128 MiB of HBM per device.

v0:
```python
import jax
import jax.numpy as jnp
from jax import lax
from jax.sharding import PartitionSpec as P

QH = 28
KVH = 4
HD = 128
DOC_MAX = 256


NEG = -1e30


def from_behind(value, axis, steps):
    count = lax.axis_size(axis)
    leading, last = (max(0, -steps), min(count, count - steps))
    return lax.ppermute(value, axis, [(source, source + steps) for source in range(leading, last)])


def doc_of(positions, ends):
    return jnp.sum((ends[None, :] <= positions[:, None]).astype(jnp.int32), axis=1)


def body(queries, keys, values, d_out, lengths):
    rows = queries.shape[0]
    groups = QH // KVH
    scale = HD ** (-0.5)
    reach = (DOC_MAX + rows - 2) // rows
    ends = jnp.cumsum(lengths)
    start = lax.axis_index(("ctx", "dp")) * rows
    q_pos = start + jnp.arange(rows, dtype=jnp.int32)
    q_doc = doc_of(q_pos, ends)
    query_blk = queries.reshape(rows, KVH, groups, HD)
    grad_blk = d_out.reshape(rows, KVH, groups, HD)
    pieces = [(keys, values)]
    for dist in range(1, reach + 1):
        pieces.append(from_behind((keys, values), ("ctx", "dp"), dist))
    masks = []
    lives = []
    for dist in range(reach + 1):
        k_pos = start - dist * rows + jnp.arange(rows, dtype=jnp.int32)
        allowed = (
            (doc_of(k_pos, ends)[None, :] == q_doc[:, None])
            & (k_pos[None, :] <= q_pos[:, None])
            & (k_pos[None, :] >= 0)
        )
        masks.append(allowed)
        lives.append(jnp.any(allowed))
    stat_shape = (KVH, groups, rows)
    peak = jnp.full(stat_shape, NEG, jnp.float32)
    total = jnp.zeros(stat_shape, jnp.float32)
    scores = []
    for dist in range(reach + 1):

        def stats_work(dist=dist):
            key_blk = pieces[dist][0].reshape(rows, KVH, HD)
            raw = (
                jnp.einsum("tkgd,skd->kgts", query_blk, key_blk, preferred_element_type=jnp.float32)
                * scale
            )
            score = jnp.where(masks[dist], raw, NEG)
            block_max = jnp.max(score, axis=-1)
            return (score, block_max, jnp.sum(jnp.exp(score - block_max[..., None]), axis=-1))

        score, block_max, block_sum = stats_work()
        scores.append(score)
        new_peak = jnp.maximum(peak, block_max)
        total = total * jnp.exp(peak - new_peak) + block_sum * jnp.exp(block_max - new_peak)
        peak = new_peak
    lse = peak + jnp.log(total)
    probs = []
    out_acc = jnp.zeros((rows, KVH, groups, HD), jnp.float32)
    for dist in range(reach + 1):

        def prob_work(dist=dist):
            prob = jnp.where(masks[dist], jnp.exp(scores[dist] - lse[..., None]), 0.0)
            value_blk = pieces[dist][1].reshape(rows, KVH, HD)
            term = jnp.einsum(
                "kgts,skd->tkgd",
                prob.astype(jnp.bfloat16),
                value_blk,
                preferred_element_type=jnp.float32,
            )
            return (prob, term)

        prob, term = prob_work()
        probs.append(prob)
        out_acc = out_acc + term
    attended = out_acc.astype(jnp.bfloat16)
    delta = jnp.sum(attended.astype(jnp.float32) * grad_blk.astype(jnp.float32), axis=-1).transpose(
        1, 2, 0
    )

    def grad_terms(dist):
        key_blk = pieces[dist][0].reshape(rows, KVH, HD)
        value_blk = pieces[dist][1].reshape(rows, KVH, HD)
        prob = probs[dist]
        d_prob = jnp.einsum(
            "tkgd,skd->kgts", grad_blk, value_blk, preferred_element_type=jnp.float32
        )
        d_score = (prob * (d_prob - delta[..., None])).astype(jnp.bfloat16)
        d_query = jnp.einsum("kgts,skd->tkgd", d_score, key_blk, preferred_element_type=jnp.float32)
        d_key = scale * jnp.einsum(
            "kgts,tkgd->skd", d_score, query_blk, preferred_element_type=jnp.float32
        )
        d_value = jnp.einsum(
            "kgts,tkgd->skd",
            prob.astype(jnp.bfloat16),
            grad_blk,
            preferred_element_type=jnp.float32,
        )
        return (d_query, d_key.reshape(rows, KVH * HD), d_value.reshape(rows, KVH * HD))

    dq_acc, dk_acc, dv_acc = grad_terms(0)
    for dist in range(1, reach + 1):
        d_query, d_key, d_value = grad_terms(dist)
        dq_acc = dq_acc + d_query
        back_k, back_v = (
            from_behind(d_key.astype(jnp.bfloat16), ("ctx", "dp"), -dist).astype(d_key.dtype),
            from_behind(d_value.astype(jnp.bfloat16), ("ctx", "dp"), -dist).astype(d_value.dtype),
        )
        dk_acc = dk_acc + back_k
        dv_acc = dv_acc + back_v
    d_queries = (scale * dq_acc).astype(jnp.bfloat16).reshape(rows, QH * HD)
    return (
        attended.reshape(rows, QH * HD),
        d_queries,
        dk_acc.astype(jnp.bfloat16),
        dv_acc.astype(jnp.bfloat16),
    )


def solution(mesh):
    in_specs = (
        P(("ctx", "dp"), None),
        P(("ctx", "dp"), None),
        P(("ctx", "dp"), None),
        P(("ctx", "dp"), None),
        P(),
    )
    out_specs = (
        P(("ctx", "dp"), None),
        P(("ctx", "dp"), None),
        P(("ctx", "dp"), None),
        P(("ctx", "dp"), None),
    )
    return jax.shard_map(body, mesh=mesh, in_specs=in_specs, out_specs=out_specs, check_vma=False)
```

profile of v0, /device:TPU:255, one launch (start us, length us, event | category | flops | bytes accessed | tf_op | source)
XLA Modules:
  0.0 74.5 jit_solution(17143743226862049794)
XLA Ops:
  1.7 4.3 %collective-permute-start.1 = (bf16[128,512]{0,1:T(8,128)(2,1)S(1)}, bf16[128,512]{0,1:T(8,128)(2,1)S(1)}, u32[]{:S(2)}, u32[]{:S(2)}) collective-permute-start(bf16[128,512]{0,1:T(8,128)(2,1)S(1)} %copy.92), channel_id=1, source_target_pairs={{0,2},{1,3},{2,4},{3,5},{4,6},{5,7},{6,8},{7,9},{8,10},{9,11},{10,... | collective-permute-start | bytes 393224 | tf_op jit(solution)/shard_map/ppermute | solution.py:18
  6.1 4.0 %collective-permute-start = (bf16[128,512]{0,1:T(8,128)(2,1)S(1)}, bf16[128,512]{0,1:T(8,128)(2,1)S(1)}, u32[]{:S(2)}, u32[]{:S(2)}) collective-permute-start(bf16[128,512]{0,1:T(8,128)(2,1)S(1)} %copy.92), channel_id=1, source_target_pairs={{0,1},{1,2},{2,3},{3,4},{4,5},{5,6},{6,7},{7,8},{8,9},{9,10},{10,1... | collective-permute-start | bytes 393224 | tf_op jit(solution)/shard_map/ppermute | solution.py:18
  10.1 3.0 %collective-permute-start.3 = (bf16[128,512]{1,0:T(8,128)(2,1)}, bf16[128,512]{1,0:T(8,128)(2,1)}, u32[]{:S(2)}, u32[]{:S(2)}) collective-permute-start(bf16[128,512]{1,0:T(8,128)(2,1)} %param.7), channel_id=1, source_target_pairs={{0,2},{1,3},{2,4},{3,5},{4,6},{5,7},{6,8},{7,9},{8,10},{9,11},{10,... | collective-permute-start | bytes 393224 | tf_op jit(solution)/shard_map/ppermute | solution.py:18
  13.2 2.2 %collective-permute-start.2 = (bf16[128,512]{1,0:T(8,128)(2,1)}, bf16[128,512]{1,0:T(8,128)(2,1)}, u32[]{:S(2)}, u32[]{:S(2)}) collective-permute-start(bf16[128,512]{1,0:T(8,128)(2,1)} %param.7), channel_id=1, source_target_pairs={{0,1},{1,2},{2,3},{3,4},{4,5},{5,6},{6,7},{7,8},{8,9},{9,10},{10,1... | collective-permute-start | bytes 393224 | tf_op jit(solution)/shard_map/ppermute | solution.py:18
  18.7 1.6 %copy.89 = bf16[128,3584]{0,1:T(8,128)(2,1)S(1)} copy(bf16[128,3584]{1,0:T(8,128)(2,1)} %param.5) | data formatting | bytes 1835008 | tf_op args[0]
  20.3 1.3 %copy.104 = bf16[128,3584]{0,1:T(8,128)(2,1)} copy(bf16[128,3584]{1,0:T(8,128)(2,1)S(1)} %copy-done.10) | data formatting | bytes 1835008 | tf_op args[3]
  25.2 1.2 %fusion.21 = f32[4,128,128,1]{1,2,3,0:T(8,128)} fusion(bf16[128,4,7,128]{0,3,2,1:T(8,128)(2,1)S(1)} %bitcast.158, f32[4,7,128,128]{2,3,1,0:T(8,128)S(1)} %get-tuple-element.23, f32[4,7,128]{2,1,0:T(8,128)S(1)} %fusion.35, pred[128,128]{0,1:T(8,128)(4,1)S(1)} %get-tuple-element.21), kind=kOutput, calls=%fused_computation.42 | convolution fusion | flops 118816768 | bytes 3045376 | tf_op jit(solution)/shard_map/kgts,tkgd->skd/dot_general | solution.py:107
  28.5 3.2 %fusion.19 = f32[4,7,128,128]{2,3,1,0:T(8,128)} fusion(bf16[128,4,128,1]{0,2,3,1:T(8,128)(2,1)S(1)} %bitcast.170, f32[4,7,128,128]{2,3,1,0:T(8,128)} %copy-done.3, f32[4,7,128]{2,1,0:T(8,128)S(1)} %fusion.35, pred[128,128]{0,1:T(8,128)(4,1)S(1)} %get-tuple-element.19), kind=kOutput, calls=%fused_computation.41 | convolution fusion | flops 118816768 | bytes 3831808 | tf_op jit(solution)/shard_map/kgts,skd->tkgd/dot_general | solution.py:79
  31.7 1.7 %fusion.23 = f32[4,7,128,128]{2,3,1,0:T(8,128)} fusion(f32[4,7,128,128]{2,3,1,0:T(8,128)S(1)} %get-tuple-element.23, f32[4,7,128]{2,1,0:T(8,128)S(1)} %fusion.35, pred[128,128]{0,1:T(8,128)(4,1)S(1)} %get-tuple-element.21, bf16[128,4,128,1]{2,1,0,3:T(4,128)(2,1)S(1)} %bitcast.168), kind=kOutput, calls=%fused_computation.43 | convolution fusion | flops 118816768 | bytes 3831808 | tf_op jit(solution)/shard_map/kgts,skd->tkgd/dot_general | solution.py:79
  36.3 4.6 %multiply_reduce_fusion = (f32[128,4,7]{0,2,1:T(8,128)S(1)}, bf16[4,7,128,128]{2,3,1,0:T(8,128)(2,1)}) fusion(bf16[128,4,7,128]{0,3,2,1:T(8,128)(2,1)} %bitcast.157, bf16[128,4,128,1]{0,2,3,1:T(8,128)(2,1)S(1)} %bitcast.166, f32[4,7,128,128]{2,3,1,0:T(8,128)} %copy-done, f32[4,7,128]{2,1,0:T(8,128)S(1)} %fusion.35, pred[128,128]{0,1:T(8,128)(4,1)} %copy-done.14, ...), kind=kOutput, calls=%fused_computation.13 | convolution fusion | flops 122024448 | bytes 7516160 | tf_op jit(solution)/shard_map/kgts,skd->tkgd/dot_general | solution.py:79
  42.4 1.6 %fusion.1 = bf16[4,7,128,128]{2,3,1,0:T(8,128)(2,1)} fusion(bf16[128,4,128,1]{0,2,3,1:T(8,128)(2,1)S(1)} %bitcast.167, bf16[128,4,7,128]{0,3,2,1:T(8,128)(2,1)S(1)} %bitcast.162, f32[4,7,128,128]{2,3,1,0:T(8,128)S(1)} %copy-done.2, f32[4,7,128]{2,1,0:T(8,128)S(1)} %bitcast.181, f32[4,7,128]{2,1,0:T(8,128)S(1)} %fusion.35, pred[128,128]{0,1:T(8,128)(4,1)S(1)} %copy-done.15), kind=kOutput, calls=%fused_computation.2 | convolution fusion | flops 119734272 | bytes 3846144 | tf_op jit(solution)/shard_map/tkgd,skd->kgts/dot_general | solution.py:99
  45.0 1.6 %fusion.52 = f32[4,7,128,128]{2,3,1,0:T(8,128)} fusion(bf16[128,4,128,1]{0,2,3,1:T(8,128)(2,1)S(1)} %copy.144, bf16[4,7,128,128]{2,3,1,0:T(8,128)(2,1)S(1)} %fusion.5), kind=kOutput, calls=%fused_computation.87 | convolution fusion | flops 117440512 | bytes 2883584 | tf_op jit(solution)/shard_map/kgts,skd->tkgd/dot_general | solution.py:103
  46.7 1.1 %fusion.13 = bf16[4,128,128]{1,2,0:T(8,128)(2,1)} fusion(bf16[4,7,128,128]{2,3,1,0:T(8,128)(2,1)S(1)} %fusion.3, bf16[128,4,7,128]{0,3,2,1:T(8,128)(2,1)S(1)} %bitcast.155), kind=kOutput, calls=%fused_computation.33 | convolution fusion | flops 117571584 | bytes 1966080 | tf_op jit(solution)/shard_map/kgts,tkgd->skd/dot_general | solution.py:104
  47.8 1.6 %fusion.53 = f32[4,7,128,128]{2,3,1,0:T(8,128)} fusion(bf16[128,4,128,1]{0,2,3,1:T(8,128)(2,1)S(1)} %bitcast.176, bf16[4,7,128,128]{2,3,1,0:T(8,128)(2,1)S(1)} %fusion.3), kind=kOutput, calls=%fused_computation.88 | convolution fusion | flops 117440512 | bytes 2883584 | tf_op jit(solution)/shard_map/kgts,skd->tkgd/dot_general | solution.py:103
  50.9 2.3 %collective-permute-start.7 = (bf16[128,512]{1,0:T(8,128)(2,1)}, bf16[128,512]{1,0:T(8,128)(2,1)S(1)}, u32[]{:S(2)}, u32[]{:S(2)}) collective-permute-start(bf16[128,512]{1,0:T(8,128)(2,1)} %copy.126), channel_id=1, source_target_pairs={{2,0},{3,1},{4,2},{5,3},{6,4},{7,5},{8,6},{9,7},{10,8},{11,9},{12,... | collective-permute-start | bytes 393224 | tf_op jit(solution)/shard_map/ppermute | solution.py:18
  53.2 2.4 %collective-permute-start.6 = (bf16[128,512]{1,0:T(8,128)(2,1)}, bf16[128,512]{1,0:T(8,128)(2,1)}, u32[]{:S(2)}, u32[]{:S(2)}) collective-permute-start(bf16[128,512]{1,0:T(8,128)(2,1)} %copy.123), channel_id=1, source_target_pairs={{1,0},{2,1},{3,2},{4,3},{5,4},{6,5},{7,6},{8,7},{9,8},{10,9},{11,1... | collective-permute-start | bytes 393224 | tf_op jit(solution)/shard_map/ppermute | solution.py:18
  56.7 1.3 %copy.127 = bf16[128,3584]{1,0:T(8,128)(2,1)} copy(bf16[128,3584]{0,1:T(8,128)(2,1)S(1)} %bitcast.164) | data formatting | bytes 1835008
  59.0 2.9 %collective-permute-start.4 = (bf16[128,512]{1,0:T(8,128)(2,1)S(1)}, bf16[128,512]{1,0:T(8,128)(2,1)S(1)}, u32[]{:S(2)}, u32[]{:S(2)}) collective-permute-start(bf16[128,512]{1,0:T(8,128)(2,1)S(1)} %copy.117), channel_id=1, source_target_pairs={{1,0},{2,1},{3,2},{4,3},{5,4},{6,5},{7,6},{8,7},{9,8},{10,9},{11,1... | collective-permute-start | bytes 393224 | tf_op jit(solution)/shard_map/ppermute | solution.py:18
  61.9 2.1 %collective-permute-start.5 = (bf16[128,512]{1,0:T(8,128)(2,1)S(1)}, bf16[128,512]{1,0:T(8,128)(2,1)S(1)}, u32[]{:S(2)}, u32[]{:S(2)}) collective-permute-start(bf16[128,512]{1,0:T(8,128)(2,1)S(1)} %copy.120), channel_id=1, source_target_pairs={{2,0},{3,1},{4,2},{5,3},{6,4},{7,5},{8,6},{9,7},{10,8},{11,9},{12,... | collective-permute-start | bytes 393224 | tf_op jit(solution)/shard_map/ppermute | solution.py:18
  64.0 2.5 %multiply_convert_fusion = bf16[4,7,128,128]{2,3,1,0:T(8,128)(2,1)S(1)} fusion(f32[4,7,128,128]{2,3,1,0:T(8,128)} %fusion.52, f32[4,7,128,128]{2,3,1,0:T(8,128)} %fusion.53, bf16[128,4,128,1]{0,2,3,1:T(8,128)(2,1)S(1)} %bitcast.174, bf16[4,7,128,128]{2,3,1,0:T(8,128)(2,1)S(1)} %copy-done.8), kind=kOutput, calls=%fused_computation.12 | convolution fusion | flops 119275520 | bytes 5636096 | tf_op jit(solution)/shard_map/kgts,skd->tkgd/dot_general | solution.py:103
  66.5 1.3 %copy.128 = bf16[128,3584]{1,0:T(8,128)(2,1)} copy(bf16[128,3584]{0,1:T(8,128)(2,1)S(1)} %bitcast.165) | data formatting | bytes 1835008
  67.7 1.6 %add_convert_fusion.1 = bf16[128,512]{1,0:T(8,128)(2,1)} fusion(bf16[128,512]{1,0:T(8,128)(2,1)S(1)} %collective-permute-done.7, f32[128,512]{1,0:T(8,128)S(1)} %copy.124, bf16[128,512]{1,0:T(8,128)(2,1)} %collective-permute-done.6), kind=kLoop, calls=%fused_computation.36 | loop fusion | flops 327680 | bytes 655360 | tf_op jit(solution)/shard_map/convert_element_type | solution.py:130
  69.3 1.4 %collective-permute-done.4 = bf16[128,512]{1,0:T(8,128)(2,1)S(1)} collective-permute-done((bf16[128,512]{1,0:T(8,128)(2,1)S(1)}, bf16[128,512]{1,0:T(8,128)(2,1)S(1)}, u32[]{:S(2)}, u32[]{:S(2)}) %collective-permute-start.4) | collective-permute-done | bytes 131104 | tf_op jit(solution)/shard_map/ppermute | solution.py:18
  70.7 3.1 %collective-permute-done.5 = bf16[128,512]{1,0:T(8,128)(2,1)S(1)} collective-permute-done((bf16[128,512]{1,0:T(8,128)(2,1)S(1)}, bf16[128,512]{1,0:T(8,128)(2,1)S(1)}, u32[]{:S(2)}, u32[]{:S(2)}) %collective-permute-start.5) | collective-permute-done | bytes 131104 | tf_op jit(solution)/shard_map/ppermute | solution.py:18
  (83 shorter events, 19.7 us)
Async XLA Ops:
  0.6 19.7 %copy-start.10 = (bf16[128,3584]{1,0:T(8,128)(2,1)S(1)}, bf16[128,3584]{1,0:T(8,128)(2,1)}, u32[]{:S(2)}) copy-start(bf16[128,3584]{1,0:T(8,128)(2,1)} %param.8) | copy-start | bytes 2752516
  1.7 21.1 %collective-permute-start.1 = (bf16[128,512]{0,1:T(8,128)(2,1)S(1)}, bf16[128,512]{0,1:T(8,128)(2,1)S(1)}, u32[]{:S(2)}, u32[]{:S(2)}) collective-permute-start(bf16[128,512]{0,1:T(8,128)(2,1)S(1)} %copy.92), channel_id=1, source_target_pairs={{0,2},{1,3},{2,4},{3,5},{4,6},{5,7},{6,8},{7,9},{8,10},{9,11},{10,... | collective-permute-start | bytes 393224 | tf_op jit(solution)/shard_map/ppermute | solution.py:18
  6.1 17.6 %collective-permute-start = (bf16[128,512]{0,1:T(8,128)(2,1)S(1)}, bf16[128,512]{0,1:T(8,128)(2,1)S(1)}, u32[]{:S(2)}, u32[]{:S(2)}) collective-permute-start(bf16[128,512]{0,1:T(8,128)(2,1)S(1)} %copy.92), channel_id=1, source_target_pairs={{0,1},{1,2},{2,3},{3,4},{4,5},{5,6},{6,7},{7,8},{8,9},{9,10},{10,1... | collective-permute-start | bytes 393224 | tf_op jit(solution)/shard_map/ppermute | solution.py:18
  10.1 25.1 %collective-permute-start.3 = (bf16[128,512]{1,0:T(8,128)(2,1)}, bf16[128,512]{1,0:T(8,128)(2,1)}, u32[]{:S(2)}, u32[]{:S(2)}) collective-permute-start(bf16[128,512]{1,0:T(8,128)(2,1)} %param.7), channel_id=1, source_target_pairs={{0,2},{1,3},{2,4},{3,5},{4,6},{5,7},{6,8},{7,9},{8,10},{9,11},{10,... | collective-permute-start | bytes 393224 | tf_op jit(solution)/shard_map/ppermute | solution.py:18
  13.2 14.3 %collective-permute-start.2 = (bf16[128,512]{1,0:T(8,128)(2,1)}, bf16[128,512]{1,0:T(8,128)(2,1)}, u32[]{:S(2)}, u32[]{:S(2)}) collective-permute-start(bf16[128,512]{1,0:T(8,128)(2,1)} %param.7), channel_id=1, source_target_pairs={{0,1},{1,2},{2,3},{3,4},{4,5},{5,6},{6,7},{7,8},{8,9},{9,10},{10,1... | collective-permute-start | bytes 393224 | tf_op jit(solution)/shard_map/ppermute | solution.py:18
  22.1 6.4 %copy-start.16 = (pred[128,128]{0,1:T(8,128)(4,1)}, pred[128,128]{0,1:T(8,128)(4,1)S(1)}, u32[]{:S(2)}) copy-start(pred[128,128]{0,1:T(8,128)(4,1)S(1)} %get-tuple-element.19) | copy-start | bytes 49156
  22.1 9.6 %copy-start.12 = (pred[128,128]{0,1:T(8,128)(4,1)}, pred[128,128]{0,1:T(8,128)(4,1)S(1)}, u32[]{:S(2)}) copy-start(pred[128,128]{0,1:T(8,128)(4,1)S(1)} %get-tuple-element.21) | copy-start | bytes 49156
  22.1 11.3 %copy-start.14 = (pred[128,128]{0,1:T(8,128)(4,1)}, pred[128,128]{0,1:T(8,128)(4,1)S(1)}, u32[]{:S(2)}) copy-start(pred[128,128]{0,1:T(8,128)(4,1)S(1)} %get-tuple-element.20) | copy-start | bytes 49156
  23.7 1.5 %copy-start.5 = (bf16[128,3584]{0,1:T(8,128)(2,1)S(1)}, bf16[128,3584]{0,1:T(8,128)(2,1)}, u32[]{:S(2)}) copy-start(bf16[128,3584]{0,1:T(8,128)(2,1)} %copy.104) | copy-start | bytes 2752516
  24.6 1.7 %copy-start.3 = (f32[4,7,128,128]{2,3,1,0:T(8,128)}, f32[4,7,128,128]{2,3,1,0:T(8,128)S(1)}, u32[]{:S(2)}) copy-start(f32[4,7,128,128]{2,3,1,0:T(8,128)S(1)} %get-tuple-element.27) | copy-start | bytes 5505028
  31.7 1.7 %copy-start.1 = (f32[4,7,128,128]{2,3,1,0:T(8,128)S(1)}, f32[4,7,128,128]{2,3,1,0:T(8,128)}, u32[]{:S(2)}) copy-start(f32[4,7,128,128]{2,3,1,0:T(8,128)} %copy-done) | copy-start | bytes 5505028
  31.7 2.4 %copy-start.6 = (bf16[128,3584]{0,1:T(8,128)(2,1)S(1)}, bf16[128,3584]{0,1:T(8,128)(2,1)}, u32[]{:S(2)}) copy-start(bf16[128,3584]{0,1:T(8,128)(2,1)} %copy.104) | copy-start | bytes 2752516
  36.2 4.7 %copy-start.4 = (f32[4,7,128,128]{2,3,1,0:T(8,128)S(1)}, f32[4,7,128,128]{2,3,1,0:T(8,128)}, u32[]{:S(2)}) copy-start(f32[4,7,128,128]{2,3,1,0:T(8,128)} %copy-done.3) | copy-start | bytes 5505028
  36.2 4.7 %copy-start.7 = (bf16[128,3584]{0,1:T(8,128)(2,1)S(1)}, bf16[128,3584]{0,1:T(8,128)(2,1)}, u32[]{:S(2)}) copy-start(bf16[128,3584]{0,1:T(8,128)(2,1)} %copy.104) | copy-start | bytes 2752516
  36.2 4.6 %copy-start.17 = (pred[128,128]{0,1:T(8,128)(4,1)S(1)}, pred[128,128]{0,1:T(8,128)(4,1)}, u32[]{:S(2)}) copy-start(pred[128,128]{0,1:T(8,128)(4,1)} %copy-done.16) | copy-start | bytes 49156
  42.4 1.6 %copy-start.13 = (pred[128,128]{0,1:T(8,128)(4,1)S(1)}, pred[128,128]{0,1:T(8,128)(4,1)}, u32[]{:S(2)}) copy-start(pred[128,128]{0,1:T(8,128)(4,1)} %copy-done.12) | copy-start | bytes 49156
  47.8 1.6 %copy-start.18 = (bf16[4,128,128]{1,2,0:T(8,128)(2,1)S(1)}, bf16[4,128,128]{1,2,0:T(8,128)(2,1)}, u32[]{:S(2)}) copy-start(bf16[4,128,128]{1,2,0:T(8,128)(2,1)} %fusion.14) | copy-start | bytes 393220
  47.8 2.4 %copy-start.19 = (bf16[4,128,128]{1,2,0:T(8,128)(2,1)S(1)}, bf16[4,128,128]{1,2,0:T(8,128)(2,1)}, u32[]{:S(2)}) copy-start(bf16[4,128,128]{1,2,0:T(8,128)(2,1)} %fusion.15) | copy-start | bytes 393220
  47.8 8.9 %copy-start.9 = (bf16[4,7,128,128]{2,3,1,0:T(8,128)(2,1)S(1)}, bf16[4,7,128,128]{2,3,1,0:T(8,128)(2,1)}, u32[]{:S(2)}) copy-start(bf16[4,7,128,128]{2,3,1,0:T(8,128)(2,1)} %get-tuple-element.29) | copy-start | bytes 2752516
  49.4 8.6 %copy-start.8 = (bf16[4,7,128,128]{2,3,1,0:T(8,128)(2,1)S(1)}, bf16[4,7,128,128]{2,3,1,0:T(8,128)(2,1)}, u32[]{:S(2)}) copy-start(bf16[4,7,128,128]{2,3,1,0:T(8,128)(2,1)} %fusion.1) | copy-start | bytes 2752516
  50.9 16.8 %collective-permute-start.7 = (bf16[128,512]{1,0:T(8,128)(2,1)}, bf16[128,512]{1,0:T(8,128)(2,1)S(1)}, u32[]{:S(2)}, u32[]{:S(2)}) collective-permute-start(bf16[128,512]{1,0:T(8,128)(2,1)} %copy.126), channel_id=1, source_target_pairs={{2,0},{3,1},{4,2},{5,3},{6,4},{7,5},{8,6},{9,7},{10,8},{11,9},{12,... | collective-permute-start | bytes 393224 | tf_op jit(solution)/shard_map/ppermute | solution.py:18
  53.2 14.5 %collective-permute-start.6 = (bf16[128,512]{1,0:T(8,128)(2,1)}, bf16[128,512]{1,0:T(8,128)(2,1)}, u32[]{:S(2)}, u32[]{:S(2)}) collective-permute-start(bf16[128,512]{1,0:T(8,128)(2,1)} %copy.123), channel_id=1, source_target_pairs={{1,0},{2,1},{3,2},{4,3},{5,4},{6,5},{7,6},{8,7},{9,8},{10,9},{11,1... | collective-permute-start | bytes 393224 | tf_op jit(solution)/shard_map/ppermute | solution.py:18
  59.0 11.7 %collective-permute-start.4 = (bf16[128,512]{1,0:T(8,128)(2,1)S(1)}, bf16[128,512]{1,0:T(8,128)(2,1)S(1)}, u32[]{:S(2)}, u32[]{:S(2)}) collective-permute-start(bf16[128,512]{1,0:T(8,128)(2,1)S(1)} %copy.117), channel_id=1, source_target_pairs={{1,0},{2,1},{3,2},{4,3},{5,4},{6,5},{7,6},{8,7},{9,8},{10,9},{11,1... | collective-permute-start | bytes 393224 | tf_op jit(solution)/shard_map/ppermute | solution.py:18
  61.9 11.9 %collective-permute-start.5 = (bf16[128,512]{1,0:T(8,128)(2,1)S(1)}, bf16[128,512]{1,0:T(8,128)(2,1)S(1)}, u32[]{:S(2)}, u32[]{:S(2)}) collective-permute-start(bf16[128,512]{1,0:T(8,128)(2,1)S(1)} %copy.120), channel_id=1, source_target_pairs={{2,0},{3,1},{4,2},{5,3},{6,4},{7,5},{8,6},{9,7},{10,8},{11,9},{12,... | collective-permute-start | bytes 393224 | tf_op jit(solution)/shard_map/ppermute | solution.py:18
  (4 other events, 5.2 us)
where the time goes:
time: 75.8 us; the launch traced here: 74.5 us
  matrix products  24.8 us (33%)
  starting transfers between devices  23.2 us (31%)
  local copies, waits for them, and re-layouts  16.2 us (21%)
  other arithmetic  4.8 us (6%)
  waiting for transfers between devices  4.47 us (6%)
  between operations  1.03 us (1%)
    ppermute x8, starting transfers between devices, from_behind(): lax.ppermute(value, axis, [(source, source + steps) for source in range(l...  23.2 us
    dot_general x3, matrix products, prob_work(): jnp.einsum('kgts,skd->tkgd', prob.astype(jnp.bfloat16), value_blk, prefer...  9.54 us
    unnamed x45, local copies, waits for them, and re-layouts  8.96 us
    dot_general x3, matrix products, grad_terms(): jnp.einsum('kgts,skd->tkgd', d_score, key_blk, preferred_element_type=jnp...  5.74 us
    ppermute x8, waiting for transfers between devices, from_behind(): lax.ppermute(value, axis, [(source, source + steps) for source in range(l...  4.47 us
    dot_general x3, matrix products, grad_terms(): jnp.einsum('kgts,tkgd->skd', prob.astype(jnp.bfloat16), grad_blk, preferr...  3.37 us
    dot_general x3, matrix products, grad_terms(): jnp.einsum('tkgd,skd->kgts', grad_blk, value_blk, preferred_element_type=...  2.77 us
    ppermute x2, local copies, waits for them, and re-layouts, from_behind(): lax.ppermute(value, axis, [(source, source + steps) for source in range(l...  2.04 us
  transfers between devices with their start and end apart: 8, of which 2 were waited for; matrix products, arithmetic and copies ran while one was open for 36% of the time, Pallas kernels for 0%

commit v1 on v0

v1 whole, which is shorter than its diff:
```python
import functools
import jax
import jax.numpy as jnp
from jax import lax
from jax.experimental import pallas as pl
from jax.experimental.pallas import tpu as pltpu
from jax.sharding import PartitionSpec as P

QH = 28
KVH = 4
GROUPS = QH // KVH
HD = 128
ROWS = 128
DOCS = 512
AXES = ("ctx", "dp")
NEG = -1e30
SCALE = HD**-0.5
LOG2E = 1.4426950408889634
WIDE = GROUPS * HD

NT = (((1,), (1,)), ((), ()))
NN = (((1,), (0,)), ((), ()))


def dot(a, b, dims):
    return lax.dot_general(a, b, dims, preferred_element_type=jnp.float32)


def shifted(value, steps):
    count = lax.axis_size(AXES)
    leading, last = (max(0, -steps), min(count, count - steps))
    return lax.ppermute(value, AXES, [(source, source + steps) for source in range(leading, last)])


def mask_kernel(start_ref, lengths_ref, bias_ref):
    start = start_ref[0]
    lens = jnp.broadcast_to(lengths_ref[...].astype(jnp.float32), (ROWS, DOCS)).astype(jnp.bfloat16)
    doc = lax.broadcasted_iota(jnp.int32, (DOCS, DOCS), 0)
    upto = lax.broadcasted_iota(jnp.int32, (DOCS, DOCS), 1)
    before = jnp.where(upto <= doc, 1.0, 0.0).astype(jnp.bfloat16)
    ends = dot(before, lens, NT).astype(jnp.int32)
    query = start + lax.broadcasted_iota(jnp.int32, (DOCS, ROWS), 1)
    first = jnp.max(jnp.where(ends <= query, ends, 0), axis=0, keepdims=True)
    first = first - start
    s = lax.broadcasted_iota(jnp.int32, (ROWS, ROWS), 0)
    t = lax.broadcasted_iota(jnp.int32, (ROWS, ROWS), 1)
    merged = jnp.where(s <= t, s, s - 2 * ROWS)
    bias_ref[0:ROWS, :] = jnp.where(merged >= first, 0.0, NEG)
    bias_ref[ROWS:, :] = jnp.where(s - ROWS >= first, 0.0, NEG)


def score_kernel(q_ref, do_ref, ko_ref, vo_ref, kp_ref, vp_ref, kf_ref, vf_ref, bias_ref,
                 prob_ref, ds_ref, near_k_ref, near_v_ref, far_k_ref, far_v_ref):
    def heads(ref):
        return jnp.concatenate([ref[:, h * HD:(h + 1) * HD] for h in range(GROUPS)], axis=0)

    qs = heads(q_ref)
    dos = heads(do_ref)
    s_far = dot(kf_ref[...], qs, NT)
    s_own = dot(ko_ref[...], qs, NT)
    s_near = dot(kp_ref[...], qs, NT)
    d_far = dot(vf_ref[...], dos, NT)
    d_own = dot(vo_ref[...], dos, NT)
    d_near = dot(vp_ref[...], dos, NT)
    tri = (lax.broadcasted_iota(jnp.int32, (ROWS, ROWS), 0)
           <= lax.broadcasted_iota(jnp.int32, (ROWS, ROWS), 1))
    factor = SCALE * LOG2E
    for h in range(GROUPS):
        cols = slice(h * HD, (h + 1) * HD)
        a = jnp.where(tri, s_own[:, cols], s_far[:, cols]) + bias_ref[0:ROWS, :]
        b = s_near[:, cols] + bias_ref[ROWS:, :]
        peak = jnp.max(jnp.maximum(a, b), axis=0, keepdims=True)
        a = jnp.exp2((a - peak) * factor)
        b = jnp.exp2((b - peak) * factor)
        inv = 1.0 / jnp.sum(a + b, axis=0, keepdims=True)
        a = a * inv
        b = b * inv
        da = jnp.where(tri, d_own[:, cols], d_far[:, cols])
        db = d_near[:, cols]
        delta = jnp.sum(a * da + b * db, axis=0, keepdims=True)
        prob_ref[0:ROWS, cols] = a.astype(jnp.bfloat16)
        prob_ref[ROWS:, cols] = b.astype(jnp.bfloat16)
        ds_ref[0:ROWS, cols] = (a * (da - delta)).astype(jnp.bfloat16)
        ds_ref[ROWS:, cols] = (b * (db - delta)).astype(jnp.bfloat16)
    wide_tri = (lax.broadcasted_iota(jnp.int32, (ROWS, WIDE), 0)
                <= lax.broadcasted_iota(jnp.int32, (ROWS, WIDE), 1) % HD)
    none = jnp.zeros((ROWS, WIDE), jnp.bfloat16)
    far_v_ref[...] = dot(jnp.where(wide_tri, none, prob_ref[0:ROWS, :]), dos, NN).astype(jnp.bfloat16)
    near_v_ref[...] = dot(prob_ref[ROWS:, :], dos, NN).astype(jnp.bfloat16)
    far_k_ref[...] = (SCALE * dot(jnp.where(wide_tri, none, ds_ref[0:ROWS, :]), qs, NN)).astype(jnp.bfloat16)
    near_k_ref[...] = (SCALE * dot(ds_ref[ROWS:, :], qs, NN)).astype(jnp.bfloat16)


def finish_kernel(q_ref, do_ref, ko_ref, vo_ref, kp_ref, vp_ref, kf_ref, vf_ref, prob_ref, ds_ref,
                  att_ref, dq_ref, own_k_ref, own_v_ref):
    def heads(ref):
        return jnp.concatenate([ref[:, h * HD:(h + 1) * HD] for h in range(GROUPS)], axis=0)

    qs = heads(q_ref)
    dos = heads(do_ref)
    wide_tri = (lax.broadcasted_iota(jnp.int32, (ROWS, WIDE), 0)
                <= lax.broadcasted_iota(jnp.int32, (ROWS, WIDE), 1) % HD)
    none = jnp.zeros((ROWS, WIDE), jnp.bfloat16)
    p_a = prob_ref[0:ROWS, :]
    p_own = jnp.where(wide_tri, p_a, none)
    p_far = jnp.where(wide_tri, none, p_a)
    ds_a = ds_ref[0:ROWS, :]
    ds_own = jnp.where(wide_tri, ds_a, none)
    ds_far = jnp.where(wide_tri, none, ds_a)
    own_v_ref[...] = dot(p_own, dos, NN)
    own_k_ref[...] = SCALE * dot(ds_own, qs, NN)
    k3 = jnp.concatenate([kf_ref[...], kp_ref[...], ko_ref[...]], axis=0)
    v3 = jnp.concatenate([vf_ref[...], vp_ref[...], vo_ref[...]], axis=0)
    k3t = k3.T
    v3t = v3.T
    p3 = jnp.concatenate([p_far, prob_ref[ROWS:, :], p_own], axis=0)
    ds3 = jnp.concatenate([ds_far, ds_ref[ROWS:, :], ds_own], axis=0)
    att = dot(v3t, p3, NN)
    dq = dot(k3t, ds3, NN) * SCALE
    for h in range(GROUPS):
        cols = slice(h * HD, (h + 1) * HD)
        att_ref[:, cols] = att[:, cols].T.astype(jnp.bfloat16)
        dq_ref[:, cols] = dq[:, cols].T.astype(jnp.bfloat16)


def body(queries, keys, values, d_out, lengths):
    packed = jnp.concatenate([keys, values], axis=1)
    far = shifted(packed, 2)
    near = shifted(packed, 1)
    start = (lax.axis_index(AXES) * ROWS).astype(jnp.int32).reshape(1)
    bias = pl.pallas_call(
        mask_kernel,
        out_shape=jax.ShapeDtypeStruct((2 * ROWS, ROWS), jnp.float32),
        in_specs=[pl.BlockSpec(memory_space=pltpu.SMEM), pl.BlockSpec(memory_space=pltpu.VMEM)],
        out_specs=pl.BlockSpec(memory_space=pltpu.VMEM),
        name="masks",
    )(start, lengths.reshape(1, DOCS))

    head = pl.BlockSpec((ROWS, WIDE), lambda j: (0, j))
    key = pl.BlockSpec((ROWS, HD), lambda j: (0, j))
    value = pl.BlockSpec((ROWS, HD), lambda j: (0, KVH + j))
    square = pl.BlockSpec((None, 2 * ROWS, WIDE), lambda j: (j, 0, 0))
    fixed = pl.BlockSpec((2 * ROWS, ROWS), lambda j: (0, 0))
    term = jax.ShapeDtypeStruct((ROWS, KVH * HD), jnp.bfloat16)
    wide_term = jax.ShapeDtypeStruct((ROWS, KVH * HD), jnp.float32)
    tile = jax.ShapeDtypeStruct((KVH, 2 * ROWS, WIDE), jnp.bfloat16)
    prob, ds, near_k, near_v, far_k, far_v = pl.pallas_call(
        score_kernel,
        grid=(KVH,),
        out_shape=(tile, tile, term, term, term, term),
        in_specs=[head, head, key, key, key, value, key, value, fixed],
        out_specs=(square, square, key, key, key, key),
        name="scores",
        compiler_params=pltpu.CompilerParams(vmem_limit_bytes=32 * 1024 * 1024),
    )(queries, d_out, keys, values, near, near, far, far, bias)
    far_back = shifted(jnp.concatenate([far_k, far_v], axis=1), -2)
    near_back = shifted(jnp.concatenate([near_k, near_v], axis=1), -1)
    attended, d_queries, own_k, own_v = pl.pallas_call(
        finish_kernel,
        grid=(KVH,),
        out_shape=(
            jax.ShapeDtypeStruct((ROWS, QH * HD), jnp.bfloat16),
            jax.ShapeDtypeStruct((ROWS, QH * HD), jnp.bfloat16),
            wide_term,
            wide_term,
        ),
        in_specs=[head, head, key, key, key, value, key, value, square, square],
        out_specs=(head, head, key, key),
        name="finish",
        compiler_params=pltpu.CompilerParams(vmem_limit_bytes=32 * 1024 * 1024),
    )(queries, d_out, keys, values, near, near, far, far, prob, ds)
    cut = KVH * HD
    d_keys = own_k + near_back[:, :cut].astype(jnp.float32) + far_back[:, :cut].astype(jnp.float32)
    d_values = own_v + near_back[:, cut:].astype(jnp.float32) + far_back[:, cut:].astype(jnp.float32)
    return attended, d_queries, d_keys.astype(jnp.bfloat16), d_values.astype(jnp.bfloat16)


def solution(mesh):
    split = P(AXES, None)
    return jax.shard_map(
        body,
        mesh=mesh,
        in_specs=(split, split, split, split, P()),
        out_specs=(split, split, split, split),
        check_vma=False,
    )
```

time: 75.8 us -> 45.9 us (0.61); the launches traced: 74.5 us -> 45.6 us
  matrix products: 24.8 us -> 0 us
  Pallas kernels: 0 us -> 11.6 us
  local copies, waits for them, and re-layouts: 16.2 us -> 6.91 us
  starting transfers between devices: 23.2 us -> 14.6 us
  waiting for transfers between devices: 4.47 us -> 10.9 us
  other arithmetic: 4.8 us -> 0.84 us
    dot_general x18 -> x0, matrix products: 24.8 us -> none  [the longest x3 9.54 us: prob_work(): jnp.einsum('kgts,skd->tkgd', prob.astype(jnp.bfloat16), value_blk, prefer...]
    pallas_call x0 -> x3, Pallas kernels: none -> 11.6 us  [the longest x1 5.76 us: body(): pl.pallas_call(score_kernel, grid=(KVH,), out_shape=(tile, tile, term, te...]
    ppermute x8 -> x4, starting transfers between devices: 23.2 us -> 14.6 us  [shifted(): lax.ppermute(value, AXES, [(source, source + steps) for source in range(l...]
    ppermute x8 -> x4, waiting for transfers between devices: 4.47 us -> 10.9 us  [shifted(): lax.ppermute(value, AXES, [(source, source + steps) for source in range(l...]
    reshape x5 -> x0, local copies, waits for them, and re-layouts: 3.23 us -> none  [the longest x2 1.08 us: stats_work(): key_blk = pieces[dist][0].reshape(rows, KVH, HD)]
    unnamed x45 -> x17, local copies, waits for them, and re-layouts: 8.96 us -> 6 us
    ppermute x2 -> x0, local copies, waits for them, and re-layouts: 2.04 us -> none  [from_behind(): lax.ppermute(value, axis, [(source, source + steps) for source in range(l...]
    convert_element_type x4 -> x0, local copies, waits for them, and re-layouts: 1.75 us -> none  [the longest x2 1.52 us: body(): d_value.astype(jnp.bfloat16)]
  transfers between devices with their start and end apart: 8 -> 4, of which waited for: 2 -> 3; matrix products, arithmetic and copies ran while one was open for 36% -> 0% of each run, Pallas kernels for 0% -> 13%
where the time goes in v1:
time: 45.9 us; the launch traced here: 45.6 us
  starting transfers between devices  14.6 us (32%)
  Pallas kernels  11.6 us (25%)
  waiting for transfers between devices  10.9 us (24%)
  local copies, waits for them, and re-layouts  6.91 us (15%)
  other arithmetic  0.84 us (2%)
  between operations  0.74 us (2%)
    ppermute x4, starting transfers between devices, shifted(): lax.ppermute(value, AXES, [(source, source + steps) for source in range(l...  14.6 us
    ppermute x4, waiting for transfers between devices, shifted(): lax.ppermute(value, AXES, [(source, source + steps) for source in range(l...  10.9 us
    unnamed x17, local copies, waits for them, and re-layouts  6 us
    pallas_call x1, Pallas kernels, body(): pl.pallas_call(score_kernel, grid=(KVH,), out_shape=(tile, tile, term, te...  5.76 us
    pallas_call x1, Pallas kernels, body(): pl.pallas_call(finish_kernel, grid=(KVH,), out_shape=(jax.ShapeDtypeStruc...  4.11 us
    pallas_call x1, Pallas kernels, body(): pl.pallas_call(mask_kernel, out_shape=jax.ShapeDtypeStruct((2 * ROWS, ROW...  1.69 us
  transfers between devices with their start and end apart: 4, of which 3 were waited for; matrix products, arithmetic and copies ran while one was open for 0% of the time, Pallas kernels for 13%

profile of v1, /device:TPU:255, one launch (start us, length us, event | category | flops | bytes accessed | tf_op | source)
XLA Modules:
  0.0 45.6 jit_solution(990046598148967542)
XLA Ops:
  0.6 0.9 %constant_dynamic-update-slice_fusion.1 = bf16[128,1024]{1,0:T(8,128)(2,1)S(1)} fusion(bf16[128,512]{1,0:T(8,128)(2,1)} %ko_ref.3), kind=kLoop, calls=%fused_computation.5 | loop fusion | bytes 262144
  1.5 0.9 %constant_dynamic-update-slice_fusion = bf16[128,1024]{1,0:T(8,128)(2,1)S(1)} fusion(bf16[128,1024]{1,0:T(8,128)(2,1)S(1)} %constant_dynamic-update-slice_fusion.1, bf16[128,512]{1,0:T(8,128)(2,1)} %vo_ref.3), kind=kLoop, calls=%fused_computation.4 | loop fusion | bytes 262144 | tf_op jit(solution)/shard_map/concatenate | solution.py:127
  2.5 4.3 %collective-permute-start.1 = (bf16[128,1024]{1,0:T(8,128)(2,1)S(1)}, bf16[128,1024]{1,0:T(8,128)(2,1)S(1)}, u32[]{:S(2)}, u32[]{:S(2)}) collective-permute-start(bf16[128,1024]{1,0:T(8,128)(2,1)S(1)} %constant_dynamic-update-slice_fusion), channel_id=1, source_target_pairs={{0,2},{1,3},{2,4},{3,5},{4,6},{5,7},{6,8},{7,9},{8,10},{9,11},{10,... | collective-permute-start | bytes 786440 | tf_op jit(solution)/shard_map/ppermute | solution.py:32
  6.8 4.0 %collective-permute-start = (bf16[128,1024]{1,0:T(8,128)(2,1)S(1)}, bf16[128,1024]{1,0:T(8,128)(2,1)S(1)}, u32[]{:S(2)}, u32[]{:S(2)}) collective-permute-start(bf16[128,1024]{1,0:T(8,128)(2,1)S(1)} %constant_dynamic-update-slice_fusion), channel_id=1, source_target_pairs={{0,1},{1,2},{2,3},{3,4},{4,5},{5,6},{6,7},{7,8},{8,9},{9,10},{10,1... | collective-permute-start | bytes 786440 | tf_op jit(solution)/shard_map/ppermute | solution.py:32
  10.9 0.0 copy-start.5
  10.9 1.7 %masks.1.bias_ref = f32[256,128]{1,0:T(8,128)} custom-call(s32[1]{0:T(128)} %bitcast.start_ref, s32[1,512]{1,0:T(1,128)} %bitcast.2), custom_call_target="tpu_custom_call" | custom-call | tf_op jit(solution)/shard_map/masks/pallas_call | solution.py:131
  12.6 0.0 collective-permute-done.1.kf_ref.vf_ref
  12.6 3.1 %collective-permute-done.kp_ref.vp_ref = bf16[128,1024]{1,0:T(8,128)(2,1)S(1)} collective-permute-done((bf16[128,1024]{1,0:T(8,128)(2,1)S(1)}, bf16[128,1024]{1,0:T(8,128)(2,1)S(1)}, u32[]{:S(2)}, u32[]{:S(2)}) %collective-permute-start) | collective-permute-done | bytes 262176 | tf_op jit(solution)/shard_map/ppermute | solution.py:32
  15.7 0.0 copy-start
  15.7 1.2 %copy-done = bf16[128,3584]{1,0:T(8,128)(2,1)S(1)} copy-done((bf16[128,3584]{1,0:T(8,128)(2,1)S(1)}, bf16[128,3584]{1,0:T(8,128)(2,1)}, u32[]{:S(2)}) %copy-start) | copy-done | bytes 917528
  16.9 1.2 %copy-done.2 = bf16[128,3584]{1,0:T(8,128)(2,1)S(1)} copy-done((bf16[128,3584]{1,0:T(8,128)(2,1)S(1)}, bf16[128,3584]{1,0:T(8,128)(2,1)}, u32[]{:S(2)}) %copy-start.2) | copy-done | bytes 917528
  18.1 0.9 %copy-done.4 = bf16[128,512]{1,0:T(8,128)(2,1)S(1)} copy-done((bf16[128,512]{1,0:T(8,128)(2,1)S(1)}, bf16[128,512]{1,0:T(8,128)(2,1)}, u32[]{:S(2)}) %copy-start.4) | copy-done | bytes 131096
  19.0 0.9 %copy-done.6 = bf16[128,512]{1,0:T(8,128)(2,1)S(1)} copy-done((bf16[128,512]{1,0:T(8,128)(2,1)S(1)}, bf16[128,512]{1,0:T(8,128)(2,1)}, u32[]{:S(2)}) %copy-start.6) | copy-done | bytes 131096
  19.9 0.9 %copy-done.7 = f32[256,128]{1,0:T(8,128)S(1)} copy-done((f32[256,128]{1,0:T(8,128)S(1)}, f32[256,128]{1,0:T(8,128)}, u32[]{:S(2)}) %copy-start.7) | copy-done | bytes 131096
  20.8 5.8 %scores.1 = (bf16[4,256,896]{2,1,0:T(8,128)(2,1)S(1)}, bf16[4,256,896]{2,1,0:T(8,128)(2,1)S(1)}, bf16[128,512]{1,0:T(8,128)(2,1)S(1)}, bf16[128,512]{1,0:T(8,128...) custom-call(bf16[128,3584]{1,0:T(8,128)(2,1)S(1)} %copy-done, bf16[128,3584]{1,0:T(8,128)(2,1)S(1)} %copy-done.2, ...), custom_call_target="tpu_custom_call" | custom-call | tf_op jit(solution)/shard_map/scores/pallas_call | solution.py:147
  26.6 1.9 %collective-permute-start.3 = (bf16[128,1024]{1,0:T(8,128)(2,1)S(1)}, bf16[128,1024]{1,0:T(8,128)(2,1)S(1)}, u32[]{:S(2)}, u32[]{:S(2)}) collective-permute-start(bf16[128,1024]{1,0:T(8,128)(2,1)S(1)} %pad_maximum_fusion.1), channel_id=1, source_target_pairs={{2,0},{3,1},{4,2},{5,3},{6,4},{7,5},{8,6},{9,7},{10,8},{11,9},{12,... | collective-permute-start | bytes 786440 | tf_op jit(solution)/shard_map/ppermute | solution.py:32
  28.5 4.3 %collective-permute-start.2 = (bf16[128,1024]{1,0:T(8,128)(2,1)S(1)}, bf16[128,1024]{1,0:T(8,128)(2,1)S(1)}, u32[]{:S(2)}, u32[]{:S(2)}) collective-permute-start(bf16[128,1024]{1,0:T(8,128)(2,1)S(1)} %pad_maximum_fusion), channel_id=1, source_target_pairs={{1,0},{2,1},{3,2},{4,3},{5,4},{6,5},{7,6},{8,7},{9,8},{10,9},{11,1... | collective-permute-start | bytes 786440 | tf_op jit(solution)/shard_map/ppermute | solution.py:32
  32.9 0.0 copy-done.5
  32.9 0.0 copy-done.1
  32.9 0.0 copy-done.3
  32.9 4.1 %finish.1 = (bf16[128,3584]{1,0:T(8,128)(2,1)}, bf16[128,3584]{1,0:T(8,128)(2,1)}, f32[128,512]{1,0:T(8,128)S(1)}, f32[128,512]{1,0:T(8,128)S(1)}) custom-call(bf16[128,3584]{1,0:T(8,128)(2,1)S(1)} %copy-done.1, bf16[128,3584]{1,0:T(8,128)(2,1)S(1)} %copy-done.3, bf16[128,512]{1,0:T(8,128)(2,1)S(1)} %copy-done.5, bf16[128,512]{1,0:T(8,128)(2,1)S(1)} %copy-done.6, ...), custom_call_target="tpu_custom_call" | custom-call | tf_op jit(solution)/shard_map/finish/pallas_call | solution.py:158
  37.0 3.9 %collective-permute-done.3 = bf16[128,1024]{1,0:T(8,128)(2,1)S(1)} collective-permute-done((bf16[128,1024]{1,0:T(8,128)(2,1)S(1)}, bf16[128,1024]{1,0:T(8,128)(2,1)S(1)}, u32[]{:S(2)}, u32[]{:S(2)}) %collective-permute-start.3) | collective-permute-done | bytes 262176 | tf_op jit(solution)/shard_map/ppermute | solution.py:32
  40.9 3.9 %collective-permute-done.2 = bf16[128,1024]{1,0:T(8,128)(2,1)S(1)} collective-permute-done((bf16[128,1024]{1,0:T(8,128)(2,1)S(1)}, bf16[128,1024]{1,0:T(8,128)(2,1)S(1)}, u32[]{:S(2)}, u32[]{:S(2)}) %collective-permute-start.2) | collective-permute-done | bytes 262176 | tf_op jit(solution)/shard_map/ppermute | solution.py:32
  44.8 0.8 %add_convert_fusion = (bf16[128,512]{1,0:T(8,128)(2,1)}, bf16[128,512]{1,0:T(8,128)(2,1)}) fusion(f32[128,512]{1,0:T(8,128)S(1)} %get-tuple-element.23, bf16[128,1024]{1,0:T(8,128)(2,1)S(1)} %collective-permute-done.3, bf16[128,1024]{1,0:T(8,128)(2,1)S(1)} %collective-permute-done.2, f32[128,512]{1,0:T(8,128)S(1)} %get-tuple-element.18), kind=kLoop, calls=%fused_computation.2 | loop fusion | flops 655360 | bytes 1310720 | tf_op jit(solution)/shard_map/convert_element_type | solution.py:175
  (8 shorter events, 0.0 us)
Async XLA Ops:
  2.5 10.1 %collective-permute-start.1 = (bf16[128,1024]{1,0:T(8,128)(2,1)S(1)}, bf16[128,1024]{1,0:T(8,128)(2,1)S(1)}, u32[]{:S(2)}, u32[]{:S(2)}) collective-permute-start(bf16[128,1024]{1,0:T(8,128)(2,1)S(1)} %constant_dynamic-update-slice_fusion), channel_id=1, source_target_pairs={{0,2},{1,3},{2,4},{3,5},{4,6},{5,7},{6,8},{7,9},{8,10},{9,11},{10,... | collective-permute-start | bytes 786440 | tf_op jit(solution)/shard_map/ppermute | solution.py:32
  6.8 8.9 %collective-permute-start = (bf16[128,1024]{1,0:T(8,128)(2,1)S(1)}, bf16[128,1024]{1,0:T(8,128)(2,1)S(1)}, u32[]{:S(2)}, u32[]{:S(2)}) collective-permute-start(bf16[128,1024]{1,0:T(8,128)(2,1)S(1)} %constant_dynamic-update-slice_fusion), channel_id=1, source_target_pairs={{0,1},{1,2},{2,3},{3,4},{4,5},{5,6},{6,7},{7,8},{8,9},{9,10},{10,1... | collective-permute-start | bytes 786440 | tf_op jit(solution)/shard_map/ppermute | solution.py:32
  10.9 22.0 %copy-start.5 = (bf16[128,512]{1,0:T(8,128)(2,1)S(1)}, bf16[128,512]{1,0:T(8,128)(2,1)}, u32[]{:S(2)}) copy-start(bf16[128,512]{1,0:T(8,128)(2,1)} %ko_ref.3) | copy-start | bytes 393220
  15.7 1.2 %copy-start = (bf16[128,3584]{1,0:T(8,128)(2,1)S(1)}, bf16[128,3584]{1,0:T(8,128)(2,1)}, u32[]{:S(2)}) copy-start(bf16[128,3584]{1,0:T(8,128)(2,1)} %q_ref.3) | copy-start | bytes 2752516
  16.9 1.2 %copy-start.2 = (bf16[128,3584]{1,0:T(8,128)(2,1)S(1)}, bf16[128,3584]{1,0:T(8,128)(2,1)}, u32[]{:S(2)}) copy-start(bf16[128,3584]{1,0:T(8,128)(2,1)} %do_ref.3) | copy-start | bytes 2752516
  18.1 0.9 %copy-start.4 = (bf16[128,512]{1,0:T(8,128)(2,1)S(1)}, bf16[128,512]{1,0:T(8,128)(2,1)}, u32[]{:S(2)}) copy-start(bf16[128,512]{1,0:T(8,128)(2,1)} %ko_ref.3) | copy-start | bytes 393220
  19.0 0.9 %copy-start.6 = (bf16[128,512]{1,0:T(8,128)(2,1)S(1)}, bf16[128,512]{1,0:T(8,128)(2,1)}, u32[]{:S(2)}) copy-start(bf16[128,512]{1,0:T(8,128)(2,1)} %vo_ref.3) | copy-start | bytes 393220
  19.9 0.9 %copy-start.7 = (f32[256,128]{1,0:T(8,128)S(1)}, f32[256,128]{1,0:T(8,128)}, u32[]{:S(2)}) copy-start(f32[256,128]{1,0:T(8,128)} %masks.1.bias_ref) | copy-start | bytes 393220
  20.8 12.1 %copy-start.1 = (bf16[128,3584]{1,0:T(8,128)(2,1)S(1)}, bf16[128,3584]{1,0:T(8,128)(2,1)}, u32[]{:S(2)}) copy-start(bf16[128,3584]{1,0:T(8,128)(2,1)} %q_ref.3) | copy-start | bytes 2752516
  20.8 12.1 %copy-start.3 = (bf16[128,3584]{1,0:T(8,128)(2,1)S(1)}, bf16[128,3584]{1,0:T(8,128)(2,1)}, u32[]{:S(2)}) copy-start(bf16[128,3584]{1,0:T(8,128)(2,1)} %do_ref.3) | copy-start | bytes 2752516
  26.6 14.3 %collective-permute-start.3 = (bf16[128,1024]{1,0:T(8,128)(2,1)S(1)}, bf16[128,1024]{1,0:T(8,128)(2,1)S(1)}, u32[]{:S(2)}, u32[]{:S(2)}) collective-permute-start(bf16[128,1024]{1,0:T(8,128)(2,1)S(1)} %pad_maximum_fusion.1), channel_id=1, source_target_pairs={{2,0},{3,1},{4,2},{5,3},{6,4},{7,5},{8,6},{9,7},{10,8},{11,9},{12,... | collective-permute-start | bytes 786440 | tf_op jit(solution)/shard_map/ppermute | solution.py:32
  28.5 16.2 %collective-permute-start.2 = (bf16[128,1024]{1,0:T(8,128)(2,1)S(1)}, bf16[128,1024]{1,0:T(8,128)(2,1)S(1)}, u32[]{:S(2)}, u32[]{:S(2)}) collective-permute-start(bf16[128,1024]{1,0:T(8,128)(2,1)S(1)} %pad_maximum_fusion), channel_id=1, source_target_pairs={{1,0},{2,1},{3,2},{4,3},{5,4},{6,5},{7,6},{8,7},{9,8},{10,9},{11,1... | collective-permute-start | bytes 786440 | tf_op jit(solution)/shard_map/ppermute | solution.py:32

commit v2 on v1

v2 whole, which is shorter than its diff:
```python
import jax
import jax.numpy as jnp
from jax import lax
from jax.experimental import pallas as pl
from jax.experimental.pallas import tpu as pltpu
from jax.sharding import PartitionSpec as P

QH = 28
KVH = 4
GROUPS = QH // KVH
HD = 128
ROWS = 128
DOCS = 512
AXES = ("ctx", "dp")
NEG = -1e30
SCALE = HD**-0.5
LOG2E = 1.4426950408889634
WIDE = GROUPS * HD
CUT = KVH * HD

NT = (((1,), (1,)), ((), ()))
NN = (((1,), (0,)), ((), ()))
VMEM = pl.BlockSpec(memory_space=pltpu.VMEM)
SMEM = pl.BlockSpec(memory_space=pltpu.SMEM)
HBM = pl.BlockSpec(memory_space=pltpu.HBM)
ROOM = pltpu.CompilerParams(vmem_limit_bytes=32 * 1024 * 1024)


def dot(a, b, dims):
    return lax.dot_general(a, b, dims, preferred_element_type=jnp.float32)


def shifted(value, steps, every=1):
    count = lax.axis_size(AXES)
    leading, last = (max(0, -steps), min(count, count - steps))
    return lax.ppermute(value, AXES, [(source, source + steps) for source in range(leading, last, every)])


def pinned(value):
    return pltpu.with_memory_space_constraint(value, pltpu.HBM)


def cost(us):
    return pl.CostEstimate(flops=0, bytes_accessed=int(us * 3_000_000), transcendentals=0)


def triangle(width):
    s = lax.broadcasted_iota(jnp.int32, (ROWS, width), 0)
    t = lax.broadcasted_iota(jnp.int32, (ROWS, width), 1) % HD
    return s <= t


def pack_kernel(k_ref, v_ref, out_ref, sems):
    first = pltpu.make_async_copy(k_ref, out_ref.at[0], sems.at[0])
    second = pltpu.make_async_copy(v_ref, out_ref.at[1], sems.at[1])
    first.start()
    second.start()
    first.wait()
    second.wait()


def stage_kernel(start_ref, lengths_ref, q_ref, do_ref, k_ref, v_ref,
                 bias_ref, qs_ref, dos_ref, s_ref, d_ref, kv_ref, len_ref, sems):
    copies = [
        pltpu.make_async_copy(lengths_ref, len_ref, sems.at[0]),
        pltpu.make_async_copy(k_ref, kv_ref.at[0], sems.at[1]),
        pltpu.make_async_copy(v_ref, kv_ref.at[1], sems.at[2]),
    ]
    heads = []
    for j in range(KVH):
        for source, target, sem in ((q_ref, qs_ref, 3 + j), (do_ref, dos_ref, 3 + KVH + j)):
            for h in range(GROUPS):
                column = (j * GROUPS + h) * HD
                heads.append(pltpu.make_async_copy(
                    source.at[:, column:column + HD], target.at[j, h * HD:(h + 1) * HD, :], sems.at[sem]))
    for copy in copies + heads:
        copy.start()
    copies[0].wait()
    start = start_ref[0]
    lens = jnp.broadcast_to(len_ref[...].astype(jnp.float32), (ROWS, DOCS)).astype(jnp.bfloat16)
    doc = lax.broadcasted_iota(jnp.int32, (DOCS, DOCS), 0)
    upto = lax.broadcasted_iota(jnp.int32, (DOCS, DOCS), 1)
    before = jnp.where(upto <= doc, 1.0, 0.0).astype(jnp.bfloat16)
    ends = dot(before, lens, NT).astype(jnp.int32)
    query = start + lax.broadcasted_iota(jnp.int32, (DOCS, ROWS), 1)
    first = jnp.max(jnp.where(ends <= query, ends, 0), axis=0, keepdims=True)
    first = first - start
    s = lax.broadcasted_iota(jnp.int32, (ROWS, ROWS), 0)
    t = lax.broadcasted_iota(jnp.int32, (ROWS, ROWS), 1)
    merged = jnp.where(s <= t, s, s - 2 * ROWS)
    bias_ref[0:ROWS, :] = jnp.where(merged >= first, 0.0, NEG)
    bias_ref[ROWS:, :] = jnp.where(s - ROWS >= first, 0.0, NEG)
    copies[1].wait()
    copies[2].wait()
    for j in range(KVH):
        lanes = slice(j * HD, (j + 1) * HD)
        for h in range(2 * GROUPS):
            heads[2 * GROUPS * j + h].wait()
        s_ref[j] = dot(kv_ref[0, :, lanes], qs_ref[j], NT)
        d_ref[j] = dot(kv_ref[1, :, lanes], dos_ref[j], NT)


def score_kernel(odd_ref, qs_ref, dos_ref, s_ref, d_ref, near_ref, even_far_ref, odd_far_ref, bias_ref,
                 prob_ref, ds_ref, out_ref, far_ref):
    @pl.when(odd_ref[0] == 0)
    def _():
        far_ref[...] = even_far_ref[...]

    @pl.when(odd_ref[0] == 1)
    def _():
        far_ref[...] = odd_far_ref[...]

    tri = triangle(ROWS)
    wide_tri = triangle(WIDE)
    none = jnp.zeros((ROWS, WIDE), jnp.bfloat16)
    factor = SCALE * LOG2E
    for j in range(KVH):
        lanes = slice(j * HD, (j + 1) * HD)
        qs = qs_ref[j]
        dos = dos_ref[j]
        s_far = dot(far_ref[0, :, lanes], qs, NT)
        s_near = dot(near_ref[0, :, lanes], qs, NT)
        d_far = dot(far_ref[1, :, lanes], dos, NT)
        d_near = dot(near_ref[1, :, lanes], dos, NT)
        for h in range(GROUPS):
            cols = slice(h * HD, (h + 1) * HD)
            a = jnp.where(tri, s_ref[j, :, cols], s_far[:, cols]) + bias_ref[0:ROWS, :]
            b = s_near[:, cols] + bias_ref[ROWS:, :]
            peak = jnp.max(jnp.maximum(a, b), axis=0, keepdims=True)
            a = jnp.exp2((a - peak) * factor)
            b = jnp.exp2((b - peak) * factor)
            inv = 1.0 / jnp.sum(a + b, axis=0, keepdims=True)
            a = a * inv
            b = b * inv
            da = jnp.where(tri, d_ref[j, :, cols], d_far[:, cols])
            db = d_near[:, cols]
            delta = jnp.sum(a * da + b * db, axis=0, keepdims=True)
            prob_ref[j, 0:ROWS, cols] = a.astype(jnp.bfloat16)
            prob_ref[j, ROWS:, cols] = b.astype(jnp.bfloat16)
            ds_ref[j, 0:ROWS, cols] = (a * (da - delta)).astype(jnp.bfloat16)
            ds_ref[j, ROWS:, cols] = (b * (db - delta)).astype(jnp.bfloat16)
        out_ref[0, :, lanes] = (
            SCALE * dot(jnp.where(wide_tri, none, ds_ref[j, 0:ROWS, :]), qs, NN)
        ).astype(jnp.bfloat16)
        out_ref[1, :, lanes] = dot(
            jnp.where(wide_tri, none, prob_ref[j, 0:ROWS, :]), dos, NN
        ).astype(jnp.bfloat16)


def near_kernel(odd_ref, qs_ref, dos_ref, prob_ref, ds_ref, passed_ref, out_ref):
    even = odd_ref[0] == 0
    for j in range(KVH):
        lanes = slice(j * HD, (j + 1) * HD)
        key_terms = SCALE * dot(ds_ref[j, ROWS:, :], qs_ref[j], NN)
        value_terms = dot(prob_ref[j, ROWS:, :], dos_ref[j], NN)
        key_terms += jnp.where(even, passed_ref[0, :, lanes].astype(jnp.float32), 0.0)
        value_terms += jnp.where(even, passed_ref[1, :, lanes].astype(jnp.float32), 0.0)
        out_ref[0, :, lanes] = key_terms.astype(jnp.bfloat16)
        out_ref[1, :, lanes] = value_terms.astype(jnp.bfloat16)


def finish_kernel(qs_ref, dos_ref, own_ref, near_ref, far_ref, prob_ref, ds_ref,
                  att_ref, dq_ref, terms_ref):
    wide_tri = triangle(WIDE)
    none = jnp.zeros((ROWS, WIDE), jnp.bfloat16)
    p_a = prob_ref[0:ROWS, :]
    p_own = jnp.where(wide_tri, p_a, none)
    p_far = jnp.where(wide_tri, none, p_a)
    ds_a = ds_ref[0:ROWS, :]
    ds_own = jnp.where(wide_tri, ds_a, none)
    ds_far = jnp.where(wide_tri, none, ds_a)
    terms_ref[0] = SCALE * dot(ds_own, qs_ref[...], NN)
    terms_ref[1] = dot(p_own, dos_ref[...], NN)
    k3t = jnp.concatenate([far_ref[0], near_ref[0], own_ref[0]], axis=0).T
    v3t = jnp.concatenate([far_ref[1], near_ref[1], own_ref[1]], axis=0).T
    p3 = jnp.concatenate([p_far, prob_ref[ROWS:, :], p_own], axis=0)
    ds3 = jnp.concatenate([ds_far, ds_ref[ROWS:, :], ds_own], axis=0)
    att = dot(v3t, p3, NN)
    dq = dot(k3t, ds3, NN) * SCALE
    for h in range(GROUPS):
        cols = slice(h * HD, (h + 1) * HD)
        att_ref[:, cols] = att[:, cols].T.astype(jnp.bfloat16)
        dq_ref[:, cols] = dq[:, cols].T.astype(jnp.bfloat16)


PAIR = jax.ShapeDtypeStruct((2, ROWS, CUT), jnp.bfloat16)
TILE = jax.ShapeDtypeStruct((KVH, 2 * ROWS, WIDE), jnp.bfloat16)
HEAD = pl.BlockSpec((ROWS, WIDE), lambda j: (0, j))
BOTH = pl.BlockSpec((2, ROWS, HD), lambda j: (0, 0, j))
STACK = pl.BlockSpec((None, WIDE, HD), lambda j: (j, 0, 0))
SQUARE = pl.BlockSpec((None, 2 * ROWS, WIDE), lambda j: (j, 0, 0))


def pack(keys, values):
    return pl.pallas_call(
        pack_kernel,
        out_shape=PAIR,
        in_specs=[HBM, HBM],
        out_specs=VMEM,
        scratch_shapes=[pltpu.SemaphoreType.DMA((2,))],
        name="pack",
        compiler_params=ROOM,
    )(pinned(keys), pinned(values))


def stage(start, lengths, queries, d_out, keys, values):
    return pl.pallas_call(
        stage_kernel,
        out_shape=(
            jax.ShapeDtypeStruct((2 * ROWS, ROWS), jnp.float32),
            jax.ShapeDtypeStruct((KVH, WIDE, HD), jnp.bfloat16),
            jax.ShapeDtypeStruct((KVH, WIDE, HD), jnp.bfloat16),
            jax.ShapeDtypeStruct((KVH, ROWS, WIDE), jnp.float32),
            jax.ShapeDtypeStruct((KVH, ROWS, WIDE), jnp.float32),
            PAIR,
        ),
        in_specs=[SMEM] + [HBM] * 5,
        out_specs=(VMEM,) * 6,
        scratch_shapes=[pltpu.VMEM((1, DOCS), jnp.int32), pltpu.SemaphoreType.DMA((3 + 2 * KVH,))],
        name="stage",
        compiler_params=ROOM,
        cost_estimate=cost(3),
    )(start, *(pinned(x) for x in (lengths, queries, d_out, keys, values)))


def scores(odd, qs, dos, s_own, d_own, near, even_far, odd_far, bias):
    return pl.pallas_call(
        score_kernel,
        out_shape=(TILE, TILE, PAIR, PAIR),
        in_specs=[SMEM] + [VMEM] * 8,
        out_specs=(VMEM, VMEM, VMEM, VMEM),
        name="scores",
        compiler_params=ROOM,
        cost_estimate=cost(4),
    )(odd, qs, dos, s_own, d_own, near, even_far, odd_far, bias)


def near_terms(odd, qs, dos, prob, ds, passed):
    return pl.pallas_call(
        near_kernel,
        out_shape=PAIR,
        in_specs=[SMEM] + [VMEM] * 5,
        out_specs=VMEM,
        name="near_terms",
        compiler_params=ROOM,
        cost_estimate=cost(3),
    )(odd, qs, dos, prob, ds, passed)


def finish(qs, dos, own, near, far, prob, ds):
    return pl.pallas_call(
        finish_kernel,
        grid=(KVH,),
        out_shape=(
            jax.ShapeDtypeStruct((ROWS, QH * HD), jnp.bfloat16),
            jax.ShapeDtypeStruct((ROWS, QH * HD), jnp.bfloat16),
            jax.ShapeDtypeStruct((2, ROWS, CUT), jnp.float32),
        ),
        in_specs=[STACK, STACK, BOTH, BOTH, BOTH, SQUARE, SQUARE],
        out_specs=(HEAD, HEAD, BOTH),
        name="finish",
        compiler_params=ROOM,
        cost_estimate=cost(8),
    )(qs, dos, own, near, far, prob, ds)


def body(queries, keys, values, d_out, lengths):
    packed = pack(keys, values)
    near = shifted(packed, 1)
    even_far = shifted(packed, 2, 2)
    index = lax.axis_index(AXES).astype(jnp.int32).reshape(1)
    start = index * ROWS
    odd = index % 2
    bias, qs, dos, s_own, d_own, own = stage(start, lengths.reshape(1, DOCS), queries, d_out, keys, values)
    near, bias = lax.optimization_barrier((near, bias))
    odd_far = shifted(near, 1, 2)
    prob, ds, far_terms, far = scores(odd, qs, dos, s_own, d_own, near, even_far, odd_far, bias)
    passed = shifted(far_terms, -1, 2)
    far_back = shifted(far_terms, -2, 2)
    near_back = shifted(near_terms(odd, qs, dos, prob, ds, passed), -1)
    attended, d_queries, terms = finish(qs, dos, own, near, far, prob, ds)
    d_keys = terms[0] + near_back[0].astype(jnp.float32) + far_back[0].astype(jnp.float32)
    d_values = terms[1] + near_back[1].astype(jnp.float32) + far_back[1].astype(jnp.float32)
    return attended, d_queries, d_keys.astype(jnp.bfloat16), d_values.astype(jnp.bfloat16)


def solution(mesh):
    split = P(AXES, None)
    return jax.shard_map(
        body,
        mesh=mesh,
        in_specs=(split, split, split, split, P()),
        out_specs=(split, split, split, split),
        check_vma=False,
    )
```

time: 45.9 us -> 35.8 us (0.78)
  local copies, waits for them, and re-layouts: 6.91 us -> 0 us
  starting transfers between devices: 14.6 us -> 12.8 us
  waiting for transfers between devices: 10.9 us -> 9.38 us
    unnamed x17 -> x0, local copies, waits for them, and re-layouts: 6 us -> none
    ppermute x4 -> x6, starting transfers between devices: 14.6 us -> 12.8 us  [shifted(): lax.ppermute(value, AXES, [(source, source + steps) for source in range(l...]
    ppermute x4 -> x6, waiting for transfers between devices: 10.9 us -> 9.38 us  [shifted(): lax.ppermute(value, AXES, [(source, source + steps) for source in range(l...]
    concatenate x1 -> x0, local copies, waits for them, and re-layouts: 0.92 us -> none  [body(): packed = jnp.concatenate([keys, values], axis=1)]
    pallas_call x3 -> x5, Pallas kernels: 11.6 us -> 11.8 us  [the longest x1 3.86 us: finish(): pl.pallas_call(finish_kernel, grid=(KVH,), out_shape=(jax.ShapeDtypeStruc...]
  transfers between devices with their start and end apart: 4 -> 6, of which waited for: 3 -> 4; matrix products, arithmetic and copies ran while one was open for 0% -> 0% of each run, Pallas kernels for 13% -> 20%
where the time goes in v2:
time: 35.8 us; the launch traced here: 35.6 us
  starting transfers between devices  12.8 us (36%)
  Pallas kernels  11.8 us (33%)
  waiting for transfers between devices  9.38 us (26%)
  other arithmetic  0.8 us (2%)
  between operations  0.73 us (2%)
    ppermute x6, starting transfers between devices, shifted(): lax.ppermute(value, AXES, [(source, source + steps) for source in range(l...  12.8 us
    ppermute x6, waiting for transfers between devices, shifted(): lax.ppermute(value, AXES, [(source, source + steps) for source in range(l...  9.38 us
    pallas_call x1, Pallas kernels, finish(): pl.pallas_call(finish_kernel, grid=(KVH,), out_shape=(jax.ShapeDtypeStruc...  3.86 us
    pallas_call x1, Pallas kernels, scores(): pl.pallas_call(score_kernel, out_shape=(TILE, TILE, PAIR, PAIR), in_specs...  3.77 us
    pallas_call x1, Pallas kernels, stage(): pl.pallas_call(stage_kernel, out_shape=(jax.ShapeDtypeStruct((2 * ROWS, R...  2.57 us
    pallas_call x1, Pallas kernels, pack(): pl.pallas_call(pack_kernel, out_shape=PAIR, in_specs=[HBM, HBM], out_spec...  0.99 us
    convert_element_type x1, other arithmetic, body(): d_values.astype(jnp.bfloat16)  0.8 us
  transfers between devices with their start and end apart: 6, of which 4 were waited for; matrix products, arithmetic and copies ran while one was open for 0% of the time, Pallas kernels for 20%

profile of v2, /device:TPU:255, one launch (start us, length us, event | category | flops | bytes accessed | tf_op | source)
XLA Modules:
  0.0 35.6 jit_solution(11616534042729670328)
XLA Ops:
  0.6 1.0 %pack.1 = bf16[2,128,512]{2,1,0:T(8,128)(2,1)S(1)} custom-call(bf16[128,512]{1,0:T(8,128)(2,1)} %k_ref.3, bf16[128,512]{1,0:T(8,128)(2,1)} %v_ref.3), custom_call_target="tpu_custom_call" | custom-call | tf_op jit(solution)/shard_map/pack/pallas_call | solution.py:195
  1.6 4.9 %collective-permute-start = (bf16[2,128,512]{2,1,0:T(8,128)(2,1)S(1)}, bf16[2,128,512]{2,1,0:T(8,128)(2,1)S(1)}, u32[]{:S(2)}, u32[]{:S(2)}) collective-permute-start(bf16[2,128,512]{2,1,0:T(8,128)(2,1)S(1)} %pack.1), channel_id=1, source_target_pairs={{0,1},{1,2},{2,3},{3,4},{4,5},{5,6},{6,7},{7,8},{8,9},{9,10},{10,1... | collective-permute-start | bytes 786440 | tf_op jit(solution)/shard_map/ppermute | solution.py:36
  6.5 0.7 %collective-permute-start.1 = (bf16[2,128,512]{2,1,0:T(8,128)(2,1)S(1)}, bf16[2,128,512]{2,1,0:T(8,128)(2,1)S(1)}, u32[]{:S(2)}, u32[]{:S(2)}) collective-permute-start(bf16[2,128,512]{2,1,0:T(8,128)(2,1)S(1)} %pack.1), channel_id=1, source_target_pairs={{0,2},{2,4},{4,6},{6,8},{8,10},{10,12},{12,14},{14,16},{16,18},{18... | collective-permute-start | bytes 786440 | tf_op jit(solution)/shard_map/ppermute | solution.py:36
  7.2 2.6 %stage.1 = (f32[256,128]{1,0:T(8,128)S(1)}, bf16[4,896,128]{2,1,0:T(8,128)(2,1)S(1)}, bf16[4,896,128]{2,1,0:T(8,128)(2,1)S(1)}, f32[4,128,896]{2,1,0:T(8,128)S(1...) custom-call(s32[1]{0:T(128)S(6)} %mul.7.start_ref, s32[1,512]{1,0:T(1,128)} %bitcast.6, ...), custom_call_target="tpu_custom_call" | custom-call | bytes 9000000 | tf_op jit(solution)/shard_map/stage/pallas_call | solution.py:207
  9.8 0.3 collective-permute-done.near_ref
  10.1 1.3 %collective-permute-start.2 = (bf16[2,128,512]{2,1,0:T(8,128)(2,1)S(1)}, bf16[2,128,512]{2,1,0:T(8,128)(2,1)S(1)}, u32[]{:S(2)}, u32[]{:S(2)}) collective-permute-start(bf16[2,128,512]{2,1,0:T(8,128)(2,1)S(1)} %collective-permute-done.near_ref), channel_id=1, source_target_pairs={{0,1},{2,3},{4,5},{6,7},{8,9},{10,11},{12,13},{14,15},{16,17},{18,... | collective-permute-start | bytes 786440 | tf_op jit(solution)/shard_map/ppermute | solution.py:36
  11.4 0.0 collective-permute-done.1.even_far_ref
  11.4 2.4 %collective-permute-done.2.odd_far_ref = bf16[2,128,512]{2,1,0:T(8,128)(2,1)S(1)} collective-permute-done((bf16[2,128,512]{2,1,0:T(8,128)(2,1)S(1)}, bf16[2,128,512]{2,1,0:T(8,128)(2,1)S(1)}, u32[]{:S(2)}, u32[]{:S(2)}) %collective-permute-start.2) | collective-permute-done | bytes 262176 | tf_op jit(solution)/shard_map/ppermute | solution.py:36
  13.8 3.8 %scores.1 = (bf16[4,256,896]{2,1,0:T(8,128)(2,1)S(1)}, bf16[4,256,896]{2,1,0:T(8,128)(2,1)S(1)}, bf16[2,128,512]{2,1,0:T(8,128)(2,1)S(1)}, bf16[2,128,512]{2,1,0:T(8,128)(2,1)S(1)}) custom-call(s32[1]{0:T(128)S(6)} %select_n.7.odd_ref, bf16[4,896,128]{2,1,0:T(8,128)(2,1)S(1)} %get-tuple-element.19.qs_ref, ...), custom_call_target="tpu_custom_call" | custom-call | bytes 12000000 | tf_op jit(solution)/shard_map/scores/pallas_call | solution.py:227
  17.5 2.1 %collective-permute-start.3 = (bf16[2,128,512]{2,1,0:T(8,128)(2,1)S(1)}, bf16[2,128,512]{2,1,0:T(8,128)(2,1)S(1)}, u32[]{:S(2)}, u32[]{:S(2)}) collective-permute-start(bf16[2,128,512]{2,1,0:T(8,128)(2,1)S(1)} %get-tuple-element.33), channel_id=1, source_target_pairs={{1,0},{3,2},{5,4},{7,6},{9,8},{11,10},{13,12},{15,14},{17,16},{19,... | collective-permute-start | bytes 786440 | tf_op jit(solution)/shard_map/ppermute | solution.py:36
  19.6 0.7 %collective-permute-start.5 = (bf16[2,128,512]{2,1,0:T(8,128)(2,1)S(1)}, bf16[2,128,512]{2,1,0:T(8,128)(2,1)S(1)}, u32[]{:S(2)}, u32[]{:S(2)}) collective-permute-start(bf16[2,128,512]{2,1,0:T(8,128)(2,1)S(1)} %get-tuple-element.33), channel_id=1, source_target_pairs={{2,0},{4,2},{6,4},{8,6},{10,8},{12,10},{14,12},{16,14},{18,16},{20... | collective-permute-start | bytes 786440 | tf_op jit(solution)/shard_map/ppermute | solution.py:36
  20.3 0.4 %collective-permute-done.3.passed_ref = bf16[2,128,512]{2,1,0:T(8,128)(2,1)S(1)} collective-permute-done((bf16[2,128,512]{2,1,0:T(8,128)(2,1)S(1)}, bf16[2,128,512]{2,1,0:T(8,128)(2,1)S(1)}, u32[]{:S(2)}, u32[]{:S(2)}) %collective-permute-start.3) | collective-permute-done | bytes 262176 | tf_op jit(solution)/shard_map/ppermute | solution.py:36
  20.7 0.7 %near_terms.1 = bf16[2,128,512]{2,1,0:T(8,128)(2,1)S(1)} custom-call(s32[1]{0:T(128)S(6)} %select_n.7.odd_ref, bf16[4,896,128]{2,1,0:T(8,128)(2,1)S(1)} %get-tuple-element.19.qs_ref, bf16[4,896,128]{2,1,0:T(8,128)(2,1)S(1)} %get-tuple-element.20.dos_ref, bf16[4,256,896]{2,1,0:T(8,128)(2,1)S(1)} %get-tuple-element.28.prob_ref, ...), custom_call_target="tpu_custom_call" | custom-call | bytes 9000000 | tf_op jit(solution)/shard_map/near_terms/pallas_call | solution.py:239
  21.4 3.2 %collective-permute-start.4 = (bf16[2,128,512]{2,1,0:T(8,128)(2,1)S(1)}, bf16[2,128,512]{2,1,0:T(8,128)(2,1)S(1)}, u32[]{:S(2)}, u32[]{:S(2)}) collective-permute-start(bf16[2,128,512]{2,1,0:T(8,128)(2,1)S(1)} %near_terms.1), channel_id=1, source_target_pairs={{1,0},{2,1},{3,2},{4,3},{5,4},{6,5},{7,6},{8,7},{9,8},{10,9},{11,1... | collective-permute-start | bytes 786440 | tf_op jit(solution)/shard_map/ppermute | solution.py:36
  24.6 3.9 %finish.1 = (bf16[128,3584]{1,0:T(8,128)(2,1)}, bf16[128,3584]{1,0:T(8,128)(2,1)}, f32[2,128,512]{2,1,0:T(8,128)S(1)}) custom-call(bf16[4,896,128]{2,1,0:T(8,128)(2,1)S(1)} %get-tuple-element.19.qs_ref, bf16[4,896,128]{2,1,0:T(8,128)(2,1)S(1)} %get-tuple-element.20.dos_ref, bf16[2,128,512]{2,1,0:T(8,128)(2,1)S(1)} %get-tuple-element.21.own_ref, ...), custom_call_target="tpu_custom_call" | custom-call | bytes 24000000 | tf_op jit(solution)/shard_map/finish/pallas_call | solution.py:251
  28.5 0.0 collective-permute-done.5
  28.5 6.3 %collective-permute-done.4 = bf16[2,128,512]{2,1,0:T(8,128)(2,1)S(1)} collective-permute-done((bf16[2,128,512]{2,1,0:T(8,128)(2,1)S(1)}, bf16[2,128,512]{2,1,0:T(8,128)(2,1)S(1)}, u32[]{:S(2)}, u32[]{:S(2)}) %collective-permute-start.4) | collective-permute-done | bytes 262176 | tf_op jit(solution)/shard_map/ppermute | solution.py:36
  34.8 0.8 %fusion.1 = (bf16[128,512]{1,0:T(8,128)(2,1)}, bf16[128,512]{1,0:T(8,128)(2,1)}) fusion(f32[2,128,512]{2,1,0:T(8,128)S(1)} %get-tuple-element.32, bf16[2,128,512]{2,1,0:T(8,128)(2,1)S(1)} %collective-permute-done.5, bf16[2,128,512]{2,1,0:T(8,128)(2,1)S(1)} %collective-permute-done.4), kind=kLoop, calls=%fused_computation.3 | loop fusion | flops 655360 | bytes 1310720 | tf_op jit(solution)/shard_map/convert_element_type | solution.py:284
Async XLA Ops:
  1.6 8.4 %collective-permute-start = (bf16[2,128,512]{2,1,0:T(8,128)(2,1)S(1)}, bf16[2,128,512]{2,1,0:T(8,128)(2,1)S(1)}, u32[]{:S(2)}, u32[]{:S(2)}) collective-permute-start(bf16[2,128,512]{2,1,0:T(8,128)(2,1)S(1)} %pack.1), channel_id=1, source_target_pairs={{0,1},{1,2},{2,3},{3,4},{4,5},{5,6},{6,7},{7,8},{8,9},{9,10},{10,1... | collective-permute-start | bytes 786440 | tf_op jit(solution)/shard_map/ppermute | solution.py:36
  6.5 4.8 %collective-permute-start.1 = (bf16[2,128,512]{2,1,0:T(8,128)(2,1)S(1)}, bf16[2,128,512]{2,1,0:T(8,128)(2,1)S(1)}, u32[]{:S(2)}, u32[]{:S(2)}) collective-permute-start(bf16[2,128,512]{2,1,0:T(8,128)(2,1)S(1)} %pack.1), channel_id=1, source_target_pairs={{0,2},{2,4},{4,6},{6,8},{8,10},{10,12},{12,14},{14,16},{16,18},{18... | collective-permute-start | bytes 786440 | tf_op jit(solution)/shard_map/ppermute | solution.py:36
  10.1 3.7 %collective-permute-start.2 = (bf16[2,128,512]{2,1,0:T(8,128)(2,1)S(1)}, bf16[2,128,512]{2,1,0:T(8,128)(2,1)S(1)}, u32[]{:S(2)}, u32[]{:S(2)}) collective-permute-start(bf16[2,128,512]{2,1,0:T(8,128)(2,1)S(1)} %collective-permute-done.near_ref), channel_id=1, source_target_pairs={{0,1},{2,3},{4,5},{6,7},{8,9},{10,11},{12,13},{14,15},{16,17},{18,... | collective-permute-start | bytes 786440 | tf_op jit(solution)/shard_map/ppermute | solution.py:36
  17.5 3.2 %collective-permute-start.3 = (bf16[2,128,512]{2,1,0:T(8,128)(2,1)S(1)}, bf16[2,128,512]{2,1,0:T(8,128)(2,1)S(1)}, u32[]{:S(2)}, u32[]{:S(2)}) collective-permute-start(bf16[2,128,512]{2,1,0:T(8,128)(2,1)S(1)} %get-tuple-element.33), channel_id=1, source_target_pairs={{1,0},{3,2},{5,4},{7,6},{9,8},{11,10},{13,12},{15,14},{17,16},{19,... | collective-permute-start | bytes 786440 | tf_op jit(solution)/shard_map/ppermute | solution.py:36
  19.6 8.9 %collective-permute-start.5 = (bf16[2,128,512]{2,1,0:T(8,128)(2,1)S(1)}, bf16[2,128,512]{2,1,0:T(8,128)(2,1)S(1)}, u32[]{:S(2)}, u32[]{:S(2)}) collective-permute-start(bf16[2,128,512]{2,1,0:T(8,128)(2,1)S(1)} %get-tuple-element.33), channel_id=1, source_target_pairs={{2,0},{4,2},{6,4},{8,6},{10,8},{12,10},{14,12},{16,14},{18,16},{20... | collective-permute-start | bytes 786440 | tf_op jit(solution)/shard_map/ppermute | solution.py:36
  21.4 13.4 %collective-permute-start.4 = (bf16[2,128,512]{2,1,0:T(8,128)(2,1)S(1)}, bf16[2,128,512]{2,1,0:T(8,128)(2,1)S(1)}, u32[]{:S(2)}, u32[]{:S(2)}) collective-permute-start(bf16[2,128,512]{2,1,0:T(8,128)(2,1)S(1)} %near_terms.1), channel_id=1, source_target_pairs={{1,0},{2,1},{3,2},{4,3},{5,4},{6,5},{7,6},{8,7},{9,8},{10,9},{11,1... | collective-permute-start | bytes 786440 | tf_op jit(solution)/shard_map/ppermute | solution.py:36

commit v3 on v2

--- a/solution.py
+++ b/solution.py
@@ -11,10 +11,11 @@
 HD = 128
 ROWS = 128
 DOCS = 512
+PARTS = 4
 AXES = ("ctx", "dp")
 NEG = -1e30
 SCALE = HD**-0.5
-LOG2E = 1.4426950408889634
+FACTOR = SCALE * 1.4426950408889634
 WIDE = GROUPS * HD
 CUT = KVH * HD
 
@@ -51,12 +52,15 @@
 
 
 def pack_kernel(k_ref, v_ref, out_ref, sems):
-    first = pltpu.make_async_copy(k_ref, out_ref.at[0], sems.at[0])
-    second = pltpu.make_async_copy(v_ref, out_ref.at[1], sems.at[1])
-    first.start()
-    second.start()
-    first.wait()
-    second.wait()
+    copies = []
+    for i, ref in enumerate((k_ref, v_ref)):
+        for part in range(PARTS):
+            rows = slice(part * ROWS // PARTS, (part + 1) * ROWS // PARTS)
+            copies.append(pltpu.make_async_copy(ref.at[rows], out_ref.at[i, rows], sems.at[i * PARTS + part]))
+    for copy in copies:
+        copy.start()
+    for copy in copies:
+        copy.wait()
 
 
 def stage_kernel(start_ref, lengths_ref, q_ref, do_ref, k_ref, v_ref,
@@ -68,11 +72,11 @@
     ]
     heads = []
     for j in range(KVH):
-        for source, target, sem in ((q_ref, qs_ref, 3 + j), (do_ref, dos_ref, 3 + KVH + j)):
+        for source, target in ((q_ref, qs_ref), (do_ref, dos_ref)):
             for h in range(GROUPS):
                 column = (j * GROUPS + h) * HD
                 heads.append(pltpu.make_async_copy(
-                    source.at[:, column:column + HD], target.at[j, h * HD:(h + 1) * HD, :], sems.at[sem]))
+                    source.at[:, column:column + HD], target.at[j, h * HD:(h + 1) * HD, :], sems.at[3 + len(heads)]))
     for copy in copies + heads:
         copy.start()
     copies[0].wait()
@@ -96,54 +100,55 @@
         lanes = slice(j * HD, (j + 1) * HD)
         for h in range(2 * GROUPS):
             heads[2 * GROUPS * j + h].wait()
-        s_ref[j] = dot(kv_ref[0, :, lanes], qs_ref[j], NT)
+        s_ref[j] = dot(kv_ref[0, :, lanes], qs_ref[j], NT) * FACTOR
         d_ref[j] = dot(kv_ref[1, :, lanes], dos_ref[j], NT)
 
 
-def score_kernel(odd_ref, qs_ref, dos_ref, s_ref, d_ref, near_ref, even_far_ref, odd_far_ref, bias_ref,
+def near_score_kernel(qs_ref, dos_ref, near_ref, bias_ref, s_ref, d_ref):
+    for j in range(KVH):
+        lanes = slice(j * HD, (j + 1) * HD)
+        s = dot(near_ref[0, :, lanes], qs_ref[j], NT)
+        for h in range(GROUPS):
+            cols = slice(h * HD, (h + 1) * HD)
+            s_ref[j, :, cols] = s[:, cols] * FACTOR + bias_ref[ROWS:, :]
+        d_ref[j] = dot(near_ref[1, :, lanes], dos_ref[j], NT)
+
+
+def score_kernel(odd_ref, qs_ref, dos_ref, so_ref, do_ref, sn_ref, dn_ref, even_far_ref, odd_far_ref, bias_ref,
                  prob_ref, ds_ref, out_ref, far_ref):
-    @pl.when(odd_ref[0] == 0)
-    def _():
-        far_ref[...] = even_far_ref[...]
-
-    @pl.when(odd_ref[0] == 1)
-    def _():
-        far_ref[...] = odd_far_ref[...]
-
+    odd = odd_ref[0] == 1
+    far_ref[...] = jnp.where(odd, odd_far_ref[...], even_far_ref[...])
     tri = triangle(ROWS)
     wide_tri = triangle(WIDE)
     none = jnp.zeros((ROWS, WIDE), jnp.bfloat16)
-    factor = SCALE * LOG2E
-    for j in range(KVH):
-        lanes = slice(j * HD, (j + 1) * HD)
-        qs = qs_ref[j]
-        dos = dos_ref[j]
-        s_far = dot(far_ref[0, :, lanes], qs, NT)
-        s_near = dot(near_ref[0, :, lanes], qs, NT)
-        d_far = dot(far_ref[1, :, lanes], dos, NT)
-        d_near = dot(near_ref[1, :, lanes], dos, NT)
+    for j in range(KVH):
+        lanes = slice(j * HD, (j + 1) * HD)
+        s_far = dot(far_ref[0, :, lanes], qs_ref[j], NT)
+        d_far = dot(far_ref[1, :, lanes], dos_ref[j], NT)
         for h in range(GROUPS):
             cols = slice(h * HD, (h + 1) * HD)
-            a = jnp.where(tri, s_ref[j, :, cols], s_far[:, cols]) + bias_ref[0:ROWS, :]
-            b = s_near[:, cols] + bias_ref[ROWS:, :]
+            a = jnp.where(tri, so_ref[j, :, cols], s_far[:, cols] * FACTOR) + bias_ref[0:ROWS, :]
+            b = sn_ref[j, :, cols]
             peak = jnp.max(jnp.maximum(a, b), axis=0, keepdims=True)
-            a = jnp.exp2((a - peak) * factor)
-            b = jnp.exp2((b - peak) * factor)
+            a = jnp.exp2(a - peak)
+            b = jnp.exp2(b - peak)
             inv = 1.0 / jnp.sum(a + b, axis=0, keepdims=True)
             a = a * inv
             b = b * inv
-            da = jnp.where(tri, d_ref[j, :, cols], d_far[:, cols])
-            db = d_near[:, cols]
+            da = jnp.where(tri, do_ref[j, :, cols], d_far[:, cols])
+            db = dn_ref[j, :, cols]
             delta = jnp.sum(a * da + b * db, axis=0, keepdims=True)
             prob_ref[j, 0:ROWS, cols] = a.astype(jnp.bfloat16)
             prob_ref[j, ROWS:, cols] = b.astype(jnp.bfloat16)
             ds_ref[j, 0:ROWS, cols] = (a * (da - delta)).astype(jnp.bfloat16)
             ds_ref[j, ROWS:, cols] = (b * (db - delta)).astype(jnp.bfloat16)
+    for j in range(KVH):
+        lanes = slice(j * HD, (j + 1) * HD)
         out_ref[0, :, lanes] = (
-            SCALE * dot(jnp.where(wide_tri, none, ds_ref[j, 0:ROWS, :]), qs, NN)
+            SCALE * dot(jnp.where(wide_tri, none, ds_ref[j, 0:ROWS, :]), qs_ref[j], NN)
         ).astype(jnp.bfloat16)
         out_ref[1, :, lanes] = dot(
-            jnp.where(wide_tri, none, prob_ref[j, 0:ROWS, :]), dos, NN
+            jnp.where(wide_tri, none, prob_ref[j, 0:ROWS, :]), dos_ref[j], NN
         ).astype(jnp.bfloat16)
 
 
@@ -184,6 +189,7 @@
 
 
 PAIR = jax.ShapeDtypeStruct((2, ROWS, CUT), jnp.bfloat16)
+SCORE = jax.ShapeDtypeStruct((KVH, ROWS, WIDE), jnp.float32)
 TILE = jax.ShapeDtypeStruct((KVH, 2 * ROWS, WIDE), jnp.bfloat16)
 HEAD = pl.BlockSpec((ROWS, WIDE), lambda j: (0, j))
 BOTH = pl.BlockSpec((2, ROWS, HD), lambda j: (0, 0, j))
@@ -197,7 +203,7 @@
         out_shape=PAIR,
         in_specs=[HBM, HBM],
         out_specs=VMEM,
-        scratch_shapes=[pltpu.SemaphoreType.DMA((2,))],
+        scratch_shapes=[pltpu.SemaphoreType.DMA((2 * PARTS,))],
         name="pack",
         compiler_params=ROOM,
     )(pinned(keys), pinned(values))
@@ -210,29 +216,41 @@
             jax.ShapeDtypeStruct((2 * ROWS, ROWS), jnp.float32),
             jax.ShapeDtypeStruct((KVH, WIDE, HD), jnp.bfloat16),
             jax.ShapeDtypeStruct((KVH, WIDE, HD), jnp.bfloat16),
-            jax.ShapeDtypeStruct((KVH, ROWS, WIDE), jnp.float32),
-            jax.ShapeDtypeStruct((KVH, ROWS, WIDE), jnp.float32),
+            SCORE,
+            SCORE,
             PAIR,
         ),
         in_specs=[SMEM] + [HBM] * 5,
         out_specs=(VMEM,) * 6,
-        scratch_shapes=[pltpu.VMEM((1, DOCS), jnp.int32), pltpu.SemaphoreType.DMA((3 + 2 * KVH,))],
+        scratch_shapes=[pltpu.VMEM((1, DOCS), jnp.int32), pltpu.SemaphoreType.DMA((3 + 2 * QH,))],
         name="stage",
         compiler_params=ROOM,
         cost_estimate=cost(3),
     )(start, *(pinned(x) for x in (lengths, queries, d_out, keys, values)))
 
 
-def scores(odd, qs, dos, s_own, d_own, near, even_far, odd_far, bias):
+def near_scores(qs, dos, near, bias):
+    return pl.pallas_call(
+        near_score_kernel,
+        out_shape=(SCORE, SCORE),
+        in_specs=[VMEM] * 4,
+        out_specs=(VMEM, VMEM),
+        name="near_scores",
+        compiler_params=ROOM,
+        cost_estimate=cost(2),
+    )(qs, dos, near, bias)
+
+
+def scores(odd, qs, dos, s_own, d_own, s_near, d_near, even_far, odd_far, bias):
     return pl.pallas_call(
         score_kernel,
         out_shape=(TILE, TILE, PAIR, PAIR),
-        in_specs=[SMEM] + [VMEM] * 8,
+        in_specs=[SMEM] + [VMEM] * 9,
         out_specs=(VMEM, VMEM, VMEM, VMEM),
         name="scores",
         compiler_params=ROOM,
         cost_estimate=cost(4),
-    )(odd, qs, dos, s_own, d_own, near, even_far, odd_far, bias)
+    )(odd, qs, dos, s_own, d_own, s_near, d_near, even_far, odd_far, bias)
 
 
 def near_terms(odd, qs, dos, prob, ds, passed):
@@ -274,7 +292,8 @@
     bias, qs, dos, s_own, d_own, own = stage(start, lengths.reshape(1, DOCS), queries, d_out, keys, values)
     near, bias = lax.optimization_barrier((near, bias))
     odd_far = shifted(near, 1, 2)
-    prob, ds, far_terms, far = scores(odd, qs, dos, s_own, d_own, near, even_far, odd_far, bias)
+    s_near, d_near = near_scores(qs, dos, near, bias)
+    prob, ds, far_terms, far = scores(odd, qs, dos, s_own, d_own, s_near, d_near, even_far, odd_far, bias)
     passed = shifted(far_terms, -1, 2)
     far_back = shifted(far_terms, -2, 2)
     near_back = shifted(near_terms(odd, qs, dos, prob, ds, passed), -1)

time: 35.8 us -> 35.7 us (level)
  Pallas kernels: 11.8 us -> 12.4 us
  starting transfers between devices: 12.8 us -> 12.3 us
    pallas_call x0 -> x1, Pallas kernels: none -> 0.74 us  [near_scores(): pl.pallas_call(near_score_kernel, out_shape=(SCORE, SCORE), in_specs=[VME...]
    pallas_call x1, Pallas kernels: 3.77 us -> 3.07 us  [scores(): pl.pallas_call(score_kernel, out_shape=(TILE, TILE, PAIR, PAIR), in_specs...]
    pallas_call x1, Pallas kernels: 2.57 us -> 3.07 us  [stage(): pl.pallas_call(stage_kernel, out_shape=(jax.ShapeDtypeStruct((2 * ROWS, R...]
    ppermute x6, starting transfers between devices: 12.8 us -> 12.3 us  [shifted(): lax.ppermute(value, AXES, [(source, source + steps) for source in range(l...]
  transfers between devices with their start and end apart: 6 -> 6, of which waited for: 4 -> 3; matrix products, arithmetic and copies ran while one was open for 0% -> 0% of each run, Pallas kernels for 20% -> 24%
where the time goes in v3:
time: 35.7 us; the launch traced here: 35.4 us
  Pallas kernels  12.4 us (35%)
  starting transfers between devices  12.3 us (34%)
  waiting for transfers between devices  9.08 us (25%)
  other arithmetic  0.82 us (2%)
  between operations  0.74 us (2%)
    ppermute x6, starting transfers between devices, shifted(): lax.ppermute(value, AXES, [(source, source + steps) for source in range(l...  12.3 us
    ppermute x6, waiting for transfers between devices, shifted(): lax.ppermute(value, AXES, [(source, source + steps) for source in range(l...  9.08 us
    pallas_call x1, Pallas kernels, finish(): pl.pallas_call(finish_kernel, grid=(KVH,), out_shape=(jax.ShapeDtypeStruc...  3.92 us
    pallas_call x1, Pallas kernels, stage(): pl.pallas_call(stage_kernel, out_shape=(jax.ShapeDtypeStruct((2 * ROWS, R...  3.07 us
    pallas_call x1, Pallas kernels, scores(): pl.pallas_call(score_kernel, out_shape=(TILE, TILE, PAIR, PAIR), in_specs...  3.07 us
    pallas_call x1, Pallas kernels, pack(): pl.pallas_call(pack_kernel, out_shape=PAIR, in_specs=[HBM, HBM], out_spec...  0.94 us
    convert_element_type x1, other arithmetic, body(): d_values.astype(jnp.bfloat16)  0.82 us
    pallas_call x1, Pallas kernels, near_scores(): pl.pallas_call(near_score_kernel, out_shape=(SCORE, SCORE), in_specs=[VME...  0.74 us
  transfers between devices with their start and end apart: 6, of which 3 were waited for; matrix products, arithmetic and copies ran while one was open for 0% of the time, Pallas kernels for 24%

profile of v3, /device:TPU:255, one launch (start us, length us, event | category | flops | bytes accessed | tf_op | source)
XLA Modules:
  0.0 35.4 jit_solution(6155108900133094475)
XLA Ops:
  0.6 0.9 %pack.1 = bf16[2,128,512]{2,1,0:T(8,128)(2,1)S(1)} custom-call(bf16[128,512]{1,0:T(8,128)(2,1)} %k_ref.3, bf16[128,512]{1,0:T(8,128)(2,1)} %v_ref.3), custom_call_target="tpu_custom_call" | custom-call | tf_op jit(solution)/shard_map/pack/pallas_call | solution.py:201
  1.6 4.9 %collective-permute-start = (bf16[2,128,512]{2,1,0:T(8,128)(2,1)S(1)}, bf16[2,128,512]{2,1,0:T(8,128)(2,1)S(1)}, u32[]{:S(2)}, u32[]{:S(2)}) collective-permute-start(bf16[2,128,512]{2,1,0:T(8,128)(2,1)S(1)} %pack.1), channel_id=1, source_target_pairs={{0,1},{1,2},{2,3},{3,4},{4,5},{5,6},{6,7},{7,8},{8,9},{9,10},{10,1... | collective-permute-start | bytes 786440 | tf_op jit(solution)/shard_map/ppermute | solution.py:37
  6.5 0.7 %collective-permute-start.1 = (bf16[2,128,512]{2,1,0:T(8,128)(2,1)S(1)}, bf16[2,128,512]{2,1,0:T(8,128)(2,1)S(1)}, u32[]{:S(2)}, u32[]{:S(2)}) collective-permute-start(bf16[2,128,512]{2,1,0:T(8,128)(2,1)S(1)} %pack.1), channel_id=1, source_target_pairs={{0,2},{2,4},{4,6},{6,8},{8,10},{10,12},{12,14},{14,16},{16,18},{18... | collective-permute-start | bytes 786440 | tf_op jit(solution)/shard_map/ppermute | solution.py:37
  7.2 3.1 %stage.1 = (f32[256,128]{1,0:T(8,128)S(1)}, bf16[4,896,128]{2,1,0:T(8,128)(2,1)S(1)}, bf16[4,896,128]{2,1,0:T(8,128)(2,1)S(1)}, f32[4,128,896]{2,1,0:T(8,128)S(1...) custom-call(s32[1]{0:T(128)S(6)} %mul.7.start_ref, s32[1,512]{1,0:T(1,128)} %bitcast.6, ...), custom_call_target="tpu_custom_call" | custom-call | bytes 9000000 | tf_op jit(solution)/shard_map/stage/pallas_call | solution.py:213
  10.3 0.0 collective-permute-done.near_ref
  10.3 1.3 %collective-permute-start.2 = (bf16[2,128,512]{2,1,0:T(8,128)(2,1)S(1)}, bf16[2,128,512]{2,1,0:T(8,128)(2,1)S(1)}, u32[]{:S(2)}, u32[]{:S(2)}) collective-permute-start(bf16[2,128,512]{2,1,0:T(8,128)(2,1)S(1)} %collective-permute-done.near_ref), channel_id=1, source_target_pairs={{0,1},{2,3},{4,5},{6,7},{8,9},{10,11},{12,13},{14,15},{16,17},{18,... | collective-permute-start | bytes 786440 | tf_op jit(solution)/shard_map/ppermute | solution.py:37
  11.6 0.7 %near_scores.1 = (f32[4,128,896]{2,1,0:T(8,128)S(1)}, f32[4,128,896]{2,1,0:T(8,128)S(1)}) custom-call(bf16[4,896,128]{2,1,0:T(8,128)(2,1)S(1)} %get-tuple-element.21.qs_ref, bf16[4,896,128]{2,1,0:T(8,128)(2,1)S(1)} %get-tuple-element.22.dos_ref, bf16[2,128,512]{2,1,0:T(8,128)(2,1)S(1)} %collective-permute-done.near_ref, ...), custom_call_target="tpu_custom_call" | custom-call | bytes 6000000 | tf_op jit(solution)/shard_map/near_scores/pallas_call | solution.py:233
  12.3 0.0 collective-permute-done.1.even_far_ref
  12.3 1.9 %collective-permute-done.2.odd_far_ref = bf16[2,128,512]{2,1,0:T(8,128)(2,1)S(1)} collective-permute-done((bf16[2,128,512]{2,1,0:T(8,128)(2,1)S(1)}, bf16[2,128,512]{2,1,0:T(8,128)(2,1)S(1)}, u32[]{:S(2)}, u32[]{:S(2)}) %collective-permute-start.2) | collective-permute-done | bytes 262176 | tf_op jit(solution)/shard_map/ppermute | solution.py:37
  14.2 3.1 %scores.1 = (bf16[4,256,896]{2,1,0:T(8,128)(2,1)S(1)}, bf16[4,256,896]{2,1,0:T(8,128)(2,1)S(1)}, bf16[2,128,512]{2,1,0:T(8,128)(2,1)S(1)}, bf16[2,128,512]{2,1,0:T(8,128)(2,1)S(1)}) custom-call(s32[1]{0:T(128)S(6)} %select_n.7.odd_ref, bf16[4,896,128]{2,1,0:T(8,128)(2,1)S(1)} %get-tuple-element.21.qs_ref, ...), custom_call_target="tpu_custom_call" | custom-call | bytes 12000000 | tf_op jit(solution)/shard_map/scores/pallas_call | solution.py:245
  17.3 2.1 %collective-permute-start.3 = (bf16[2,128,512]{2,1,0:T(8,128)(2,1)S(1)}, bf16[2,128,512]{2,1,0:T(8,128)(2,1)S(1)}, u32[]{:S(2)}, u32[]{:S(2)}) collective-permute-start(bf16[2,128,512]{2,1,0:T(8,128)(2,1)S(1)} %get-tuple-element.37), channel_id=1, source_target_pairs={{1,0},{3,2},{5,4},{7,6},{9,8},{11,10},{13,12},{15,14},{17,16},{19,... | collective-permute-start | bytes 786440 | tf_op jit(solution)/shard_map/ppermute | solution.py:37
  19.3 0.7 %collective-permute-start.5 = (bf16[2,128,512]{2,1,0:T(8,128)(2,1)S(1)}, bf16[2,128,512]{2,1,0:T(8,128)(2,1)S(1)}, u32[]{:S(2)}, u32[]{:S(2)}) collective-permute-start(bf16[2,128,512]{2,1,0:T(8,128)(2,1)S(1)} %get-tuple-element.37), channel_id=1, source_target_pairs={{2,0},{4,2},{6,4},{8,6},{10,8},{12,10},{14,12},{16,14},{18,16},{20... | collective-permute-start | bytes 786440 | tf_op jit(solution)/shard_map/ppermute | solution.py:37
  20.0 0.4 %collective-permute-done.3.passed_ref = bf16[2,128,512]{2,1,0:T(8,128)(2,1)S(1)} collective-permute-done((bf16[2,128,512]{2,1,0:T(8,128)(2,1)S(1)}, bf16[2,128,512]{2,1,0:T(8,128)(2,1)S(1)}, u32[]{:S(2)}, u32[]{:S(2)}) %collective-permute-start.3) | collective-permute-done | bytes 262176 | tf_op jit(solution)/shard_map/ppermute | solution.py:37
  20.5 0.6 %near_terms.1 = bf16[2,128,512]{2,1,0:T(8,128)(2,1)S(1)} custom-call(s32[1]{0:T(128)S(6)} %select_n.7.odd_ref, bf16[4,896,128]{2,1,0:T(8,128)(2,1)S(1)} %get-tuple-element.21.qs_ref, bf16[4,896,128]{2,1,0:T(8,128)(2,1)S(1)} %get-tuple-element.22.dos_ref, bf16[4,256,896]{2,1,0:T(8,128)(2,1)S(1)} %get-tuple-element.32.prob_ref, ...), custom_call_target="tpu_custom_call" | custom-call | bytes 9000000 | tf_op jit(solution)/shard_map/near_terms/pallas_call | solution.py:257
  21.1 2.7 %collective-permute-start.4 = (bf16[2,128,512]{2,1,0:T(8,128)(2,1)S(1)}, bf16[2,128,512]{2,1,0:T(8,128)(2,1)S(1)}, u32[]{:S(2)}, u32[]{:S(2)}) collective-permute-start(bf16[2,128,512]{2,1,0:T(8,128)(2,1)S(1)} %near_terms.1), channel_id=1, source_target_pairs={{1,0},{2,1},{3,2},{4,3},{5,4},{6,5},{7,6},{8,7},{9,8},{10,9},{11,1... | collective-permute-start | bytes 786440 | tf_op jit(solution)/shard_map/ppermute | solution.py:37
  23.9 3.9 %finish.1 = (bf16[128,3584]{1,0:T(8,128)(2,1)}, bf16[128,3584]{1,0:T(8,128)(2,1)}, f32[2,128,512]{2,1,0:T(8,128)S(1)}) custom-call(bf16[4,896,128]{2,1,0:T(8,128)(2,1)S(1)} %get-tuple-element.21.qs_ref, bf16[4,896,128]{2,1,0:T(8,128)(2,1)S(1)} %get-tuple-element.22.dos_ref, bf16[2,128,512]{2,1,0:T(8,128)(2,1)S(1)} %get-tuple-element.23.own_ref, ...), custom_call_target="tpu_custom_call" | custom-call | bytes 24000000 | tf_op jit(solution)/shard_map/finish/pallas_call | solution.py:269
  27.8 0.0 collective-permute-done.5
  27.8 6.7 %collective-permute-done.4 = bf16[2,128,512]{2,1,0:T(8,128)(2,1)S(1)} collective-permute-done((bf16[2,128,512]{2,1,0:T(8,128)(2,1)S(1)}, bf16[2,128,512]{2,1,0:T(8,128)(2,1)S(1)}, u32[]{:S(2)}, u32[]{:S(2)}) %collective-permute-start.4) | collective-permute-done | bytes 262176 | tf_op jit(solution)/shard_map/ppermute | solution.py:37
  34.5 0.8 %fusion.1 = (bf16[128,512]{1,0:T(8,128)(2,1)}, bf16[128,512]{1,0:T(8,128)(2,1)}) fusion(f32[2,128,512]{2,1,0:T(8,128)S(1)} %get-tuple-element.36, bf16[2,128,512]{2,1,0:T(8,128)(2,1)S(1)} %collective-permute-done.5, bf16[2,128,512]{2,1,0:T(8,128)(2,1)S(1)} %collective-permute-done.4), kind=kLoop, calls=%fused_computation.3 | loop fusion | flops 655360 | bytes 1310720 | tf_op jit(solution)/shard_map/convert_element_type | solution.py:303
Async XLA Ops:
  1.6 8.7 %collective-permute-start = (bf16[2,128,512]{2,1,0:T(8,128)(2,1)S(1)}, bf16[2,128,512]{2,1,0:T(8,128)(2,1)S(1)}, u32[]{:S(2)}, u32[]{:S(2)}) collective-permute-start(bf16[2,128,512]{2,1,0:T(8,128)(2,1)S(1)} %pack.1), channel_id=1, source_target_pairs={{0,1},{1,2},{2,3},{3,4},{4,5},{5,6},{6,7},{7,8},{8,9},{9,10},{10,1... | collective-permute-start | bytes 786440 | tf_op jit(solution)/shard_map/ppermute | solution.py:37
  6.5 5.8 %collective-permute-start.1 = (bf16[2,128,512]{2,1,0:T(8,128)(2,1)S(1)}, bf16[2,128,512]{2,1,0:T(8,128)(2,1)S(1)}, u32[]{:S(2)}, u32[]{:S(2)}) collective-permute-start(bf16[2,128,512]{2,1,0:T(8,128)(2,1)S(1)} %pack.1), channel_id=1, source_target_pairs={{0,2},{2,4},{4,6},{6,8},{8,10},{10,12},{12,14},{14,16},{16,18},{18... | collective-permute-start | bytes 786440 | tf_op jit(solution)/shard_map/ppermute | solution.py:37
  10.3 3.9 %collective-permute-start.2 = (bf16[2,128,512]{2,1,0:T(8,128)(2,1)S(1)}, bf16[2,128,512]{2,1,0:T(8,128)(2,1)S(1)}, u32[]{:S(2)}, u32[]{:S(2)}) collective-permute-start(bf16[2,128,512]{2,1,0:T(8,128)(2,1)S(1)} %collective-permute-done.near_ref), channel_id=1, source_target_pairs={{0,1},{2,3},{4,5},{6,7},{8,9},{10,11},{12,13},{14,15},{16,17},{18,... | collective-permute-start | bytes 786440 | tf_op jit(solution)/shard_map/ppermute | solution.py:37
  17.3 3.2 %collective-permute-start.3 = (bf16[2,128,512]{2,1,0:T(8,128)(2,1)S(1)}, bf16[2,128,512]{2,1,0:T(8,128)(2,1)S(1)}, u32[]{:S(2)}, u32[]{:S(2)}) collective-permute-start(bf16[2,128,512]{2,1,0:T(8,128)(2,1)S(1)} %get-tuple-element.37), channel_id=1, source_target_pairs={{1,0},{3,2},{5,4},{7,6},{9,8},{11,10},{13,12},{15,14},{17,16},{19,... | collective-permute-start | bytes 786440 | tf_op jit(solution)/shard_map/ppermute | solution.py:37
  19.3 8.4 %collective-permute-start.5 = (bf16[2,128,512]{2,1,0:T(8,128)(2,1)S(1)}, bf16[2,128,512]{2,1,0:T(8,128)(2,1)S(1)}, u32[]{:S(2)}, u32[]{:S(2)}) collective-permute-start(bf16[2,128,512]{2,1,0:T(8,128)(2,1)S(1)} %get-tuple-element.37), channel_id=1, source_target_pairs={{2,0},{4,2},{6,4},{8,6},{10,8},{12,10},{14,12},{16,14},{18,16},{20... | collective-permute-start | bytes 786440 | tf_op jit(solution)/shard_map/ppermute | solution.py:37
  21.1 13.4 %collective-permute-start.4 = (bf16[2,128,512]{2,1,0:T(8,128)(2,1)S(1)}, bf16[2,128,512]{2,1,0:T(8,128)(2,1)S(1)}, u32[]{:S(2)}, u32[]{:S(2)}) collective-permute-start(bf16[2,128,512]{2,1,0:T(8,128)(2,1)S(1)} %near_terms.1), channel_id=1, source_target_pairs={{1,0},{2,1},{3,2},{4,3},{5,4},{6,5},{7,6},{8,7},{9,8},{10,9},{11,1... | collective-permute-start | bytes 786440 | tf_op jit(solution)/shard_map/ppermute | solution.py:37

commit v4 on v3

v4 whole, which is shorter than its diff:
```python
import jax
import jax.numpy as jnp
from jax import lax
from jax.experimental import pallas as pl
from jax.experimental.pallas import tpu as pltpu
from jax.sharding import PartitionSpec as P

QH = 28
KVH = 4
GROUPS = QH // KVH
HD = 128
ROWS = 128
DOCS = 512
PARTS = 4
AXES = ("ctx", "dp")
NEG = -1e30
SCALE = HD**-0.5
FACTOR = SCALE * 1.4426950408889634
WIDE = GROUPS * HD
CUT = KVH * HD

NT = (((1,), (1,)), ((), ()))
NN = (((1,), (0,)), ((), ()))
VMEM = pl.BlockSpec(memory_space=pltpu.VMEM)
SMEM = pl.BlockSpec(memory_space=pltpu.SMEM)
HBM = pl.BlockSpec(memory_space=pltpu.HBM)
ROOM = pltpu.CompilerParams(vmem_limit_bytes=32 * 1024 * 1024)


def dot(a, b, dims):
    return lax.dot_general(a, b, dims, preferred_element_type=jnp.float32)


def shifted(value, steps, every=1):
    count = lax.axis_size(AXES)
    leading, last = (max(0, -steps), min(count, count - steps))
    return lax.ppermute(value, AXES, [(source, source + steps) for source in range(leading, last, every)])


def pinned(value):
    return pltpu.with_memory_space_constraint(value, pltpu.HBM)


def cost(us):
    return pl.CostEstimate(flops=0, bytes_accessed=int(us * 3_000_000), transcendentals=0)


def triangle(width):
    s = lax.broadcasted_iota(jnp.int32, (ROWS, width), 0)
    t = lax.broadcasted_iota(jnp.int32, (ROWS, width), 1) % HD
    return s <= t


def pack_kernel(k_ref, v_ref, lengths_ref, out_ref, len_ref, sems):
    copies = [pltpu.make_async_copy(lengths_ref, len_ref, sems.at[2 * PARTS])]
    for i, ref in enumerate((k_ref, v_ref)):
        for part in range(PARTS):
            rows = slice(part * ROWS // PARTS, (part + 1) * ROWS // PARTS)
            copies.append(pltpu.make_async_copy(ref.at[rows], out_ref.at[i, rows], sems.at[i * PARTS + part]))
    for copy in copies:
        copy.start()
    for copy in copies:
        copy.wait()


def heads(ref, j):
    first = j * GROUPS
    return jnp.concatenate([ref[:, h * HD:(h + 1) * HD] for h in range(first, first + GROUPS)], axis=0)


def down(fold, x):
    return fold(x, axis=0, keepdims=True)


def stage_kernel(start_ref, len_ref, q_in, do_in, kv_ref,
                 bias_ref, q_ref, do_ref, e_ref, d_ref, stat_ref, sems):
    copies = []
    for i, wide in enumerate((slice(0, WIDE), slice(WIDE, KVH * WIDE))):
        copies.append(pltpu.make_async_copy(q_in.at[:, wide], q_ref.at[:, wide], sems.at[2 * i]))
        copies.append(pltpu.make_async_copy(do_in.at[:, wide], do_ref.at[:, wide], sems.at[2 * i + 1]))
    for copy in copies:
        copy.start()
    start = start_ref[0]
    lens = jnp.broadcast_to(len_ref[...].astype(jnp.float32), (ROWS, DOCS)).astype(jnp.bfloat16)
    doc = lax.broadcasted_iota(jnp.int32, (DOCS, DOCS), 0)
    upto = lax.broadcasted_iota(jnp.int32, (DOCS, DOCS), 1)
    before = jnp.where(upto <= doc, 1.0, 0.0).astype(jnp.bfloat16)
    ends = dot(before, lens, NT).astype(jnp.int32)
    query = start + lax.broadcasted_iota(jnp.int32, (DOCS, ROWS), 1)
    first = down(jnp.max, jnp.where(ends <= query, ends, 0)) - start
    s = lax.broadcasted_iota(jnp.int32, (ROWS, ROWS), 0)
    t = lax.broadcasted_iota(jnp.int32, (ROWS, ROWS), 1)
    own_bias = jnp.where((s <= t) & (s >= first), 0.0, NEG)
    bias_ref[0] = jnp.where((s > t) & (s - 2 * ROWS >= first), 0.0, NEG)
    bias_ref[1] = jnp.where(s - ROWS >= first, 0.0, NEG)
    for j in range(KVH):
        lanes = slice(j * HD, (j + 1) * HD)
        if j < 2:
            copies[2 * j].wait()
            copies[2 * j + 1].wait()
        score = dot(kv_ref[0, :, lanes], heads(q_ref, j), NT)
        d_prob = dot(kv_ref[1, :, lanes], heads(do_ref, j), NT)
        for h in range(GROUPS):
            cols = slice(h * HD, (h + 1) * HD)
            x = score[:, cols] * FACTOR + own_bias
            peak = down(jnp.max, x)
            e = jnp.exp2(x - peak)
            e_ref[j, :, cols] = e
            d_ref[j, :, cols] = d_prob[:, cols]
            stat_ref[j, 0:1, cols] = peak
            stat_ref[j, 1:2, cols] = down(jnp.sum, e)
            stat_ref[j, 2:3, cols] = down(jnp.sum, e * d_prob[:, cols])


def near_score_kernel(q_ref, do_ref, near_ref, bias_ref, stat_ref, e_ref, d_ref, out_ref):
    for j in range(KVH):
        lanes = slice(j * HD, (j + 1) * HD)
        score = dot(near_ref[0, :, lanes], heads(q_ref, j), NT)
        d_prob = dot(near_ref[1, :, lanes], heads(do_ref, j), NT)
        for h in range(GROUPS):
            cols = slice(h * HD, (h + 1) * HD)
            x = score[:, cols] * FACTOR + bias_ref[1]
            peak = jnp.maximum(stat_ref[j, 0:1, cols], down(jnp.max, x))
            own = jnp.exp2(stat_ref[j, 0:1, cols] - peak)
            e = jnp.exp2(x - peak)
            e_ref[j, :, cols] = e
            d_ref[j, :, cols] = d_prob[:, cols]
            out_ref[j, 0:1, cols] = peak
            out_ref[j, 1:2, cols] = stat_ref[j, 1:2, cols] * own + down(jnp.sum, e)
            out_ref[j, 2:3, cols] = stat_ref[j, 2:3, cols] * own + down(jnp.sum, e * d_prob[:, cols])
            out_ref[j, 3:4, cols] = own


def score_kernel(odd_ref, q_ref, do_ref, e_ref, d_ref, stat_ref, even_far_ref, odd_far_ref, bias_ref,
                 prob_ref, ds_ref, terms_ref, far_ref, out_ref):
    odd = odd_ref[0] == 1
    far_ref[...] = jnp.where(odd, odd_far_ref[...], even_far_ref[...])
    for j in range(KVH):
        lanes = slice(j * HD, (j + 1) * HD)
        score = dot(far_ref[0, :, lanes], heads(q_ref, j), NT)
        d_prob = dot(far_ref[1, :, lanes], heads(do_ref, j), NT)
        for h in range(GROUPS):
            cols = slice(h * HD, (h + 1) * HD)
            x = score[:, cols] * FACTOR + bias_ref[0]
            peak = jnp.maximum(stat_ref[j, 0:1, cols], down(jnp.max, x))
            old = jnp.exp2(stat_ref[j, 0:1, cols] - peak)
            e = jnp.exp2(x - peak)
            inv = 1.0 / (stat_ref[j, 1:2, cols] * old + down(jnp.sum, e))
            delta = (stat_ref[j, 2:3, cols] * old + down(jnp.sum, e * d_prob[:, cols])) * inv
            a = e * inv
            b = e_ref[j, :, cols] * (old * inv)
            prob_ref[j, 0:ROWS, cols] = a.astype(jnp.bfloat16)
            prob_ref[j, ROWS:, cols] = b.astype(jnp.bfloat16)
            ds_ref[j, 0:ROWS, cols] = (a * (d_prob[:, cols] - delta)).astype(jnp.bfloat16)
            ds_ref[j, ROWS:, cols] = (b * (d_ref[j, :, cols] - delta)).astype(jnp.bfloat16)
            out_ref[j, 0:1, cols] = stat_ref[j, 3:4, cols] * old * inv
            out_ref[j, 1:2, cols] = delta
    for j in range(KVH):
        lanes = slice(j * HD, (j + 1) * HD)
        terms_ref[0, :, lanes] = (SCALE * dot(ds_ref[j, 0:ROWS, :], heads(q_ref, j), NN)).astype(jnp.bfloat16)
        terms_ref[1, :, lanes] = dot(prob_ref[j, 0:ROWS, :], heads(do_ref, j), NN).astype(jnp.bfloat16)


def near_kernel(odd_ref, q_ref, do_ref, prob_ref, ds_ref, passed_ref, out_ref):
    even = odd_ref[0] == 0
    for j in range(KVH):
        lanes = slice(j * HD, (j + 1) * HD)
        key_terms = SCALE * dot(ds_ref[j, ROWS:, :], heads(q_ref, j), NN)
        value_terms = dot(prob_ref[j, ROWS:, :], heads(do_ref, j), NN)
        key_terms += jnp.where(even, passed_ref[0, :, lanes].astype(jnp.float32), 0.0)
        value_terms += jnp.where(even, passed_ref[1, :, lanes].astype(jnp.float32), 0.0)
        out_ref[0, :, lanes] = key_terms.astype(jnp.bfloat16)
        out_ref[1, :, lanes] = value_terms.astype(jnp.bfloat16)


def finish_kernel(q_ref, do_ref, own_ref, near_ref, far_ref, prob_ref, ds_ref, e_ref, d_ref, stat_ref,
                  att_ref, dq_ref, terms_ref):
    p_own = e_ref[...] * stat_ref[0:1, :]
    ds_own = (p_own * (d_ref[...] - stat_ref[1:2, :])).astype(jnp.bfloat16)
    p_own = p_own.astype(jnp.bfloat16)
    terms_ref[0] = SCALE * dot(ds_own, heads(q_ref, 0), NN)
    terms_ref[1] = dot(p_own, heads(do_ref, 0), NN)
    k3t = jnp.concatenate([far_ref[0], near_ref[0], own_ref[0]], axis=0).T
    v3t = jnp.concatenate([far_ref[1], near_ref[1], own_ref[1]], axis=0).T
    p3 = jnp.concatenate([prob_ref[...], p_own], axis=0)
    ds3 = jnp.concatenate([ds_ref[...], ds_own], axis=0)
    att = dot(v3t, p3, NN)
    dq = dot(k3t, ds3, NN) * SCALE
    for h in range(GROUPS):
        cols = slice(h * HD, (h + 1) * HD)
        att_ref[:, cols] = att[:, cols].T.astype(jnp.bfloat16)
        dq_ref[:, cols] = dq[:, cols].T.astype(jnp.bfloat16)


PAIR = jax.ShapeDtypeStruct((2, ROWS, CUT), jnp.bfloat16)
FULL = jax.ShapeDtypeStruct((ROWS, QH * HD), jnp.bfloat16)
SCORE = jax.ShapeDtypeStruct((KVH, ROWS, WIDE), jnp.float32)
TILE = jax.ShapeDtypeStruct((KVH, 2 * ROWS, WIDE), jnp.bfloat16)
STAT = jax.ShapeDtypeStruct((KVH, 8, WIDE), jnp.float32)
HEAD = pl.BlockSpec((ROWS, WIDE), lambda j: (0, j))
BOTH = pl.BlockSpec((2, ROWS, HD), lambda j: (0, 0, j))
SQUARE = pl.BlockSpec((None, 2 * ROWS, WIDE), lambda j: (j, 0, 0))
LINE = pl.BlockSpec((None, ROWS, WIDE), lambda j: (j, 0, 0))
FEW = pl.BlockSpec((None, 8, WIDE), lambda j: (j, 0, 0))


def pack(keys, values, lengths):
    return pl.pallas_call(
        pack_kernel,
        out_shape=(PAIR, jax.ShapeDtypeStruct((1, DOCS), jnp.int32)),
        in_specs=[HBM] * 3,
        out_specs=(VMEM, VMEM),
        scratch_shapes=[pltpu.SemaphoreType.DMA((2 * PARTS + 1,))],
        name="pack",
        compiler_params=ROOM,
    )(pinned(keys), pinned(values), pinned(lengths))


def stage(start, lengths, queries, d_out, own):
    return pl.pallas_call(
        stage_kernel,
        out_shape=(jax.ShapeDtypeStruct((2, ROWS, ROWS), jnp.float32), FULL, FULL, SCORE, SCORE, STAT),
        in_specs=[SMEM, VMEM, HBM, HBM, VMEM],
        out_specs=(VMEM,) * 6,
        scratch_shapes=[pltpu.SemaphoreType.DMA((4,))],
        name="stage",
        compiler_params=ROOM,
        cost_estimate=cost(3),
    )(start, lengths, pinned(queries), pinned(d_out), own)


def near_scores(q, do, near, bias, stat):
    return pl.pallas_call(
        near_score_kernel,
        out_shape=(SCORE, SCORE, STAT),
        in_specs=[VMEM] * 5,
        out_specs=(VMEM,) * 3,
        name="near_scores",
        compiler_params=ROOM,
        cost_estimate=cost(2),
    )(q, do, near, bias, stat)


def scores(odd, q, do, e_near, d_near, stat, even_far, odd_far, bias):
    return pl.pallas_call(
        score_kernel,
        out_shape=(TILE, TILE, PAIR, PAIR, STAT),
        in_specs=[SMEM] + [VMEM] * 8,
        out_specs=(VMEM,) * 5,
        name="scores",
        compiler_params=ROOM,
        cost_estimate=cost(4),
    )(odd, q, do, e_near, d_near, stat, even_far, odd_far, bias)


def near_terms(odd, q, do, prob, ds, passed):
    return pl.pallas_call(
        near_kernel,
        out_shape=PAIR,
        in_specs=[SMEM] + [VMEM] * 5,
        out_specs=VMEM,
        name="near_terms",
        compiler_params=ROOM,
        cost_estimate=cost(3),
    )(odd, q, do, prob, ds, passed)


def finish(q, do, own, near, far, prob, ds, e_own, d_own, stat):
    return pl.pallas_call(
        finish_kernel,
        grid=(KVH,),
        out_shape=(FULL, FULL, jax.ShapeDtypeStruct((2, ROWS, CUT), jnp.float32)),
        in_specs=[HEAD, HEAD, BOTH, BOTH, BOTH, SQUARE, SQUARE, LINE, LINE, FEW],
        out_specs=(HEAD, HEAD, BOTH),
        name="finish",
        compiler_params=ROOM,
        cost_estimate=cost(8),
    )(q, do, own, near, far, prob, ds, e_own, d_own, stat)


def body(queries, keys, values, d_out, lengths):
    own, lens = pack(keys, values, lengths.reshape(1, DOCS))
    near = shifted(own, 1)
    even_far = shifted(own, 2, 2)
    index = lax.axis_index(AXES).astype(jnp.int32).reshape(1)
    start = index * ROWS
    odd = index % 2
    bias, q, do, e_own, d_own, stat = stage(start, lens, queries, d_out, own)
    near, bias = lax.optimization_barrier((near, bias))
    odd_far = shifted(near, 1, 2)
    e_near, d_near, stat = near_scores(q, do, near, bias, stat)
    prob, ds, far_terms, far, stat = scores(odd, q, do, e_near, d_near, stat, even_far, odd_far, bias)
    passed = shifted(far_terms, -1, 2)
    far_back = shifted(far_terms, -2, 2)
    near_back = shifted(near_terms(odd, q, do, prob, ds, passed), -1)
    attended, d_queries, terms = finish(q, do, own, near, far, prob, ds, e_own, d_own, stat)
    d_keys = terms[0] + near_back[0].astype(jnp.float32) + far_back[0].astype(jnp.float32)
    d_values = terms[1] + near_back[1].astype(jnp.float32) + far_back[1].astype(jnp.float32)
    return attended, d_queries, d_keys.astype(jnp.bfloat16), d_values.astype(jnp.bfloat16)


def solution(mesh):
    split = P(AXES, None)
    return jax.shard_map(
        body,
        mesh=mesh,
        in_specs=(split, split, split, split, P()),
        out_specs=(split, split, split, split),
        check_vma=False,
    )
```

time: 35.7 us -> 34.1 us (0.955)
  Pallas kernels: 12.4 us -> 10.8 us
  waiting for transfers between devices: 9.08 us -> 8.28 us
  starting transfers between devices: 12.3 us -> 13.1 us
    pallas_call x5, Pallas kernels: 11.7 us -> 10.2 us  [the longest x1 3.95 us: finish(): pl.pallas_call(finish_kernel, grid=(KVH,), out_shape=(FULL, FULL, jax.Sha...]
    ppermute x6, waiting for transfers between devices: 9.08 us -> 8.28 us  [shifted(): lax.ppermute(value, AXES, [(source, source + steps) for source in range(l...]
    ppermute x6, starting transfers between devices: 12.3 us -> 13.1 us  [shifted(): lax.ppermute(value, AXES, [(source, source + steps) for source in range(l...]
  transfers between devices with their start and end apart: 6 -> 6, of which waited for: 3 -> 4; matrix products, arithmetic and copies ran while one was open for 0% -> 0% of each run, Pallas kernels for 24% -> 23%
where the time goes in v4:
time: 34.1 us; the launch traced here: 33.8 us
  starting transfers between devices  13.1 us (38%)
  Pallas kernels  10.8 us (32%)
  waiting for transfers between devices  8.28 us (24%)
  other arithmetic  0.81 us (2%)
  between operations  0.74 us (2%)
    ppermute x6, starting transfers between devices, shifted(): lax.ppermute(value, AXES, [(source, source + steps) for source in range(l...  13.1 us
    ppermute x6, waiting for transfers between devices, shifted(): lax.ppermute(value, AXES, [(source, source + steps) for source in range(l...  8.28 us
    pallas_call x1, Pallas kernels, finish(): pl.pallas_call(finish_kernel, grid=(KVH,), out_shape=(FULL, FULL, jax.Sha...  3.95 us
    pallas_call x1, Pallas kernels, scores(): pl.pallas_call(score_kernel, out_shape=(TILE, TILE, PAIR, PAIR, STAT), in...  2.23 us
    pallas_call x1, Pallas kernels, stage(): pl.pallas_call(stage_kernel, out_shape=(jax.ShapeDtypeStruct((2, ROWS, RO...  2.22 us
    pallas_call x1, Pallas kernels, pack(): pl.pallas_call(pack_kernel, out_shape=(PAIR, jax.ShapeDtypeStruct((1, DOC...  0.97 us
    pallas_call x1, Pallas kernels, near_scores(): pl.pallas_call(near_score_kernel, out_shape=(SCORE, SCORE, STAT), in_spec...  0.81 us
    convert_element_type x1, other arithmetic, body(): d_values.astype(jnp.bfloat16)  0.81 us
  transfers between devices with their start and end apart: 6, of which 4 were waited for; matrix products, arithmetic and copies ran while one was open for 0% of the time, Pallas kernels for 23%

profile of v4, /device:TPU:255, one launch (start us, length us, event | category | flops | bytes accessed | tf_op | source)
XLA Modules:
  0.0 33.8 jit_solution(14816063094573358969)
XLA Ops:
  0.6 1.0 %pack.1 = (bf16[2,128,512]{2,1,0:T(8,128)(2,1)S(1)}, s32[1,512]{1,0:T(1,128)S(1)}) custom-call(bf16[128,512]{1,0:T(8,128)(2,1)} %k_ref.1, bf16[128,512]{1,0:T(8,128)(2,1)} %v_ref.1, s32[1,512]{1,0:T(1,128)} %bitcast.6), custom_call_target="tpu_custom_call" | custom-call | tf_op jit(solution)/shard_map/pack/pallas_call | solution.py:208
  1.6 4.9 %collective-permute-start = (bf16[2,128,512]{2,1,0:T(8,128)(2,1)S(1)}, bf16[2,128,512]{2,1,0:T(8,128)(2,1)S(1)}, u32[]{:S(2)}, u32[]{:S(2)}) collective-permute-start(bf16[2,128,512]{2,1,0:T(8,128)(2,1)S(1)} %get-tuple-element.26.kv_ref.own_ref), channel_id=1, source_target_pairs={{0,1},{1,2},{2,3},{3,4},{4,5},{5,6},{6,7},{7,8},{8,9},{9,10},{10,1... | collective-permute-start | bytes 786440 | tf_op jit(solution)/shard_map/ppermute | solution.py:37
  6.5 0.7 %collective-permute-start.1 = (bf16[2,128,512]{2,1,0:T(8,128)(2,1)S(1)}, bf16[2,128,512]{2,1,0:T(8,128)(2,1)S(1)}, u32[]{:S(2)}, u32[]{:S(2)}) collective-permute-start(bf16[2,128,512]{2,1,0:T(8,128)(2,1)S(1)} %get-tuple-element.26.kv_ref.own_ref), channel_id=1, source_target_pairs={{0,2},{2,4},{4,6},{6,8},{8,10},{10,12},{12,14},{14,16},{16,18},{18... | collective-permute-start | bytes 786440 | tf_op jit(solution)/shard_map/ppermute | solution.py:37
  7.2 2.2 %stage.1 = (f32[2,128,128]{2,1,0:T(8,128)S(1)}, bf16[128,3584]{1,0:T(8,128)(2,1)S(1)}, bf16[128,3584]{1,0:T(8,128)(2,1)S(1)}, f32[4,128,896]{2,1,0:T(8,128)S(1)}...) custom-call(s32[1]{0:T(128)S(6)} %mul.7.start_ref, s32[1,512]{1,0:T(1,128)S(1)} %get-tuple-element.25.len_ref, ...), custom_call_target="tpu_custom_call" | custom-call | bytes 9000000 | tf_op jit(solution)/shard_map/stage/pallas_call | solution.py:220
  9.4 0.6 %collective-permute-done.near_ref = bf16[2,128,512]{2,1,0:T(8,128)(2,1)S(1)} collective-permute-done((bf16[2,128,512]{2,1,0:T(8,128)(2,1)S(1)}, bf16[2,128,512]{2,1,0:T(8,128)(2,1)S(1)}, u32[]{:S(2)}, u32[]{:S(2)}) %collective-permute-start) | collective-permute-done | bytes 262176 | tf_op jit(solution)/shard_map/ppermute | solution.py:37
  10.0 1.3 %collective-permute-start.2 = (bf16[2,128,512]{2,1,0:T(8,128)(2,1)S(1)}, bf16[2,128,512]{2,1,0:T(8,128)(2,1)S(1)}, u32[]{:S(2)}, u32[]{:S(2)}) collective-permute-start(bf16[2,128,512]{2,1,0:T(8,128)(2,1)S(1)} %collective-permute-done.near_ref), channel_id=1, source_target_pairs={{0,1},{2,3},{4,5},{6,7},{8,9},{10,11},{12,13},{14,15},{16,17},{18,... | collective-permute-start | bytes 786440 | tf_op jit(solution)/shard_map/ppermute | solution.py:37
  11.3 0.8 %near_scores.1 = (f32[4,128,896]{2,1,0:T(8,128)S(1)}, f32[4,128,896]{2,1,0:T(8,128)S(1)}, f32[4,8,896]{2,1,0:T(8,128)S(1)}) custom-call(bf16[128,3584]{1,0:T(8,128)(2,1)S(1)} %get-tuple-element.27.q_ref, bf16[128,3584]{1,0:T(8,128)(2,1)S(1)} %get-tuple-element.28.do_ref, bf16[2,128,512]{2,1,0:T(8,128)(2,1)S(1)} %collective-permute-done.near_ref, ...), custom_call_target="tpu_custom_call" | custom-call | bytes 6000000 | tf_op jit(solution)/shard_map/near_scores/pallas_call | solution.py:233
  12.2 0.0 collective-permute-done.1.even_far_ref
  12.2 1.3 %collective-permute-done.2.odd_far_ref = bf16[2,128,512]{2,1,0:T(8,128)(2,1)S(1)} collective-permute-done((bf16[2,128,512]{2,1,0:T(8,128)(2,1)S(1)}, bf16[2,128,512]{2,1,0:T(8,128)(2,1)S(1)}, u32[]{:S(2)}, u32[]{:S(2)}) %collective-permute-start.2) | collective-permute-done | bytes 262176 | tf_op jit(solution)/shard_map/ppermute | solution.py:37
  13.5 2.2 %scores.1 = (bf16[4,256,896]{2,1,0:T(8,128)(2,1)S(1)}, bf16[4,256,896]{2,1,0:T(8,128)(2,1)S(1)}, bf16[2,128,512]{2,1,0:T(8,128)(2,1)S(1)}, bf16[2,128,512]{2,1,0:T(8,128)(2,1)S(1)}, f32[4,8,896]{2,1,0:T(8,128)S(1)}) custom-call(s32[1]{0:T(128)S(6)} %select_n.7.odd_ref, bf16[128,3584]{1,0:T(8,128)(2,1)S(1)} %get-tuple-element.27.q_ref, ...), custom_call_target="tpu_custom_call" | custom-call | bytes 12000000 | tf_op jit(solution)/shard_map/scores/pallas_call | solution.py:245
  15.7 2.1 %collective-permute-start.3 = (bf16[2,128,512]{2,1,0:T(8,128)(2,1)S(1)}, bf16[2,128,512]{2,1,0:T(8,128)(2,1)S(1)}, u32[]{:S(2)}, u32[]{:S(2)}) collective-permute-start(bf16[2,128,512]{2,1,0:T(8,128)(2,1)S(1)} %get-tuple-element.45), channel_id=1, source_target_pairs={{1,0},{3,2},{5,4},{7,6},{9,8},{11,10},{13,12},{15,14},{17,16},{19,... | collective-permute-start | bytes 786440 | tf_op jit(solution)/shard_map/ppermute | solution.py:37
  17.8 0.7 %collective-permute-start.5 = (bf16[2,128,512]{2,1,0:T(8,128)(2,1)S(1)}, bf16[2,128,512]{2,1,0:T(8,128)(2,1)S(1)}, u32[]{:S(2)}, u32[]{:S(2)}) collective-permute-start(bf16[2,128,512]{2,1,0:T(8,128)(2,1)S(1)} %get-tuple-element.45), channel_id=1, source_target_pairs={{2,0},{4,2},{6,4},{8,6},{10,8},{12,10},{14,12},{16,14},{18,16},{20... | collective-permute-start | bytes 786440 | tf_op jit(solution)/shard_map/ppermute | solution.py:37
  18.4 0.4 %collective-permute-done.3.passed_ref = bf16[2,128,512]{2,1,0:T(8,128)(2,1)S(1)} collective-permute-done((bf16[2,128,512]{2,1,0:T(8,128)(2,1)S(1)}, bf16[2,128,512]{2,1,0:T(8,128)(2,1)S(1)}, u32[]{:S(2)}, u32[]{:S(2)}) %collective-permute-start.3) | collective-permute-done | bytes 262176 | tf_op jit(solution)/shard_map/ppermute | solution.py:37
  18.9 0.6 %near_terms.1 = bf16[2,128,512]{2,1,0:T(8,128)(2,1)S(1)} custom-call(s32[1]{0:T(128)S(6)} %select_n.7.odd_ref, bf16[128,3584]{1,0:T(8,128)(2,1)S(1)} %get-tuple-element.27.q_ref, bf16[128,3584]{1,0:T(8,128)(2,1)S(1)} %get-tuple-element.28.do_ref, bf16[4,256,896]{2,1,0:T(8,128)(2,1)S(1)} %get-tuple-element.37.prob_ref, ...), custom_call_target="tpu_custom_call" | custom-call | bytes 9000000 | tf_op jit(solution)/shard_map/near_terms/pallas_call | solution.py:257
  19.5 3.5 %collective-permute-start.4 = (bf16[2,128,512]{2,1,0:T(8,128)(2,1)S(1)}, bf16[2,128,512]{2,1,0:T(8,128)(2,1)S(1)}, u32[]{:S(2)}, u32[]{:S(2)}) collective-permute-start(bf16[2,128,512]{2,1,0:T(8,128)(2,1)S(1)} %near_terms.1), channel_id=1, source_target_pairs={{1,0},{2,1},{3,2},{4,3},{5,4},{6,5},{7,6},{8,7},{9,8},{10,9},{11,1... | collective-permute-start | bytes 786440 | tf_op jit(solution)/shard_map/ppermute | solution.py:37
  23.1 3.9 %finish.1 = (bf16[128,3584]{1,0:T(8,128)(2,1)}, bf16[128,3584]{1,0:T(8,128)(2,1)}, f32[2,128,512]{2,1,0:T(8,128)S(1)}) custom-call(bf16[128,3584]{1,0:T(8,128)(2,1)S(1)} %get-tuple-element.27.q_ref, bf16[128,3584]{1,0:T(8,128)(2,1)S(1)} %get-tuple-element.28.do_ref, bf16[2,128,512]{2,1,0:T(8,128)(2,1)S(1)} %get-tuple-element.26.kv_ref.own_ref, ...), custom_call_target="tpu_custom_call" | custom-call | bytes 24000000 | tf_op jit(solution)/shard_map/finish/pallas_call | solution.py:269
  27.0 0.0 collective-permute-done.5
  27.0 5.9 %collective-permute-done.4 = bf16[2,128,512]{2,1,0:T(8,128)(2,1)S(1)} collective-permute-done((bf16[2,128,512]{2,1,0:T(8,128)(2,1)S(1)}, bf16[2,128,512]{2,1,0:T(8,128)(2,1)S(1)}, u32[]{:S(2)}, u32[]{:S(2)}) %collective-permute-start.4) | collective-permute-done | bytes 262176 | tf_op jit(solution)/shard_map/ppermute | solution.py:37
  32.9 0.8 %fusion.1 = (bf16[128,512]{1,0:T(8,128)(2,1)}, bf16[128,512]{1,0:T(8,128)(2,1)}) fusion(f32[2,128,512]{2,1,0:T(8,128)S(1)} %get-tuple-element.44, bf16[2,128,512]{2,1,0:T(8,128)(2,1)S(1)} %collective-permute-done.5, bf16[2,128,512]{2,1,0:T(8,128)(2,1)S(1)} %collective-permute-done.4), kind=kLoop, calls=%fused_computation.3 | loop fusion | flops 655360 | bytes 1310720 | tf_op jit(solution)/shard_map/convert_element_type | solution.py:299
Async XLA Ops:
  1.6 8.4 %collective-permute-start = (bf16[2,128,512]{2,1,0:T(8,128)(2,1)S(1)}, bf16[2,128,512]{2,1,0:T(8,128)(2,1)S(1)}, u32[]{:S(2)}, u32[]{:S(2)}) collective-permute-start(bf16[2,128,512]{2,1,0:T(8,128)(2,1)S(1)} %get-tuple-element.26.kv_ref.own_ref), channel_id=1, source_target_pairs={{0,1},{1,2},{2,3},{3,4},{4,5},{5,6},{6,7},{7,8},{8,9},{9,10},{10,1... | collective-permute-start | bytes 786440 | tf_op jit(solution)/shard_map/ppermute | solution.py:37
  6.5 5.7 %collective-permute-start.1 = (bf16[2,128,512]{2,1,0:T(8,128)(2,1)S(1)}, bf16[2,128,512]{2,1,0:T(8,128)(2,1)S(1)}, u32[]{:S(2)}, u32[]{:S(2)}) collective-permute-start(bf16[2,128,512]{2,1,0:T(8,128)(2,1)S(1)} %get-tuple-element.26.kv_ref.own_ref), channel_id=1, source_target_pairs={{0,2},{2,4},{4,6},{6,8},{8,10},{10,12},{12,14},{14,16},{16,18},{18... | collective-permute-start | bytes 786440 | tf_op jit(solution)/shard_map/ppermute | solution.py:37
  10.0 3.4 %collective-permute-start.2 = (bf16[2,128,512]{2,1,0:T(8,128)(2,1)S(1)}, bf16[2,128,512]{2,1,0:T(8,128)(2,1)S(1)}, u32[]{:S(2)}, u32[]{:S(2)}) collective-permute-start(bf16[2,128,512]{2,1,0:T(8,128)(2,1)S(1)} %collective-permute-done.near_ref), channel_id=1, source_target_pairs={{0,1},{2,3},{4,5},{6,7},{8,9},{10,11},{12,13},{14,15},{16,17},{18,... | collective-permute-start | bytes 786440 | tf_op jit(solution)/shard_map/ppermute | solution.py:37
  15.7 3.2 %collective-permute-start.3 = (bf16[2,128,512]{2,1,0:T(8,128)(2,1)S(1)}, bf16[2,128,512]{2,1,0:T(8,128)(2,1)S(1)}, u32[]{:S(2)}, u32[]{:S(2)}) collective-permute-start(bf16[2,128,512]{2,1,0:T(8,128)(2,1)S(1)} %get-tuple-element.45), channel_id=1, source_target_pairs={{1,0},{3,2},{5,4},{7,6},{9,8},{11,10},{13,12},{15,14},{17,16},{19,... | collective-permute-start | bytes 786440 | tf_op jit(solution)/shard_map/ppermute | solution.py:37
  17.8 9.3 %collective-permute-start.5 = (bf16[2,128,512]{2,1,0:T(8,128)(2,1)S(1)}, bf16[2,128,512]{2,1,0:T(8,128)(2,1)S(1)}, u32[]{:S(2)}, u32[]{:S(2)}) collective-permute-start(bf16[2,128,512]{2,1,0:T(8,128)(2,1)S(1)} %get-tuple-element.45), channel_id=1, source_target_pairs={{2,0},{4,2},{6,4},{8,6},{10,8},{12,10},{14,12},{16,14},{18,16},{20... | collective-permute-start | bytes 786440 | tf_op jit(solution)/shard_map/ppermute | solution.py:37
  19.5 13.4 %collective-permute-start.4 = (bf16[2,128,512]{2,1,0:T(8,128)(2,1)S(1)}, bf16[2,128,512]{2,1,0:T(8,128)(2,1)S(1)}, u32[]{:S(2)}, u32[]{:S(2)}) collective-permute-start(bf16[2,128,512]{2,1,0:T(8,128)(2,1)S(1)} %near_terms.1), channel_id=1, source_target_pairs={{1,0},{2,1},{3,2},{4,3},{5,4},{6,5},{7,6},{8,7},{9,8},{10,9},{11,1... | collective-permute-start | bytes 786440 | tf_op jit(solution)/shard_map/ppermute | solution.py:37

commit v5 on v4

--- a/solution.py
+++ b/solution.py
@@ -131,14 +131,15 @@
             out_ref[j, 3:4, cols] = own
 
 
-def score_kernel(odd_ref, q_ref, do_ref, e_ref, d_ref, stat_ref, even_far_ref, odd_far_ref, bias_ref,
+def score_kernel(odd_ref, q_ref, do_ref, stat_ref, even_far_ref, odd_far_ref, bias_ref,
                  prob_ref, ds_ref, terms_ref, far_ref, out_ref):
     odd = odd_ref[0] == 1
     far_ref[...] = jnp.where(odd, odd_far_ref[...], even_far_ref[...])
-    for j in range(KVH):
-        lanes = slice(j * HD, (j + 1) * HD)
-        score = dot(far_ref[0, :, lanes], heads(q_ref, j), NT)
-        d_prob = dot(far_ref[1, :, lanes], heads(do_ref, j), NT)
+    def products(j):
+        lanes = slice(j * HD, (j + 1) * HD)
+        return dot(far_ref[0, :, lanes], heads(q_ref, j), NT), dot(far_ref[1, :, lanes], heads(do_ref, j), NT)
+
+    def softmax(j, score, d_prob):
         for h in range(GROUPS):
             cols = slice(h * HD, (h + 1) * HD)
             x = score[:, cols] * FACTOR + bias_ref[0]
@@ -148,33 +149,53 @@
             inv = 1.0 / (stat_ref[j, 1:2, cols] * old + down(jnp.sum, e))
             delta = (stat_ref[j, 2:3, cols] * old + down(jnp.sum, e * d_prob[:, cols])) * inv
             a = e * inv
-            b = e_ref[j, :, cols] * (old * inv)
-            prob_ref[j, 0:ROWS, cols] = a.astype(jnp.bfloat16)
-            prob_ref[j, ROWS:, cols] = b.astype(jnp.bfloat16)
-            ds_ref[j, 0:ROWS, cols] = (a * (d_prob[:, cols] - delta)).astype(jnp.bfloat16)
-            ds_ref[j, ROWS:, cols] = (b * (d_ref[j, :, cols] - delta)).astype(jnp.bfloat16)
+            prob_ref[j, :, cols] = a.astype(jnp.bfloat16)
+            ds_ref[j, :, cols] = (a * (d_prob[:, cols] - delta)).astype(jnp.bfloat16)
             out_ref[j, 0:1, cols] = stat_ref[j, 3:4, cols] * old * inv
             out_ref[j, 1:2, cols] = delta
+            out_ref[j, 2:3, cols] = old * inv
+
+    def terms(j):
+        lanes = slice(j * HD, (j + 1) * HD)
+        terms_ref[0, :, lanes] = (SCALE * dot(ds_ref[j], heads(q_ref, j), NN)).astype(jnp.bfloat16)
+        terms_ref[1, :, lanes] = dot(prob_ref[j], heads(do_ref, j), NN).astype(jnp.bfloat16)
+
     for j in range(KVH):
-        lanes = slice(j * HD, (j + 1) * HD)
-        terms_ref[0, :, lanes] = (SCALE * dot(ds_ref[j, 0:ROWS, :], heads(q_ref, j), NN)).astype(jnp.bfloat16)
-        terms_ref[1, :, lanes] = dot(prob_ref[j, 0:ROWS, :], heads(do_ref, j), NN).astype(jnp.bfloat16)
-
-
-def near_kernel(odd_ref, q_ref, do_ref, prob_ref, ds_ref, passed_ref, out_ref):
+        pair = products(j)
+        if j > 0:
+            terms(j - 1)
+        softmax(j, *pair)
+    terms(KVH - 1)
+
+
+def near_kernel(odd_ref, q_ref, do_ref, e_ref, d_ref, stat_ref, passed_ref, prob_ref, ds_ref, out_ref):
     even = odd_ref[0] == 0
-    for j in range(KVH):
-        lanes = slice(j * HD, (j + 1) * HD)
-        key_terms = SCALE * dot(ds_ref[j, ROWS:, :], heads(q_ref, j), NN)
-        value_terms = dot(prob_ref[j, ROWS:, :], heads(do_ref, j), NN)
+
+    def weights(j):
+        for h in range(GROUPS):
+            cols = slice(h * HD, (h + 1) * HD)
+            b = e_ref[j, :, cols] * stat_ref[j, 2:3, cols]
+            prob_ref[j, :, cols] = b.astype(jnp.bfloat16)
+            ds_ref[j, :, cols] = (b * (d_ref[j, :, cols] - stat_ref[j, 1:2, cols])).astype(jnp.bfloat16)
+
+    def terms(j):
+        lanes = slice(j * HD, (j + 1) * HD)
+        key_terms = SCALE * dot(ds_ref[j], heads(q_ref, j), NN)
+        value_terms = dot(prob_ref[j], heads(do_ref, j), NN)
         key_terms += jnp.where(even, passed_ref[0, :, lanes].astype(jnp.float32), 0.0)
         value_terms += jnp.where(even, passed_ref[1, :, lanes].astype(jnp.float32), 0.0)
         out_ref[0, :, lanes] = key_terms.astype(jnp.bfloat16)
         out_ref[1, :, lanes] = value_terms.astype(jnp.bfloat16)
 
-
-def finish_kernel(q_ref, do_ref, own_ref, near_ref, far_ref, prob_ref, ds_ref, e_ref, d_ref, stat_ref,
-                  att_ref, dq_ref, terms_ref):
+    weights(0)
+    for j in range(KVH):
+        if j + 1 < KVH:
+            weights(j + 1)
+        terms(j)
+
+
+def finish_kernel(q_ref, do_ref, own_ref, near_ref, far_ref, prob_ref, ds_ref, near_prob_ref, near_ds_ref,
+                  e_ref, d_ref, stat_ref, att_ref, dq_ref, terms_ref):
     p_own = e_ref[...] * stat_ref[0:1, :]
     ds_own = (p_own * (d_ref[...] - stat_ref[1:2, :])).astype(jnp.bfloat16)
     p_own = p_own.astype(jnp.bfloat16)
@@ -182,8 +203,8 @@
     terms_ref[1] = dot(p_own, heads(do_ref, 0), NN)
     k3t = jnp.concatenate([far_ref[0], near_ref[0], own_ref[0]], axis=0).T
     v3t = jnp.concatenate([far_ref[1], near_ref[1], own_ref[1]], axis=0).T
-    p3 = jnp.concatenate([prob_ref[...], p_own], axis=0)
-    ds3 = jnp.concatenate([ds_ref[...], ds_own], axis=0)
+    p3 = jnp.concatenate([prob_ref[...], near_prob_ref[...], p_own], axis=0)
+    ds3 = jnp.concatenate([ds_ref[...], near_ds_ref[...], ds_own], axis=0)
     att = dot(v3t, p3, NN)
     dq = dot(k3t, ds3, NN) * SCALE
     for h in range(GROUPS):
@@ -195,11 +216,10 @@
 PAIR = jax.ShapeDtypeStruct((2, ROWS, CUT), jnp.bfloat16)
 FULL = jax.ShapeDtypeStruct((ROWS, QH * HD), jnp.bfloat16)
 SCORE = jax.ShapeDtypeStruct((KVH, ROWS, WIDE), jnp.float32)
-TILE = jax.ShapeDtypeStruct((KVH, 2 * ROWS, WIDE), jnp.bfloat16)
+TILE = jax.ShapeDtypeStruct((KVH, ROWS, WIDE), jnp.bfloat16)
 STAT = jax.ShapeDtypeStruct((KVH, 8, WIDE), jnp.float32)
 HEAD = pl.BlockSpec((ROWS, WIDE), lambda j: (0, j))
 BOTH = pl.BlockSpec((2, ROWS, HD), lambda j: (0, 0, j))
-SQUARE = pl.BlockSpec((None, 2 * ROWS, WIDE), lambda j: (j, 0, 0))
 LINE = pl.BlockSpec((None, ROWS, WIDE), lambda j: (j, 0, 0))
 FEW = pl.BlockSpec((None, 8, WIDE), lambda j: (j, 0, 0))
 
@@ -241,41 +261,41 @@
     )(q, do, near, bias, stat)
 
 
-def scores(odd, q, do, e_near, d_near, stat, even_far, odd_far, bias):
+def scores(odd, q, do, stat, even_far, odd_far, bias):
     return pl.pallas_call(
         score_kernel,
         out_shape=(TILE, TILE, PAIR, PAIR, STAT),
-        in_specs=[SMEM] + [VMEM] * 8,
+        in_specs=[SMEM] + [VMEM] * 6,
         out_specs=(VMEM,) * 5,
         name="scores",
         compiler_params=ROOM,
         cost_estimate=cost(4),
-    )(odd, q, do, e_near, d_near, stat, even_far, odd_far, bias)
-
-
-def near_terms(odd, q, do, prob, ds, passed):
+    )(odd, q, do, stat, even_far, odd_far, bias)
+
+
+def near_terms(odd, q, do, e_near, d_near, stat, passed):
     return pl.pallas_call(
         near_kernel,
-        out_shape=PAIR,
-        in_specs=[SMEM] + [VMEM] * 5,
-        out_specs=VMEM,
+        out_shape=(TILE, TILE, PAIR),
+        in_specs=[SMEM] + [VMEM] * 6,
+        out_specs=(VMEM,) * 3,
         name="near_terms",
         compiler_params=ROOM,
         cost_estimate=cost(3),
-    )(odd, q, do, prob, ds, passed)
-
-
-def finish(q, do, own, near, far, prob, ds, e_own, d_own, stat):
+    )(odd, q, do, e_near, d_near, stat, passed)
+
+
+def finish(q, do, own, near, far, prob, ds, near_prob, near_ds, e_own, d_own, stat):
     return pl.pallas_call(
         finish_kernel,
         grid=(KVH,),
         out_shape=(FULL, FULL, jax.ShapeDtypeStruct((2, ROWS, CUT), jnp.float32)),
-        in_specs=[HEAD, HEAD, BOTH, BOTH, BOTH, SQUARE, SQUARE, LINE, LINE, FEW],
+        in_specs=[HEAD, HEAD, BOTH, BOTH, BOTH, LINE, LINE, LINE, LINE, LINE, LINE, FEW],
         out_specs=(HEAD, HEAD, BOTH),
         name="finish",
         compiler_params=ROOM,
         cost_estimate=cost(8),
-    )(q, do, own, near, far, prob, ds, e_own, d_own, stat)
+    )(q, do, own, near, far, prob, ds, near_prob, near_ds, e_own, d_own, stat)
 
 
 def body(queries, keys, values, d_out, lengths):
@@ -289,11 +309,13 @@
     near, bias = lax.optimization_barrier((near, bias))
     odd_far = shifted(near, 1, 2)
     e_near, d_near, stat = near_scores(q, do, near, bias, stat)
-    prob, ds, far_terms, far, stat = scores(odd, q, do, e_near, d_near, stat, even_far, odd_far, bias)
+    prob, ds, far_terms, far, stat = scores(odd, q, do, stat, even_far, odd_far, bias)
     passed = shifted(far_terms, -1, 2)
     far_back = shifted(far_terms, -2, 2)
-    near_back = shifted(near_terms(odd, q, do, prob, ds, passed), -1)
-    attended, d_queries, terms = finish(q, do, own, near, far, prob, ds, e_own, d_own, stat)
+    near_prob, near_ds, near_out = near_terms(odd, q, do, e_near, d_near, stat, passed)
+    near_back = shifted(near_out, -1)
+    attended, d_queries, terms = finish(
+        q, do, own, near, far, prob, ds, near_prob, near_ds, e_own, d_own, stat)
     d_keys = terms[0] + near_back[0].astype(jnp.float32) + far_back[0].astype(jnp.float32)
     d_values = terms[1] + near_back[1].astype(jnp.float32) + far_back[1].astype(jnp.float32)
     return attended, d_queries, d_keys.astype(jnp.bfloat16), d_values.astype(jnp.bfloat16)

time: 34.1 us -> 33.8 us (level)
    pallas_call x1, Pallas kernels: 2.23 us -> 1.77 us  [scores(): pl.pallas_call(score_kernel, out_shape=(TILE, TILE, PAIR, PAIR, STAT), in...]
  transfers between devices with their start and end apart: 6 -> 6, of which waited for: 4 -> 4; matrix products, arithmetic and copies ran while one was open for 0% -> 0% of each run, Pallas kernels for 23% -> 24%
where the time goes in v5:
time: 33.8 us; the launch traced here: 33.5 us
  starting transfers between devices  13.1 us (39%)
  Pallas kernels  10.7 us (32%)
  waiting for transfers between devices  8.15 us (24%)
  other arithmetic  0.81 us (2%)
  between operations  0.74 us (2%)
    ppermute x6, starting transfers between devices, shifted(): lax.ppermute(value, AXES, [(source, source + steps) for source in range(l...  13.1 us
    ppermute x6, waiting for transfers between devices, shifted(): lax.ppermute(value, AXES, [(source, source + steps) for source in range(l...  8.15 us
    pallas_call x1, Pallas kernels, finish(): pl.pallas_call(finish_kernel, grid=(KVH,), out_shape=(FULL, FULL, jax.Sha...  3.92 us
    pallas_call x1, Pallas kernels, stage(): pl.pallas_call(stage_kernel, out_shape=(jax.ShapeDtypeStruct((2, ROWS, RO...  2.22 us
    pallas_call x1, Pallas kernels, scores(): pl.pallas_call(score_kernel, out_shape=(TILE, TILE, PAIR, PAIR, STAT), in...  1.77 us
    pallas_call x1, Pallas kernels, pack(): pl.pallas_call(pack_kernel, out_shape=(PAIR, jax.ShapeDtypeStruct((1, DOC...  0.97 us
    pallas_call x1, Pallas kernels, near_terms(): pl.pallas_call(near_kernel, out_shape=(TILE, TILE, PAIR), in_specs=[SMEM]...  0.96 us
    pallas_call x1, Pallas kernels, near_scores(): pl.pallas_call(near_score_kernel, out_shape=(SCORE, SCORE, STAT), in_spec...  0.82 us
  transfers between devices with their start and end apart: 6, of which 4 were waited for; matrix products, arithmetic and copies ran while one was open for 0% of the time, Pallas kernels for 24%

profile of v5, /device:TPU:255, one launch (start us, length us, event | category | flops | bytes accessed | tf_op | source)
XLA Modules:
  0.0 33.5 jit_solution(15133170609640909629)
XLA Ops:
  0.6 1.0 %pack.1 = (bf16[2,128,512]{2,1,0:T(8,128)(2,1)S(1)}, s32[1,512]{1,0:T(1,128)S(1)}) custom-call(bf16[128,512]{1,0:T(8,128)(2,1)} %k_ref.1, bf16[128,512]{1,0:T(8,128)(2,1)} %v_ref.1, s32[1,512]{1,0:T(1,128)} %bitcast.6), custom_call_target="tpu_custom_call" | custom-call | tf_op jit(solution)/shard_map/pack/pallas_call | solution.py:228
  1.6 4.9 %collective-permute-start = (bf16[2,128,512]{2,1,0:T(8,128)(2,1)S(1)}, bf16[2,128,512]{2,1,0:T(8,128)(2,1)S(1)}, u32[]{:S(2)}, u32[]{:S(2)}) collective-permute-start(bf16[2,128,512]{2,1,0:T(8,128)(2,1)S(1)} %get-tuple-element.29.kv_ref.own_ref), channel_id=1, source_target_pairs={{0,1},{1,2},{2,3},{3,4},{4,5},{5,6},{6,7},{7,8},{8,9},{9,10},{10,1... | collective-permute-start | bytes 786440 | tf_op jit(solution)/shard_map/ppermute | solution.py:37
  6.5 0.7 %collective-permute-start.1 = (bf16[2,128,512]{2,1,0:T(8,128)(2,1)S(1)}, bf16[2,128,512]{2,1,0:T(8,128)(2,1)S(1)}, u32[]{:S(2)}, u32[]{:S(2)}) collective-permute-start(bf16[2,128,512]{2,1,0:T(8,128)(2,1)S(1)} %get-tuple-element.29.kv_ref.own_ref), channel_id=1, source_target_pairs={{0,2},{2,4},{4,6},{6,8},{8,10},{10,12},{12,14},{14,16},{16,18},{18... | collective-permute-start | bytes 786440 | tf_op jit(solution)/shard_map/ppermute | solution.py:37
  7.2 2.2 %stage.1 = (f32[2,128,128]{2,1,0:T(8,128)S(1)}, bf16[128,3584]{1,0:T(8,128)(2,1)S(1)}, bf16[128,3584]{1,0:T(8,128)(2,1)S(1)}, f32[4,128,896]{2,1,0:T(8,128)S(1)}...) custom-call(s32[1]{0:T(128)S(6)} %mul.7.start_ref, s32[1,512]{1,0:T(1,128)S(1)} %get-tuple-element.28.len_ref, ...), custom_call_target="tpu_custom_call" | custom-call | bytes 9000000 | tf_op jit(solution)/shard_map/stage/pallas_call | solution.py:240
  9.4 0.6 %collective-permute-done.near_ref = bf16[2,128,512]{2,1,0:T(8,128)(2,1)S(1)} collective-permute-done((bf16[2,128,512]{2,1,0:T(8,128)(2,1)S(1)}, bf16[2,128,512]{2,1,0:T(8,128)(2,1)S(1)}, u32[]{:S(2)}, u32[]{:S(2)}) %collective-permute-start) | collective-permute-done | bytes 262176 | tf_op jit(solution)/shard_map/ppermute | solution.py:37
  10.0 1.3 %collective-permute-start.2 = (bf16[2,128,512]{2,1,0:T(8,128)(2,1)S(1)}, bf16[2,128,512]{2,1,0:T(8,128)(2,1)S(1)}, u32[]{:S(2)}, u32[]{:S(2)}) collective-permute-start(bf16[2,128,512]{2,1,0:T(8,128)(2,1)S(1)} %collective-permute-done.near_ref), channel_id=1, source_target_pairs={{0,1},{2,3},{4,5},{6,7},{8,9},{10,11},{12,13},{14,15},{16,17},{18,... | collective-permute-start | bytes 786440 | tf_op jit(solution)/shard_map/ppermute | solution.py:37
  11.3 0.8 %near_scores.1 = (f32[4,128,896]{2,1,0:T(8,128)S(1)}, f32[4,128,896]{2,1,0:T(8,128)S(1)}, f32[4,8,896]{2,1,0:T(8,128)S(1)}) custom-call(bf16[128,3584]{1,0:T(8,128)(2,1)S(1)} %get-tuple-element.30.q_ref, bf16[128,3584]{1,0:T(8,128)(2,1)S(1)} %get-tuple-element.31.do_ref, bf16[2,128,512]{2,1,0:T(8,128)(2,1)S(1)} %collective-permute-done.near_ref, ...), custom_call_target="tpu_custom_call" | custom-call | bytes 6000000 | tf_op jit(solution)/shard_map/near_scores/pallas_call | solution.py:253
  12.2 0.0 collective-permute-done.1.even_far_ref
  12.2 1.3 %collective-permute-done.2.odd_far_ref = bf16[2,128,512]{2,1,0:T(8,128)(2,1)S(1)} collective-permute-done((bf16[2,128,512]{2,1,0:T(8,128)(2,1)S(1)}, bf16[2,128,512]{2,1,0:T(8,128)(2,1)S(1)}, u32[]{:S(2)}, u32[]{:S(2)}) %collective-permute-start.2) | collective-permute-done | bytes 262176 | tf_op jit(solution)/shard_map/ppermute | solution.py:37
  13.5 1.8 %scores.1 = (bf16[4,128,896]{2,1,0:T(8,128)(2,1)S(1)}, bf16[4,128,896]{2,1,0:T(8,128)(2,1)S(1)}, bf16[2,128,512]{2,1,0:T(8,128)(2,1)S(1)}, bf16[2,128,512]{2,1,0:T(8,128)(2,1)S(1)}, f32[4,8,896]{2,1,0:T(8,128)S(1)}) custom-call(s32[1]{0:T(128)S(6)} %select_n.7.odd_ref, bf16[128,3584]{1,0:T(8,128)(2,1)S(1)} %get-tuple-element.30.q_ref, ...), custom_call_target="tpu_custom_call" | custom-call | bytes 12000000 | tf_op jit(solution)/shard_map/scores/pallas_call | solution.py:265
  15.2 2.1 %collective-permute-start.3 = (bf16[2,128,512]{2,1,0:T(8,128)(2,1)S(1)}, bf16[2,128,512]{2,1,0:T(8,128)(2,1)S(1)}, u32[]{:S(2)}, u32[]{:S(2)}) collective-permute-start(bf16[2,128,512]{2,1,0:T(8,128)(2,1)S(1)} %get-tuple-element.43), channel_id=1, source_target_pairs={{1,0},{3,2},{5,4},{7,6},{9,8},{11,10},{13,12},{15,14},{17,16},{19,... | collective-permute-start | bytes 786440 | tf_op jit(solution)/shard_map/ppermute | solution.py:37
  17.3 0.7 %collective-permute-start.5 = (bf16[2,128,512]{2,1,0:T(8,128)(2,1)S(1)}, bf16[2,128,512]{2,1,0:T(8,128)(2,1)S(1)}, u32[]{:S(2)}, u32[]{:S(2)}) collective-permute-start(bf16[2,128,512]{2,1,0:T(8,128)(2,1)S(1)} %get-tuple-element.43), channel_id=1, source_target_pairs={{2,0},{4,2},{6,4},{8,6},{10,8},{12,10},{14,12},{16,14},{18,16},{20... | collective-permute-start | bytes 786440 | tf_op jit(solution)/shard_map/ppermute | solution.py:37
  18.0 0.4 %collective-permute-done.3.passed_ref = bf16[2,128,512]{2,1,0:T(8,128)(2,1)S(1)} collective-permute-done((bf16[2,128,512]{2,1,0:T(8,128)(2,1)S(1)}, bf16[2,128,512]{2,1,0:T(8,128)(2,1)S(1)}, u32[]{:S(2)}, u32[]{:S(2)}) %collective-permute-start.3) | collective-permute-done | bytes 262176 | tf_op jit(solution)/shard_map/ppermute | solution.py:37
  18.4 1.0 %near_terms.1 = (bf16[4,128,896]{2,1,0:T(8,128)(2,1)S(1)}, bf16[4,128,896]{2,1,0:T(8,128)(2,1)S(1)}, bf16[2,128,512]{2,1,0:T(8,128)(2,1)S(1)}) custom-call(s32[1]{0:T(128)S(6)} %select_n.7.odd_ref, bf16[128,3584]{1,0:T(8,128)(2,1)S(1)} %get-tuple-element.30.q_ref, bf16[128,3584]{1,0:T(8,128)(2,1)S(1)} %get-tuple-element.31.do_ref, ...), custom_call_target="tpu_custom_call" | custom-call | bytes 9000000 | tf_op jit(solution)/shard_map/near_terms/pallas_call | solution.py:277
  19.4 3.5 %collective-permute-start.4 = (bf16[2,128,512]{2,1,0:T(8,128)(2,1)S(1)}, bf16[2,128,512]{2,1,0:T(8,128)(2,1)S(1)}, u32[]{:S(2)}, u32[]{:S(2)}) collective-permute-start(bf16[2,128,512]{2,1,0:T(8,128)(2,1)S(1)} %get-tuple-element.51), channel_id=1, source_target_pairs={{1,0},{2,1},{3,2},{4,3},{5,4},{6,5},{7,6},{8,7},{9,8},{10,9},{11,1... | collective-permute-start | bytes 786440 | tf_op jit(solution)/shard_map/ppermute | solution.py:37
  22.9 3.9 %finish.1 = (bf16[128,3584]{1,0:T(8,128)(2,1)}, bf16[128,3584]{1,0:T(8,128)(2,1)}, f32[2,128,512]{2,1,0:T(8,128)S(1)}) custom-call(bf16[128,3584]{1,0:T(8,128)(2,1)S(1)} %get-tuple-element.30.q_ref, bf16[128,3584]{1,0:T(8,128)(2,1)S(1)} %get-tuple-element.31.do_ref, bf16[2,128,512]{2,1,0:T(8,128)(2,1)S(1)} %get-tuple-element.29.kv_ref.own_ref, ...), custom_call_target="tpu_custom_call" | custom-call | bytes 24000000 | tf_op jit(solution)/shard_map/finish/pallas_call | solution.py:289
  26.8 0.0 collective-permute-done.5
  26.8 5.8 %collective-permute-done.4 = bf16[2,128,512]{2,1,0:T(8,128)(2,1)S(1)} collective-permute-done((bf16[2,128,512]{2,1,0:T(8,128)(2,1)S(1)}, bf16[2,128,512]{2,1,0:T(8,128)(2,1)S(1)}, u32[]{:S(2)}, u32[]{:S(2)}) %collective-permute-start.4) | collective-permute-done | bytes 262176 | tf_op jit(solution)/shard_map/ppermute | solution.py:37
  32.7 0.8 %fusion.1 = (bf16[128,512]{1,0:T(8,128)(2,1)}, bf16[128,512]{1,0:T(8,128)(2,1)}) fusion(f32[2,128,512]{2,1,0:T(8,128)S(1)} %get-tuple-element.50, bf16[2,128,512]{2,1,0:T(8,128)(2,1)S(1)} %collective-permute-done.5, bf16[2,128,512]{2,1,0:T(8,128)(2,1)S(1)} %collective-permute-done.4), kind=kLoop, calls=%fused_computation.3 | loop fusion | flops 655360 | bytes 1310720 | tf_op jit(solution)/shard_map/convert_element_type | solution.py:321
Async XLA Ops:
  1.6 8.4 %collective-permute-start = (bf16[2,128,512]{2,1,0:T(8,128)(2,1)S(1)}, bf16[2,128,512]{2,1,0:T(8,128)(2,1)S(1)}, u32[]{:S(2)}, u32[]{:S(2)}) collective-permute-start(bf16[2,128,512]{2,1,0:T(8,128)(2,1)S(1)} %get-tuple-element.29.kv_ref.own_ref), channel_id=1, source_target_pairs={{0,1},{1,2},{2,3},{3,4},{4,5},{5,6},{6,7},{7,8},{8,9},{9,10},{10,1... | collective-permute-start | bytes 786440 | tf_op jit(solution)/shard_map/ppermute | solution.py:37
  6.5 5.7 %collective-permute-start.1 = (bf16[2,128,512]{2,1,0:T(8,128)(2,1)S(1)}, bf16[2,128,512]{2,1,0:T(8,128)(2,1)S(1)}, u32[]{:S(2)}, u32[]{:S(2)}) collective-permute-start(bf16[2,128,512]{2,1,0:T(8,128)(2,1)S(1)} %get-tuple-element.29.kv_ref.own_ref), channel_id=1, source_target_pairs={{0,2},{2,4},{4,6},{6,8},{8,10},{10,12},{12,14},{14,16},{16,18},{18... | collective-permute-start | bytes 786440 | tf_op jit(solution)/shard_map/ppermute | solution.py:37
  10.0 3.4 %collective-permute-start.2 = (bf16[2,128,512]{2,1,0:T(8,128)(2,1)S(1)}, bf16[2,128,512]{2,1,0:T(8,128)(2,1)S(1)}, u32[]{:S(2)}, u32[]{:S(2)}) collective-permute-start(bf16[2,128,512]{2,1,0:T(8,128)(2,1)S(1)} %collective-permute-done.near_ref), channel_id=1, source_target_pairs={{0,1},{2,3},{4,5},{6,7},{8,9},{10,11},{12,13},{14,15},{16,17},{18,... | collective-permute-start | bytes 786440 | tf_op jit(solution)/shard_map/ppermute | solution.py:37
  15.2 3.2 %collective-permute-start.3 = (bf16[2,128,512]{2,1,0:T(8,128)(2,1)S(1)}, bf16[2,128,512]{2,1,0:T(8,128)(2,1)S(1)}, u32[]{:S(2)}, u32[]{:S(2)}) collective-permute-start(bf16[2,128,512]{2,1,0:T(8,128)(2,1)S(1)} %get-tuple-element.43), channel_id=1, source_target_pairs={{1,0},{3,2},{5,4},{7,6},{9,8},{11,10},{13,12},{15,14},{17,16},{19,... | collective-permute-start | bytes 786440 | tf_op jit(solution)/shard_map/ppermute | solution.py:37
  17.3 9.6 %collective-permute-start.5 = (bf16[2,128,512]{2,1,0:T(8,128)(2,1)S(1)}, bf16[2,128,512]{2,1,0:T(8,128)(2,1)S(1)}, u32[]{:S(2)}, u32[]{:S(2)}) collective-permute-start(bf16[2,128,512]{2,1,0:T(8,128)(2,1)S(1)} %get-tuple-element.43), channel_id=1, source_target_pairs={{2,0},{4,2},{6,4},{8,6},{10,8},{12,10},{14,12},{16,14},{18,16},{20... | collective-permute-start | bytes 786440 | tf_op jit(solution)/shard_map/ppermute | solution.py:37
  19.4 13.3 %collective-permute-start.4 = (bf16[2,128,512]{2,1,0:T(8,128)(2,1)S(1)}, bf16[2,128,512]{2,1,0:T(8,128)(2,1)S(1)}, u32[]{:S(2)}, u32[]{:S(2)}) collective-permute-start(bf16[2,128,512]{2,1,0:T(8,128)(2,1)S(1)} %get-tuple-element.51), channel_id=1, source_target_pairs={{1,0},{2,1},{3,2},{4,3},{5,4},{6,5},{7,6},{8,7},{9,8},{10,9},{11,1... | collective-permute-start | bytes 786440 | tf_op jit(solution)/shard_map/ppermute | solution.py:37

commit v6 on v5

--- a/solution.py
+++ b/solution.py
@@ -73,7 +73,7 @@
 
 
 def stage_kernel(start_ref, len_ref, q_in, do_in, kv_ref,
-                 bias_ref, q_ref, do_ref, e_ref, d_ref, stat_ref, sems):
+                 bias_ref, live_ref, q_ref, do_ref, e_ref, d_ref, stat_ref, sems):
     copies = []
     for i, wide in enumerate((slice(0, WIDE), slice(WIDE, KVH * WIDE))):
         copies.append(pltpu.make_async_copy(q_in.at[:, wide], q_ref.at[:, wide], sems.at[2 * i]))
@@ -91,7 +91,9 @@
     s = lax.broadcasted_iota(jnp.int32, (ROWS, ROWS), 0)
     t = lax.broadcasted_iota(jnp.int32, (ROWS, ROWS), 1)
     own_bias = jnp.where((s <= t) & (s >= first), 0.0, NEG)
-    bias_ref[0] = jnp.where((s > t) & (s - 2 * ROWS >= first), 0.0, NEG)
+    far_bias = jnp.where((s > t) & (s - 2 * ROWS >= first), 0.0, NEG)
+    bias_ref[0] = far_bias
+    live_ref[...] = jnp.broadcast_to(jnp.max(down(jnp.max, far_bias), axis=1, keepdims=True), (8, HD))
     bias_ref[1] = jnp.where(s - ROWS >= first, 0.0, NEG)
     for j in range(KVH):
         lanes = slice(j * HD, (j + 1) * HD)
@@ -131,7 +133,7 @@
             out_ref[j, 3:4, cols] = own
 
 
-def score_kernel(odd_ref, q_ref, do_ref, stat_ref, even_far_ref, odd_far_ref, bias_ref,
+def score_kernel(odd_ref, live_ref, q_ref, do_ref, stat_ref, even_far_ref, odd_far_ref, bias_ref,
                  prob_ref, ds_ref, terms_ref, far_ref, out_ref):
     odd = odd_ref[0] == 1
     far_ref[...] = jnp.where(odd, odd_far_ref[...], even_far_ref[...])
@@ -160,17 +162,30 @@
         terms_ref[0, :, lanes] = (SCALE * dot(ds_ref[j], heads(q_ref, j), NN)).astype(jnp.bfloat16)
         terms_ref[1, :, lanes] = dot(prob_ref[j], heads(do_ref, j), NN).astype(jnp.bfloat16)
 
-    for j in range(KVH):
-        pair = products(j)
-        if j > 0:
-            terms(j - 1)
-        softmax(j, *pair)
-    terms(KVH - 1)
-
-
-def near_kernel(odd_ref, q_ref, do_ref, e_ref, d_ref, stat_ref, passed_ref, prob_ref, ds_ref, out_ref):
-    even = odd_ref[0] == 0
-
+    live = jnp.max(live_ref[...]) > 0.5 * NEG
+
+    @pl.when(live)
+    def _():
+        for j in range(KVH):
+            pair = products(j)
+            if j > 0:
+                terms(j - 1)
+            softmax(j, *pair)
+        terms(KVH - 1)
+
+    @pl.when(jnp.logical_not(live))
+    def _():
+        prob_ref[...] = jnp.zeros_like(prob_ref)
+        ds_ref[...] = jnp.zeros_like(ds_ref)
+        terms_ref[...] = jnp.zeros_like(terms_ref)
+        for j in range(KVH):
+            inv = 1.0 / stat_ref[j, 1:2, :]
+            out_ref[j, 0:1, :] = stat_ref[j, 3:4, :] * inv
+            out_ref[j, 1:2, :] = stat_ref[j, 2:3, :] * inv
+            out_ref[j, 2:3, :] = inv
+
+
+def near_kernel(q_ref, do_ref, e_ref, d_ref, stat_ref, prob_ref, ds_ref, out_ref):
     def weights(j):
         for h in range(GROUPS):
             cols = slice(h * HD, (h + 1) * HD)
@@ -180,18 +195,19 @@
 
     def terms(j):
         lanes = slice(j * HD, (j + 1) * HD)
-        key_terms = SCALE * dot(ds_ref[j], heads(q_ref, j), NN)
-        value_terms = dot(prob_ref[j], heads(do_ref, j), NN)
-        key_terms += jnp.where(even, passed_ref[0, :, lanes].astype(jnp.float32), 0.0)
-        value_terms += jnp.where(even, passed_ref[1, :, lanes].astype(jnp.float32), 0.0)
-        out_ref[0, :, lanes] = key_terms.astype(jnp.bfloat16)
-        out_ref[1, :, lanes] = value_terms.astype(jnp.bfloat16)
+        out_ref[0, :, lanes] = SCALE * dot(ds_ref[j], heads(q_ref, j), NN)
+        out_ref[1, :, lanes] = dot(prob_ref[j], heads(do_ref, j), NN)
 
     weights(0)
     for j in range(KVH):
         if j + 1 < KVH:
             weights(j + 1)
         terms(j)
+
+
+def add_kernel(odd_ref, terms_ref, passed_ref, out_ref):
+    passed = jnp.where(odd_ref[0] == 0, passed_ref[...].astype(jnp.float32), 0.0)
+    out_ref[...] = (terms_ref[...] + passed).astype(jnp.bfloat16)
 
 
 def finish_kernel(q_ref, do_ref, own_ref, near_ref, far_ref, prob_ref, ds_ref, near_prob_ref, near_ds_ref,
@@ -216,7 +232,9 @@
 PAIR = jax.ShapeDtypeStruct((2, ROWS, CUT), jnp.bfloat16)
 FULL = jax.ShapeDtypeStruct((ROWS, QH * HD), jnp.bfloat16)
 SCORE = jax.ShapeDtypeStruct((KVH, ROWS, WIDE), jnp.float32)
+SUMS = jax.ShapeDtypeStruct((2, ROWS, CUT), jnp.float32)
 TILE = jax.ShapeDtypeStruct((KVH, ROWS, WIDE), jnp.bfloat16)
+FLAG = jax.ShapeDtypeStruct((8, HD), jnp.float32)
 STAT = jax.ShapeDtypeStruct((KVH, 8, WIDE), jnp.float32)
 HEAD = pl.BlockSpec((ROWS, WIDE), lambda j: (0, j))
 BOTH = pl.BlockSpec((2, ROWS, HD), lambda j: (0, 0, j))
@@ -239,9 +257,9 @@
 def stage(start, lengths, queries, d_out, own):
     return pl.pallas_call(
         stage_kernel,
-        out_shape=(jax.ShapeDtypeStruct((2, ROWS, ROWS), jnp.float32), FULL, FULL, SCORE, SCORE, STAT),
+        out_shape=(jax.ShapeDtypeStruct((2, ROWS, ROWS), jnp.float32), FLAG, FULL, FULL, SCORE, SCORE, STAT),
         in_specs=[SMEM, VMEM, HBM, HBM, VMEM],
-        out_specs=(VMEM,) * 6,
+        out_specs=(VMEM,) * 7,
         scratch_shapes=[pltpu.SemaphoreType.DMA((4,))],
         name="stage",
         compiler_params=ROOM,
@@ -261,35 +279,47 @@
     )(q, do, near, bias, stat)
 
 
-def scores(odd, q, do, stat, even_far, odd_far, bias):
+def scores(odd, live, q, do, stat, even_far, odd_far, bias):
     return pl.pallas_call(
         score_kernel,
         out_shape=(TILE, TILE, PAIR, PAIR, STAT),
-        in_specs=[SMEM] + [VMEM] * 6,
+        in_specs=[SMEM] + [VMEM] * 7,
         out_specs=(VMEM,) * 5,
         name="scores",
         compiler_params=ROOM,
         cost_estimate=cost(4),
-    )(odd, q, do, stat, even_far, odd_far, bias)
-
-
-def near_terms(odd, q, do, e_near, d_near, stat, passed):
+    )(odd, live, q, do, stat, even_far, odd_far, bias)
+
+
+def near_terms(q, do, e_near, d_near, stat):
     return pl.pallas_call(
         near_kernel,
-        out_shape=(TILE, TILE, PAIR),
-        in_specs=[SMEM] + [VMEM] * 6,
+        out_shape=(TILE, TILE, SUMS),
+        in_specs=[VMEM] * 5,
         out_specs=(VMEM,) * 3,
         name="near_terms",
         compiler_params=ROOM,
-        cost_estimate=cost(3),
-    )(odd, q, do, e_near, d_near, stat, passed)
+        cost_estimate=cost(1),
+    )(q, do, e_near, d_near, stat)
+
+
+def add_passed(odd, terms, passed):
+    return pl.pallas_call(
+        add_kernel,
+        out_shape=PAIR,
+        in_specs=[SMEM, VMEM, VMEM],
+        out_specs=VMEM,
+        name="add_passed",
+        compiler_params=ROOM,
+        cost_estimate=cost(0.1),
+    )(odd, terms, passed)
 
 
 def finish(q, do, own, near, far, prob, ds, near_prob, near_ds, e_own, d_own, stat):
     return pl.pallas_call(
         finish_kernel,
         grid=(KVH,),
-        out_shape=(FULL, FULL, jax.ShapeDtypeStruct((2, ROWS, CUT), jnp.float32)),
+        out_shape=(FULL, FULL, SUMS),
         in_specs=[HEAD, HEAD, BOTH, BOTH, BOTH, LINE, LINE, LINE, LINE, LINE, LINE, FEW],
         out_specs=(HEAD, HEAD, BOTH),
         name="finish",
@@ -305,15 +335,15 @@
     index = lax.axis_index(AXES).astype(jnp.int32).reshape(1)
     start = index * ROWS
     odd = index % 2
-    bias, q, do, e_own, d_own, stat = stage(start, lens, queries, d_out, own)
+    bias, live, q, do, e_own, d_own, stat = stage(start, lens, queries, d_out, own)
     near, bias = lax.optimization_barrier((near, bias))
     odd_far = shifted(near, 1, 2)
     e_near, d_near, stat = near_scores(q, do, near, bias, stat)
-    prob, ds, far_terms, far, stat = scores(odd, q, do, stat, even_far, odd_far, bias)
+    prob, ds, far_terms, far, stat = scores(odd, live, q, do, stat, even_far, odd_far, bias)
     passed = shifted(far_terms, -1, 2)
     far_back = shifted(far_terms, -2, 2)
-    near_prob, near_ds, near_out = near_terms(odd, q, do, e_near, d_near, stat, passed)
-    near_back = shifted(near_out, -1)
+    near_prob, near_ds, near_out = near_terms(q, do, e_near, d_near, stat)
+    near_back = shifted(add_passed(odd, near_out, passed), -1)
     attended, d_queries, terms = finish(
         q, do, own, near, far, prob, ds, near_prob, near_ds, e_own, d_own, stat)
     d_keys = terms[0] + near_back[0].astype(jnp.float32) + far_back[0].astype(jnp.float32)

time: 33.8 us -> 32.3 us (0.956)
  Pallas kernels: 10.7 us -> 9.19 us
  waiting for transfers between devices: 8.15 us -> 7.63 us
  starting transfers between devices: 13.1 us -> 13.5 us
    pallas_call x1, Pallas kernels: 1.77 us -> 0.31 us  [scores(): pl.pallas_call(score_kernel, out_shape=(TILE, TILE, PAIR, PAIR, STAT), in...]
    ppermute x6, waiting for transfers between devices: 8.15 us -> 7.63 us  [shifted(): lax.ppermute(value, AXES, [(source, source + steps) for source in range(l...]
    ppermute x6, starting transfers between devices: 13.1 us -> 13.5 us  [shifted(): lax.ppermute(value, AXES, [(source, source + steps) for source in range(l...]
    pallas_call x2 -> x3, Pallas kernels: 4.88 us -> 4.87 us  [the longest x1 3.93 us: finish(): pl.pallas_call(finish_kernel, grid=(KVH,), out_shape=(FULL, FULL, SUMS),...]
  transfers between devices with their start and end apart: 6 -> 6, of which waited for: 4 -> 3; matrix products, arithmetic and copies ran while one was open for 0% -> 0% of each run, Pallas kernels for 24% -> 25%
where the time goes in v6:
time: 32.3 us; the launch traced here: 31.9 us
  starting transfers between devices  13.5 us (42%)
  Pallas kernels  9.19 us (28%)
  waiting for transfers between devices  7.63 us (24%)
  other arithmetic  0.82 us (3%)
  between operations  0.76 us (2%)
    ppermute x6, starting transfers between devices, shifted(): lax.ppermute(value, AXES, [(source, source + steps) for source in range(l...  13.5 us
    ppermute x6, waiting for transfers between devices, shifted(): lax.ppermute(value, AXES, [(source, source + steps) for source in range(l...  7.63 us
    pallas_call x1, Pallas kernels, finish(): pl.pallas_call(finish_kernel, grid=(KVH,), out_shape=(FULL, FULL, SUMS),...  3.93 us
    pallas_call x1, Pallas kernels, stage(): pl.pallas_call(stage_kernel, out_shape=(jax.ShapeDtypeStruct((2, ROWS, RO...  2.22 us
    pallas_call x1, Pallas kernels, pack(): pl.pallas_call(pack_kernel, out_shape=(PAIR, jax.ShapeDtypeStruct((1, DOC...  0.97 us
    pallas_call x1, Pallas kernels, near_terms(): pl.pallas_call(near_kernel, out_shape=(TILE, TILE, SUMS), in_specs=[VMEM]...  0.87 us
    pallas_call x1, Pallas kernels, near_scores(): pl.pallas_call(near_score_kernel, out_shape=(SCORE, SCORE, STAT), in_spec...  0.82 us
    convert_element_type x1, other arithmetic, body(): d_values.astype(jnp.bfloat16)  0.82 us
  transfers between devices with their start and end apart: 6, of which 3 were waited for; matrix products, arithmetic and copies ran while one was open for 0% of the time, Pallas kernels for 25%

profile of v6, /device:TPU:255, one launch (start us, length us, event | category | flops | bytes accessed | tf_op | source)
XLA Modules:
  0.0 31.9 jit_solution(7787416928796088736)
XLA Ops:
  0.6 1.0 %pack.1 = (bf16[2,128,512]{2,1,0:T(8,128)(2,1)S(1)}, s32[1,512]{1,0:T(1,128)S(1)}) custom-call(bf16[128,512]{1,0:T(8,128)(2,1)} %k_ref.1, bf16[128,512]{1,0:T(8,128)(2,1)} %v_ref.1, s32[1,512]{1,0:T(1,128)} %bitcast.6), custom_call_target="tpu_custom_call" | custom-call | tf_op jit(solution)/shard_map/pack/pallas_call | solution.py:246
  1.6 4.9 %collective-permute-start = (bf16[2,128,512]{2,1,0:T(8,128)(2,1)S(1)}, bf16[2,128,512]{2,1,0:T(8,128)(2,1)S(1)}, u32[]{:S(2)}, u32[]{:S(2)}) collective-permute-start(bf16[2,128,512]{2,1,0:T(8,128)(2,1)S(1)} %get-tuple-element.30.kv_ref.own_ref), channel_id=1, source_target_pairs={{0,1},{1,2},{2,3},{3,4},{4,5},{5,6},{6,7},{7,8},{8,9},{9,10},{10,1... | collective-permute-start | bytes 786440 | tf_op jit(solution)/shard_map/ppermute | solution.py:37
  6.5 0.7 %collective-permute-start.1 = (bf16[2,128,512]{2,1,0:T(8,128)(2,1)S(1)}, bf16[2,128,512]{2,1,0:T(8,128)(2,1)S(1)}, u32[]{:S(2)}, u32[]{:S(2)}) collective-permute-start(bf16[2,128,512]{2,1,0:T(8,128)(2,1)S(1)} %get-tuple-element.30.kv_ref.own_ref), channel_id=1, source_target_pairs={{0,2},{2,4},{4,6},{6,8},{8,10},{10,12},{12,14},{14,16},{16,18},{18... | collective-permute-start | bytes 786440 | tf_op jit(solution)/shard_map/ppermute | solution.py:37
  7.2 2.2 %stage.1 = (f32[2,128,128]{2,1,0:T(8,128)S(1)}, f32[8,128]{1,0:T(8,128)S(1)}, bf16[128,3584]{1,0:T(8,128)(2,1)S(1)}, bf16[128,3584]{1,0:T(8,128)(2,1)S(1)}, f32[...) custom-call(s32[1]{0:T(128)S(6)} %mul.7.start_ref, ...), custom_call_target="tpu_custom_call" | custom-call | bytes 9000000 | tf_op jit(solution)/shard_map/stage/pallas_call | solution.py:258
  9.4 0.6 %collective-permute-done.near_ref = bf16[2,128,512]{2,1,0:T(8,128)(2,1)S(1)} collective-permute-done((bf16[2,128,512]{2,1,0:T(8,128)(2,1)S(1)}, bf16[2,128,512]{2,1,0:T(8,128)(2,1)S(1)}, u32[]{:S(2)}, u32[]{:S(2)}) %collective-permute-start) | collective-permute-done | bytes 262176 | tf_op jit(solution)/shard_map/ppermute | solution.py:37
  10.0 1.3 %collective-permute-start.2 = (bf16[2,128,512]{2,1,0:T(8,128)(2,1)S(1)}, bf16[2,128,512]{2,1,0:T(8,128)(2,1)S(1)}, u32[]{:S(2)}, u32[]{:S(2)}) collective-permute-start(bf16[2,128,512]{2,1,0:T(8,128)(2,1)S(1)} %collective-permute-done.near_ref), channel_id=1, source_target_pairs={{0,1},{2,3},{4,5},{6,7},{8,9},{10,11},{12,13},{14,15},{16,17},{18,... | collective-permute-start | bytes 786440 | tf_op jit(solution)/shard_map/ppermute | solution.py:37
  11.3 0.8 %near_scores.1 = (f32[4,128,896]{2,1,0:T(8,128)S(1)}, f32[4,128,896]{2,1,0:T(8,128)S(1)}, f32[4,8,896]{2,1,0:T(8,128)S(1)}) custom-call(bf16[128,3584]{1,0:T(8,128)(2,1)S(1)} %get-tuple-element.31.q_ref, bf16[128,3584]{1,0:T(8,128)(2,1)S(1)} %get-tuple-element.32.do_ref, bf16[2,128,512]{2,1,0:T(8,128)(2,1)S(1)} %collective-permute-done.near_ref, ...), custom_call_target="tpu_custom_call" | custom-call | bytes 6000000 | tf_op jit(solution)/shard_map/near_scores/pallas_call | solution.py:271
  12.2 0.0 collective-permute-done.1.even_far_ref
  12.2 1.3 %collective-permute-done.2.odd_far_ref = bf16[2,128,512]{2,1,0:T(8,128)(2,1)S(1)} collective-permute-done((bf16[2,128,512]{2,1,0:T(8,128)(2,1)S(1)}, bf16[2,128,512]{2,1,0:T(8,128)(2,1)S(1)}, u32[]{:S(2)}, u32[]{:S(2)}) %collective-permute-start.2) | collective-permute-done | bytes 262176 | tf_op jit(solution)/shard_map/ppermute | solution.py:37
  13.5 0.3 scores.1
  13.8 2.1 %collective-permute-start.3 = (bf16[2,128,512]{2,1,0:T(8,128)(2,1)S(1)}, bf16[2,128,512]{2,1,0:T(8,128)(2,1)S(1)}, u32[]{:S(2)}, u32[]{:S(2)}) collective-permute-start(bf16[2,128,512]{2,1,0:T(8,128)(2,1)S(1)} %get-tuple-element.53), channel_id=1, source_target_pairs={{1,0},{3,2},{5,4},{7,6},{9,8},{11,10},{13,12},{15,14},{17,16},{19,... | collective-permute-start | bytes 786440 | tf_op jit(solution)/shard_map/ppermute | solution.py:37
  15.8 0.7 %collective-permute-start.5 = (bf16[2,128,512]{2,1,0:T(8,128)(2,1)S(1)}, bf16[2,128,512]{2,1,0:T(8,128)(2,1)S(1)}, u32[]{:S(2)}, u32[]{:S(2)}) collective-permute-start(bf16[2,128,512]{2,1,0:T(8,128)(2,1)S(1)} %get-tuple-element.53), channel_id=1, source_target_pairs={{2,0},{4,2},{6,4},{8,6},{10,8},{12,10},{14,12},{16,14},{18,16},{20... | collective-permute-start | bytes 786440 | tf_op jit(solution)/shard_map/ppermute | solution.py:37
  16.5 0.9 %near_terms.1 = (bf16[4,128,896]{2,1,0:T(8,128)(2,1)S(1)}, bf16[4,128,896]{2,1,0:T(8,128)(2,1)S(1)}, f32[2,128,512]{2,1,0:T(8,128)S(1)}) custom-call(bf16[128,3584]{1,0:T(8,128)(2,1)S(1)} %get-tuple-element.31.q_ref, bf16[128,3584]{1,0:T(8,128)(2,1)S(1)} %get-tuple-element.32.do_ref, f32[4,128,896]{2,1,0:T(8,128)S(1)} %get-tuple-element.42.e_ref, ...), custom_call_target="tpu_custom_call" | custom-call | bytes 3000000 | tf_op jit(solution)/shard_map/near_terms/pallas_call | solution.py:295
  17.4 0.0 collective-permute-done.3.passed_ref
  17.4 0.1 add_passed.1
  17.5 4.0 %collective-permute-start.4 = (bf16[2,128,512]{2,1,0:T(8,128)(2,1)S(1)}, bf16[2,128,512]{2,1,0:T(8,128)(2,1)S(1)}, u32[]{:S(2)}, u32[]{:S(2)}) collective-permute-start(bf16[2,128,512]{2,1,0:T(8,128)(2,1)S(1)} %add_passed.1), channel_id=1, source_target_pairs={{1,0},{2,1},{3,2},{4,3},{5,4},{6,5},{7,6},{8,7},{9,8},{10,9},{11,1... | collective-permute-start | bytes 786440 | tf_op jit(solution)/shard_map/ppermute | solution.py:37
  21.4 3.9 %finish.1 = (bf16[128,3584]{1,0:T(8,128)(2,1)}, bf16[128,3584]{1,0:T(8,128)(2,1)}, f32[2,128,512]{2,1,0:T(8,128)S(1)}) custom-call(bf16[128,3584]{1,0:T(8,128)(2,1)S(1)} %get-tuple-element.31.q_ref, bf16[128,3584]{1,0:T(8,128)(2,1)S(1)} %get-tuple-element.32.do_ref, bf16[2,128,512]{2,1,0:T(8,128)(2,1)S(1)} %get-tuple-element.30.kv_ref.own_ref, ...), custom_call_target="tpu_custom_call" | custom-call | bytes 24000000 | tf_op jit(solution)/shard_map/finish/pallas_call | solution.py:319
  25.4 0.0 collective-permute-done.5
  25.4 5.7 %collective-permute-done.4 = bf16[2,128,512]{2,1,0:T(8,128)(2,1)S(1)} collective-permute-done((bf16[2,128,512]{2,1,0:T(8,128)(2,1)S(1)}, bf16[2,128,512]{2,1,0:T(8,128)(2,1)S(1)}, u32[]{:S(2)}, u32[]{:S(2)}) %collective-permute-start.4) | collective-permute-done | bytes 262176 | tf_op jit(solution)/shard_map/ppermute | solution.py:37
  31.1 0.8 %fusion.1 = (bf16[128,512]{1,0:T(8,128)(2,1)}, bf16[128,512]{1,0:T(8,128)(2,1)}) fusion(f32[2,128,512]{2,1,0:T(8,128)S(1)} %get-tuple-element.51, bf16[2,128,512]{2,1,0:T(8,128)(2,1)S(1)} %collective-permute-done.5, bf16[2,128,512]{2,1,0:T(8,128)(2,1)S(1)} %collective-permute-done.4), kind=kLoop, calls=%fused_computation.3 | loop fusion | flops 655360 | bytes 1310720 | tf_op jit(solution)/shard_map/convert_element_type | solution.py:351
Async XLA Ops:
  1.6 8.4 %collective-permute-start = (bf16[2,128,512]{2,1,0:T(8,128)(2,1)S(1)}, bf16[2,128,512]{2,1,0:T(8,128)(2,1)S(1)}, u32[]{:S(2)}, u32[]{:S(2)}) collective-permute-start(bf16[2,128,512]{2,1,0:T(8,128)(2,1)S(1)} %get-tuple-element.30.kv_ref.own_ref), channel_id=1, source_target_pairs={{0,1},{1,2},{2,3},{3,4},{4,5},{5,6},{6,7},{7,8},{8,9},{9,10},{10,1... | collective-permute-start | bytes 786440 | tf_op jit(solution)/shard_map/ppermute | solution.py:37
  6.5 5.7 %collective-permute-start.1 = (bf16[2,128,512]{2,1,0:T(8,128)(2,1)S(1)}, bf16[2,128,512]{2,1,0:T(8,128)(2,1)S(1)}, u32[]{:S(2)}, u32[]{:S(2)}) collective-permute-start(bf16[2,128,512]{2,1,0:T(8,128)(2,1)S(1)} %get-tuple-element.30.kv_ref.own_ref), channel_id=1, source_target_pairs={{0,2},{2,4},{4,6},{6,8},{8,10},{10,12},{12,14},{14,16},{16,18},{18... | collective-permute-start | bytes 786440 | tf_op jit(solution)/shard_map/ppermute | solution.py:37
  10.0 3.4 %collective-permute-start.2 = (bf16[2,128,512]{2,1,0:T(8,128)(2,1)S(1)}, bf16[2,128,512]{2,1,0:T(8,128)(2,1)S(1)}, u32[]{:S(2)}, u32[]{:S(2)}) collective-permute-start(bf16[2,128,512]{2,1,0:T(8,128)(2,1)S(1)} %collective-permute-done.near_ref), channel_id=1, source_target_pairs={{0,1},{2,3},{4,5},{6,7},{8,9},{10,11},{12,13},{14,15},{16,17},{18,... | collective-permute-start | bytes 786440 | tf_op jit(solution)/shard_map/ppermute | solution.py:37
  13.8 3.6 %collective-permute-start.3 = (bf16[2,128,512]{2,1,0:T(8,128)(2,1)S(1)}, bf16[2,128,512]{2,1,0:T(8,128)(2,1)S(1)}, u32[]{:S(2)}, u32[]{:S(2)}) collective-permute-start(bf16[2,128,512]{2,1,0:T(8,128)(2,1)S(1)} %get-tuple-element.53), channel_id=1, source_target_pairs={{1,0},{3,2},{5,4},{7,6},{9,8},{11,10},{13,12},{15,14},{17,16},{19,... | collective-permute-start | bytes 786440 | tf_op jit(solution)/shard_map/ppermute | solution.py:37
  15.8 9.5 %collective-permute-start.5 = (bf16[2,128,512]{2,1,0:T(8,128)(2,1)S(1)}, bf16[2,128,512]{2,1,0:T(8,128)(2,1)S(1)}, u32[]{:S(2)}, u32[]{:S(2)}) collective-permute-start(bf16[2,128,512]{2,1,0:T(8,128)(2,1)S(1)} %get-tuple-element.53), channel_id=1, source_target_pairs={{2,0},{4,2},{6,4},{8,6},{10,8},{12,10},{14,12},{16,14},{18,16},{20... | collective-permute-start | bytes 786440 | tf_op jit(solution)/shard_map/ppermute | solution.py:37
  17.5 13.6 %collective-permute-start.4 = (bf16[2,128,512]{2,1,0:T(8,128)(2,1)S(1)}, bf16[2,128,512]{2,1,0:T(8,128)(2,1)S(1)}, u32[]{:S(2)}, u32[]{:S(2)}) collective-permute-start(bf16[2,128,512]{2,1,0:T(8,128)(2,1)S(1)} %add_passed.1), channel_id=1, source_target_pairs={{1,0},{2,1},{3,2},{4,3},{5,4},{6,5},{7,6},{8,7},{9,8},{10,9},{11,1... | collective-permute-start | bytes 786440 | tf_op jit(solution)/shard_map/ppermute | solution.py:37
